TPU v7x, 256 devices: a whole 4x4x8 slice. The times are simulated.
256 devices in a mesh: row: 8 (over y, z_lo), col: 32 (over x, z_hi, core).
Axes of the slice: x: 4, y: 4, z: 8 (z_hi: 4, z_lo: 2; z = z_hi * 2 + z_lo), core: 2. Of those that a mesh axis runs over, the one named last changes fastest.
Arguments:
- object_field: float32 [2, 2048, 8192], P(None, 'row', 'col'), may hold values from -5 to 5
- probe: float32 [2, 2, 256, 256], replicated, may hold values from -5 to 5
- amplitudes: float32 [8, 32, 1, 256, 256], P('row', 'col'), may hold values from 0.5 to 3
- offsets: int32 [8, 32, 1, 2], P('row', 'col'), may hold values from 0 to 128
Outputs:
- new_object: float32 [2, 2048, 8192], P(None, 'row', 'col')
- new_probe: float32 [2, 2, 256, 256], replicated
All inputs are finite; a program needn't handle non-finite values.
Results may differ from a plain program's by a relative error of at most 0.0003.
Values sent between devices are 32-bit elements; how exact they have to be, the bound alone decides.
No kernel may reach another device: no remote copies, remote signals or barrier semaphores. Data moves between devices by JAX's collectives and lax.ppermute only.
A program may use at most 64 MiB of HBM per device.

v0:
```python
import math

import jax
import jax.numpy as jnp
from jax import lax
from jax.sharding import PartitionSpec as P

H = 64
F = 256
POS = 1
ITERS = 2


object_step = 0.25
probe_step = 4.0
highest = lax.Precision.HIGHEST


def extended_2(block, sides, width):
    for axis, dim in sides:
        count = lax.axis_size(axis)
        forward = [(i, i + 1) for i in range(count - 1)]
        backward = [(target, source) for source, target in forward]
        low = lax.ppermute(
            lax.slice_in_dim(block, block.shape[dim] - width, None, axis=dim), axis, forward
        )
        high = lax.ppermute(lax.slice_in_dim(block, 0, width, axis=dim), axis, backward)
        block = jnp.concatenate([low, block, high], axis=dim)
    return block


def dft_tables(length):
    counter = jnp.arange(length, dtype=jnp.int32)
    product = counter[:, None] * counter[None, :] % length
    angle = -2.0 * math.pi / length * product.astype(jnp.float32)
    scale = 1.0 / math.sqrt(length)
    return (jnp.cos(angle) * scale, jnp.sin(angle) * scale)


def transform(real_part, imag_part, table_re, table_im):
    left_re = jnp.einsum("jk,mkl->mjl", table_re, real_part, precision=highest) - jnp.einsum(
        "jk,mkl->mjl", table_im, imag_part, precision=highest
    )
    left_im = jnp.einsum("jk,mkl->mjl", table_re, imag_part, precision=highest) + jnp.einsum(
        "jk,mkl->mjl", table_im, real_part, precision=highest
    )
    right_re = jnp.einsum("mjk,kl->mjl", left_re, table_re, precision=highest) - jnp.einsum(
        "mjk,kl->mjl", left_im, table_im, precision=highest
    )
    right_im = jnp.einsum("mjk,kl->mjl", left_re, table_im, precision=highest) + jnp.einsum(
        "mjk,kl->mjl", left_im, table_re, precision=highest
    )
    return (right_re, right_im)


def frame_terms(patch, probes, measured, table_re, table_im):
    probe_re, probe_im = (probes[0], probes[1])
    wave_re = probe_re * patch[0] - probe_im * patch[1]
    wave_im = probe_re * patch[1] + probe_im * patch[0]
    far_re, far_im = transform(wave_re, wave_im, table_re, table_im)
    intensity = jnp.sum(far_re * far_re + far_im * far_im, axis=0)
    factor = 1.0 - measured / jnp.sqrt(intensity + 1.0)
    back_re, back_im = transform(far_re * factor, far_im * factor, table_re, -table_im)
    object_re = jnp.sum(probe_re * back_re + probe_im * back_im, axis=0)
    object_im = jnp.sum(probe_re * back_im - probe_im * back_re, axis=0)
    probe_term_re = patch[0] * back_re + patch[1] * back_im
    probe_term_im = patch[0] * back_im - patch[1] * back_re
    return (jnp.stack([object_re, object_im]), jnp.stack([probe_term_re, probe_term_im]))


def local_gradients(extended, probes, amplitudes, offsets, table_re, table_im):
    grad = jnp.zeros_like(extended)
    zero = jnp.zeros((), jnp.int32)
    start = (zero, offsets[0, 0, 0, 0], offsets[0, 0, 0, 1])
    patch = lax.dynamic_slice(extended, start, (2, F, F))
    term_object, term_probe = frame_terms(patch, probes, amplitudes[0, 0, 0], table_re, table_im)
    grad = lax.dynamic_update_slice(grad, term_object, start)
    return (grad, term_probe)


def local(object_field, probe, amplitudes, offsets):
    tile = object_field.shape[1]
    span = tile + 2 * H
    table_re, table_im = dft_tables(F)
    frames = POS * lax.axis_size("row") * lax.axis_size("col")
    coeff = probe_step / frames
    extended = extended_2(object_field, (("row", 1), ("col", 2)), H)
    current = object_field
    probes = probe
    for iteration in range(ITERS):
        grad, probe_grad = local_gradients(
            extended, probes, amplitudes, offsets, table_re, table_im
        )
        band = jnp.concatenate([grad[:, :H], grad[:, span - H :]], axis=1)
        arrived = extended_2(band, (("row", 1),), H)
        inner = grad[:, H : span - H]
        inner = inner.at[:, :H].add(arrived[:, :H]).at[:, tile - H :].add(arrived[:, 3 * H :])
        band = jnp.concatenate([inner[:, :, :H], inner[:, :, span - H :]], axis=2)
        arrived = extended_2(band, (("col", 2),), H)
        core = inner[:, :, H : span - H]
        core = (
            core.at[:, :, :H]
            .add(arrived[:, :, :H])
            .at[:, :, tile - H :]
            .add(arrived[:, :, 3 * H :])
        )
        current = current - object_step * core
        if iteration + 1 < ITERS:
            extended = extended_2(current, (("row", 1), ("col", 2)), H)
        total = lax.psum(probe_grad, ("row", "col"))
        probes = probes - coeff * total
    return (current, probes)


def solution(mesh):
    return jax.shard_map(
        local,
        mesh=mesh,
        in_specs=(
            P(None, "row", "col"),
            P(),
            P("row", "col", None, None, None),
            P("row", "col", None, None),
        ),
        out_specs=(P(None, "row", "col"), P()),
        check_vma=False,
    )
```

profile of v0, /device:TPU:1, one launch (start us, length us, event | category | flops | bytes accessed | tf_op | source)
XLA Modules:
  0.0 681.8 jit_solution(13149090804276895494)
XLA Ops:
  8.2 4.4 collective-permute-start
  15.8 3.2 collective-permute-done.1
  19.2 3.5 collective-permute-start.3
  22.8 4.8 collective-permute-start.2
  32.1 3.2 collective-permute-done.3
  58.4 2.2 fusion.71
  67.7 6.2 dynamic_update_slice.6
  74.9 4.4 collective-permute-start.4
  82.8 4.1 collective-permute-done.5
  87.8 8.3 %collective-permute-start.6 = (f32[2,256,64]{2,1,0:T(8,128)}, f32[2,256,64]{2,1,0:T(8,128)S(1)}, u32[]{:S(2)}, u32[]{:S(2)}) collective-permute-start(f32[2,256,64]{2,1,0:T(8,128)} %get-tuple-element.119), channel_id=1, source_target_pairs={{0,1},{1,2},{2,3},{3,4},{4,5},{5,6},{6,7},{7,8},{8,9},{9,10},{10,1... | collective-permute-start | bytes 393224 | tf_op jit(solution)/shard_map/ppermute | solution.py:24
  101.1 7.5 %collective-permute-done.7 = f32[2,256,64]{2,1,0:T(8,128)S(1)} collective-permute-done((f32[2,256,64]{2,1,0:T(8,128)}, f32[2,256,64]{2,1,0:T(8,128)S(1)}, u32[]{:S(2)}, u32[]{:S(2)}) %collective-permute-start.7) | collective-permute-done | bytes 131104 | tf_op jit(solution)/shard_map/ppermute | solution.py:27
  114.4 5.9 collective-permute-done.9
  123.2 4.7 collective-permute-start.10
  127.9 230.2 %all-reduce.3.cloned.1.call-done = f32[2,2,256,256]{3,2,1,0:T(8,128)} async-done(((f32[2,2,256,256]{3,2,1,0:T(8,128)}), f32[2,2,256,256]{3,2,1,0:T(8,128)}) %all-reduce.3.cloned.1.call-update) | async-done | bytes 1048592 | tf_op jit(solution)/shard_map/psum | solution.py:110
  389.7 3.1 add_bitcast_fusion
  392.9 7.6 %dynamic_update_slice.7 = f32[2,384,384]{2,1,0:T(8,128)S(1)} dynamic-update-slice(f32[2,384,384]{2,1,0:T(8,128)S(1)} %broadcast.151, f32[2,256,256]{2,1,0:T(8,128)S(1)} %pad_maximum_fusion.4, s32[]{:T(128)} %constant.206.clone.1, s32[]{:T(128)S(6)} %select_n.81, s32[]{:T(128)S(6)} %select_n.82) | dynamic-update-slice | bytes 1048580 | tf_op jit(solution)/shard_map/dynamic_update_slice | solution.py:77
  400.5 3.4 collective-permute-start.12
  405.4 3.0 collective-permute-done.12
  408.4 4.1 collective-permute-done.13
  413.3 3.6 collective-permute-start.14
  418.2 2.5 collective-permute-start.15
  422.0 7.9 %collective-permute-done.15 = f32[2,256,64]{2,1,0:T(8,128)} collective-permute-done((f32[2,256,64]{2,1,0:T(8,128)}, f32[2,256,64]{2,1,0:T(8,128)}, u32[]{:S(2)}, u32[]{:S(2)}) %collective-permute-start.15) | collective-permute-done | bytes 131104 | tf_op jit(solution)/shard_map/ppermute | solution.py:27
  433.0 239.1 %all-reduce.5.cloned.1.call-done = f32[2,2,256,256]{3,2,1,0:T(8,128)} async-done(((f32[2,2,256,256]{3,2,1,0:T(8,128)}), f32[2,2,256,256]{3,2,1,0:T(8,128)}) %all-reduce.5.cloned.1.call-update) | async-done | bytes 1048592 | tf_op jit(solution)/shard_map/psum | solution.py:110
  672.2 2.3 multiply_subtract_fusion
  (103 shorter events, 93.6 us)
Async XLA Ops:
  7.2 350.9 %all-reduce.3.cloned.1.call-start = ((), (), s32[]{:S(2)}) async-start(), calls=%async_computation | async-start | bytes 2097152 | tf_op jit(solution)/shard_map/psum | solution.py:110
  8.2 6.5 collective-permute-start
  12.6 6.5 collective-permute-start.1
  15.8 11.7 %copy-start.4 = (s32[1,1,1,2]{3,2,1,0:T(1,128)S(1)}, s32[1,1,1,2]{3,2,1,0:T(1,128)}, u32[]{:S(2)}) copy-start(s32[1,1,1,2]{3,2,1,0:T(1,128)} %param.23) | copy-start | bytes 28
  19.2 16.1 %collective-permute-start.3 = (f32[2,384,64]{2,1,0:T(8,128)S(1)}, f32[2,384,64]{2,1,0:T(8,128)S(1)}, u32[]{:S(2)}, u32[]{:S(2)}) collective-permute-start(f32[2,384,64]{2,1,0:T(8,128)S(1)} %get-tuple-element.120), channel_id=1, source_target_pairs={{1,0},{2,1},{3,2},{4,3},{5,4},{6,5},{7,6},{8,7},{9,8},{10,9},{11,1... | collective-permute-start | bytes 589832 | tf_op jit(solution)/shard_map/ppermute | solution.py:27
  22.8 12.5 %collective-permute-start.2 = (f32[2,384,64]{2,1,0:T(8,128)S(1)}, f32[2,384,64]{2,1,0:T(8,128)S(1)}, u32[]{:S(2)}, u32[]{:S(2)}) collective-permute-start(f32[2,384,64]{2,1,0:T(8,128)S(1)} %get-tuple-element.121), channel_id=1, source_target_pairs={{0,1},{1,2},{2,3},{3,4},{4,5},{5,6},{6,7},{7,8},{8,9},{9,10},{10,1... | collective-permute-start | bytes 589832 | tf_op jit(solution)/shard_map/ppermute | solution.py:24
  32.0 3.7 copy-start
  49.1 1.9 copy-start.3
  74.9 7.0 %collective-permute-start.4 = (f32[2,64,384]{2,1,0:T(8,128)S(1)}, f32[2,64,384]{2,1,0:T(8,128)S(1)}, u32[]{:S(2)}, u32[]{:S(2)}) collective-permute-start(f32[2,64,384]{2,1,0:T(8,128)S(1)} %get-tuple-element.109), channel_id=1, source_target_pairs={{0,32},{32,64},{64,96},{96,128},{128,160},{160,192},{192,224},{1,3... | collective-permute-start | bytes 589832 | tf_op jit(solution)/shard_map/ppermute | solution.py:24
  80.5 6.4 collective-permute-start.5
  87.8 12.0 %collective-permute-start.6 = (f32[2,256,64]{2,1,0:T(8,128)}, f32[2,256,64]{2,1,0:T(8,128)S(1)}, u32[]{:S(2)}, u32[]{:S(2)}) collective-permute-start(f32[2,256,64]{2,1,0:T(8,128)} %get-tuple-element.119), channel_id=1, source_target_pairs={{0,1},{1,2},{2,3},{3,4},{4,5},{5,6},{6,7},{7,8},{8,9},{9,10},{10,1... | collective-permute-start | bytes 393224 | tf_op jit(solution)/shard_map/ppermute | solution.py:24
  97.2 575.0 %all-reduce.5.cloned.1.call-start = ((), (), s32[]{:S(2)}) async-start(), calls=%async_computation.1 | async-start | bytes 2097152 | tf_op jit(solution)/shard_map/psum | solution.py:110
  97.4 11.1 %collective-permute-start.7 = (f32[2,256,64]{2,1,0:T(8,128)}, f32[2,256,64]{2,1,0:T(8,128)S(1)}, u32[]{:S(2)}, u32[]{:S(2)}) collective-permute-start(f32[2,256,64]{2,1,0:T(8,128)} %get-tuple-element.118), channel_id=1, source_target_pairs={{1,0},{2,1},{3,2},{4,3},{5,4},{6,5},{7,6},{8,7},{9,8},{10,9},{11,1... | collective-permute-start | bytes 393224 | tf_op jit(solution)/shard_map/ppermute | solution.py:27
  111.0 3.3 collective-permute-start.8
  112.3 7.9 %collective-permute-start.9 = (f32[2,64,256]{2,1,0:T(8,128)S(1)}, f32[2,64,256]{2,1,0:T(8,128)S(1)}, u32[]{:S(2)}, u32[]{:S(2)}) collective-permute-start(f32[2,64,256]{2,1,0:T(8,128)S(1)} %get-tuple-element.125), channel_id=1, source_target_pairs={{32,0},{64,32},{96,64},{128,96},{160,128},{192,160},{224,192},{33,... | collective-permute-start | bytes 393224 | tf_op jit(solution)/shard_map/ppermute | solution.py:27
  121.3 238.2 %collective-permute-start.11 = (f32[2,384,64]{2,1,0:T(8,128)}, f32[2,384,64]{2,1,0:T(8,128)}, u32[]{:S(2)}, u32[]{:S(2)}) collective-permute-start(f32[2,384,64]{2,1,0:T(8,128)} %get-tuple-element.116), channel_id=1, source_target_pairs={{1,0},{2,1},{3,2},{4,3},{5,4},{6,5},{7,6},{8,7},{9,8},{10,9},{11,1... | collective-permute-start | bytes 589832 | tf_op jit(solution)/shard_map/ppermute | solution.py:27
  123.2 236.3 %collective-permute-start.10 = (f32[2,384,64]{2,1,0:T(8,128)}, f32[2,384,64]{2,1,0:T(8,128)}, u32[]{:S(2)}, u32[]{:S(2)}) collective-permute-start(f32[2,384,64]{2,1,0:T(8,128)} %get-tuple-element.117), channel_id=1, source_target_pairs={{0,1},{1,2},{2,3},{3,4},{4,5},{5,6},{6,7},{7,8},{8,9},{9,10},{10,1... | collective-permute-start | bytes 589832 | tf_op jit(solution)/shard_map/ppermute | solution.py:24
  400.5 7.9 %collective-permute-start.12 = (f32[2,64,384]{2,1,0:T(8,128)S(1)}, f32[2,64,384]{2,1,0:T(8,128)S(1)}, u32[]{:S(2)}, u32[]{:S(2)}) collective-permute-start(f32[2,64,384]{2,1,0:T(8,128)S(1)} %get-tuple-element.107), channel_id=1, source_target_pairs={{0,32},{32,64},{64,96},{96,128},{128,160},{160,192},{192,224},{1,3... | collective-permute-start | bytes 589832 | tf_op jit(solution)/shard_map/ppermute | solution.py:24
  403.9 13.0 %copy-start.1 = (f32[1,2,256,256]{3,2,1,0:T(8,128)S(1)}, f32[1,2,256,256]{3,2,1,0:T(8,128)}, u32[]{:S(2)}) copy-start(f32[1,2,256,256]{3,2,1,0:T(8,128)} %get-tuple-element.102) | copy-start | bytes 1572868
  403.9 13.0 %copy-start.2 = (f32[1,2,256,256]{3,2,1,0:T(8,128)S(1)}, f32[1,2,256,256]{3,2,1,0:T(8,128)}, u32[]{:S(2)}) copy-start(f32[1,2,256,256]{3,2,1,0:T(8,128)} %get-tuple-element.103) | copy-start | bytes 1572868
  404.0 8.5 %collective-permute-start.13 = (f32[2,64,384]{2,1,0:T(8,128)S(1)}, f32[2,64,384]{2,1,0:T(8,128)S(1)}, u32[]{:S(2)}, u32[]{:S(2)}) collective-permute-start(f32[2,64,384]{2,1,0:T(8,128)S(1)} %get-tuple-element.106), channel_id=1, source_target_pairs={{32,0},{64,32},{96,64},{128,96},{160,128},{192,160},{224,192},{33,... | collective-permute-start | bytes 589832 | tf_op jit(solution)/shard_map/ppermute | solution.py:27
  413.3 7.4 %collective-permute-start.14 = (f32[2,256,64]{2,1,0:T(8,128)S(1)}, f32[2,256,64]{2,1,0:T(8,128)S(1)}, u32[]{:S(2)}, u32[]{:S(2)}) collective-permute-start(f32[2,256,64]{2,1,0:T(8,128)S(1)} %get-tuple-element.115), channel_id=1, source_target_pairs={{0,1},{1,2},{2,3},{3,4},{4,5},{5,6},{6,7},{7,8},{8,9},{9,10},{10,1... | collective-permute-start | bytes 393224 | tf_op jit(solution)/shard_map/ppermute | solution.py:24
  418.2 11.7 %collective-permute-start.15 = (f32[2,256,64]{2,1,0:T(8,128)}, f32[2,256,64]{2,1,0:T(8,128)}, u32[]{:S(2)}, u32[]{:S(2)}) collective-permute-start(f32[2,256,64]{2,1,0:T(8,128)} %get-tuple-element.114), channel_id=1, source_target_pairs={{1,0},{2,1},{3,2},{4,3},{5,4},{6,5},{7,6},{8,7},{9,8},{10,9},{11,1... | collective-permute-start | bytes 393224 | tf_op jit(solution)/shard_map/ppermute | solution.py:27
Sparse Core Ops, SparseCore 0:
  97.3 260.7 all-reduce.2
  418.1 253.9 all-reduce.4
where the time goes:
time: 693 us; the launch traced here: 682 us
  waiting for transfers between devices  510 us (74%)
  matrix products  61.9 us (9%)
  starting transfers between devices  50.1 us (7%)
  local copies, waits for them, and re-layouts  28 us (4%)
  between operations  19 us (3%)
  other arithmetic  12.6 us (2%)
    psum x2, waiting for transfers between devices, local(): total = lax.psum(probe_grad, ('row', 'col'))  469 us
    ppermute x8, waiting for transfers between devices, extended_2(): lax.ppermute(lax.slice_in_dim(block, 0, width, axis=dim), axis, backward)  35.9 us
    ppermute x8, starting transfers between devices, extended_2(): lax.ppermute(lax.slice_in_dim(block, block.shape[dim] - width, None, axis...  34.8 us
    ppermute x8, starting transfers between devices, extended_2(): lax.ppermute(lax.slice_in_dim(block, 0, width, axis=dim), axis, backward)  15.2 us
  transfers between devices with their start and end apart: 18, of which 14 were waited for; matrix products, arithmetic and copies ran while one was open for 2% of the time, Pallas kernels for 0%

commit v1 on v0

v1 whole, which is shorter than its diff:
```python
import functools
import math

import jax
import jax.numpy as jnp
import ml_dtypes
import numpy as np
from jax import lax
from jax.experimental import pallas as pl
from jax.experimental.pallas import tpu as pltpu
from jax.sharding import PartitionSpec as P

H = 64
F = 256
M = 2
TILE = 256
SPAN = TILE + 2 * H
B = 2 * H
object_step = 0.25
probe_step = 4.0
RC = ("row", "col")
BIT_Y, BIT_ZLO, BIT_X, BIT_ZHI, BIT_CORE = 192, 32, 24, 6, 1

f32 = jnp.float32
bf16 = jnp.bfloat16
VMEM_LIMIT = 56 * 1024 * 1024
SMALL_LIMIT = 24 * 1024 * 1024


def tables():
    counter = np.arange(F)
    angle = -2.0 * math.pi / F * (counter[:, None] * counter[None, :] % F)
    out = []
    for table in (np.cos(angle) / math.sqrt(F), np.sin(angle) / math.sqrt(F)):
        high = table.astype(np.float32).astype(ml_dtypes.bfloat16)
        low = (table - high.astype(np.float64)).astype(np.float32).astype(ml_dtypes.bfloat16)
        out += [high, low]
    return np.concatenate(out, axis=0)


def blocks(table):
    rh, rl, ih, il = (table[k * F:(k + 1) * F, :] for k in range(4))

    def block(re, im, under):
        return jnp.concatenate(
            [jnp.concatenate([re, im], axis=1), jnp.concatenate([under, re], axis=1)], axis=0)

    return (block(rh, ih, -ih), block(rl, il, -il)), (block(rh, -ih, ih), block(rl, -il, il))


def split(x):
    high = x.astype(bf16)
    return high, (x - high.astype(f32)).astype(bf16)


def dot(a, b):
    return jnp.dot(a, b, preferred_element_type=f32)


def product(left, right):
    return dot(left[0], right[0]) + (dot(left[0], right[1]) + dot(left[1], right[0]))


LANE = 128


def lanes():
    return lax.broadcasted_iota(jnp.int32, (TILE, LANE), 1) < H


def half_turn(x):
    return pltpu.roll(x, H, 1)


def sides_kernel(obj, left, right):
    low = lanes()
    left[...] = jnp.where(low, obj[0, :, :LANE], half_turn(obj[1, :, :LANE]))
    right[...] = jnp.where(low, half_turn(obj[0, :, LANE:]), obj[1, :, LANE:])


def rows_kernel(obj, west, east, mid, top, bottom):
    low = lanes()
    for c in range(2):
        x, y = half_turn(obj[c, :, :LANE]), half_turn(obj[c, :, LANE:])
        w = west[...] if c == 0 else half_turn(west[...])
        e = half_turn(east[...]) if c == 0 else east[...]
        for k, part in enumerate((jnp.where(low, w, x), jnp.where(low, x, y), jnp.where(low, y, e))):
            s = slice(k * LANE, (k + 1) * LANE)
            mid[c, :, s] = part
            top[c, :, s] = part[:H]
            bottom[c, :, s] = part[TILE - H:]


def fetch(refs, scratch, sems):
    copies = [pltpu.make_async_copy(r, t, sems.at[k]) for k, (r, t) in enumerate(zip(refs, scratch))]
    for copy in copies:
        copy.start()

    def wait(*which):
        for k in which:
            copies[k].wait()

    return wait


def store(pairs, sems):
    copies = [pltpu.make_async_copy(x, y, sems.at[k]) for k, (x, y) in enumerate(pairs)]
    for copy in copies:
        copy.start()
    return copies


def finish(copies):
    for copy in copies:
        copy.wait()


def frame_kernel(first, *refs):
    count = 7 if first else 14
    arrays, refs = refs[:count], refs[count:]
    if first:
        keep, send, gu, gm, gd, ext, canvas, outs, *inner, sems = refs
        up, mid, down, off, probe, amps, table = inner
    else:
        keep, send, gu, gm, gd, obj, probe_out, ext, canvas, outs, probe, *inner, sems = refs
        up, mid, down, off, cl, cm, cr, dl, dr, probe_in, mine, other, amps, table = inner
    wait = fetch(arrays, inner, sems)
    wait(*range(4 if first else 9))
    o0 = off[0, 0, 0, 0]
    o1 = off[0, 0, 0, 1]
    row = lax.axis_index("row")
    col = lax.axis_index("col")
    core = lax.rem(col, 2)
    rest = lax.rem(o0, 8)
    base = pl.multiple_of(o0 - rest, 8)
    patch = []
    copies = []
    for c in range(2):
        whole = jnp.concatenate([up[c], mid[c], down[c]], axis=0)
        if not first:
            grad = jnp.concatenate([cl[c] + dl[c], cm[c], cr[c] + dr[c]], axis=1)
            i = lax.broadcasted_iota(jnp.int32, (SPAN, SPAN), 0) + (row * TILE - H)
            j = lax.broadcasted_iota(jnp.int32, (SPAN, SPAN), 1) + (col * TILE - H)
            inside = (i >= 0) & (i < lax.axis_size("row") * TILE) & (j >= 0) & (
                j < lax.axis_size("col") * TILE)
            whole = jnp.where(inside, whole - object_step * grad, 0.0)
        ext[c, :SPAN, :] = whole
        ext[c, SPAN:, :] = jnp.zeros((8, SPAN), f32)
        rows = pltpu.roll(ext[c, pl.ds(base, F + 8), :], SPAN - o1, 1)[:, :F]
        patch.append(pltpu.roll(rows, F + 8 - rest, 0)[:F])
    pr, pi = patch
    if first:
        wait(4, 5, 6)
    else:
        wait(*range(9, 14))
        new_probe(core, probe_in, mine, other, probe)
        copies += store(
            ((ext.at[0, H:H + TILE], obj.at[0]), (ext.at[1, H:H + TILE], obj.at[1]),
             (probe, probe_out)), outs.at[6:9])
    right, left = blocks(table)
    wave = jnp.concatenate(
        [
            jnp.concatenate(
                [
                    probe[0, m] * pr - probe[1, m] * pi,
                    probe[0, m] * pi + probe[1, m] * pr,
                ],
                axis=1,
            )
            for m in range(M)
        ],
        axis=0,
    )
    x = product(split(wave), right)
    x = jnp.concatenate(
        [jnp.concatenate([x[m * F:(m + 1) * F, p * F:(p + 1) * F] for m in range(M)], axis=1)
         for p in range(2)], axis=0)
    x = product(left, split(x))
    square = x[:F] * x[:F] + x[F:] * x[F:]
    intensity = square[:, :F] + square[:, F:]
    factor = 1.0 - amps[0, 0, 0] * lax.rsqrt(intensity + 1.0)
    factor = jnp.concatenate([factor, factor], axis=1)
    x = jnp.concatenate([x[:F] * factor, x[F:] * factor], axis=0)
    x = product(right, split(x))
    x = jnp.concatenate(
        [jnp.concatenate([x[p * F:(p + 1) * F, m * F:(m + 1) * F] for p in range(2)], axis=1)
         for m in range(M)], axis=0)
    x = product(split(x), left)
    ore = jnp.zeros((F, F), f32)
    oim = jnp.zeros((F, F), f32)
    for m in range(M):
        br, bi = x[m * F:(m + 1) * F, :F], x[m * F:(m + 1) * F, F:]
        qr, qi = probe[0, m], probe[1, m]
        ore = ore + (qr * br + qi * bi)
        oim = oim + (qr * bi - qi * br)
        for p, term in enumerate((pr * br + pi * bi, pr * bi - pi * br)):
            s = slice((p * M + m) * F, (p * M + m + 1) * F)
            keep[s, :] = jnp.where(core == 0, term[:, :LANE], term[:, LANE:])
            send[s, :] = jnp.where(core == 0, term[:, LANE:], term[:, :LANE])
    edge = gu.shape[1]
    for c, value in enumerate((ore, oim)):
        canvas[c] = jnp.zeros((SPAN + 8, SPAN), f32)
        value = jnp.concatenate([value, jnp.zeros((8, F), f32)], axis=0)
        value = pltpu.roll(value, rest, 0)
        value = jnp.concatenate([value, jnp.zeros((F + 8, SPAN - F), f32)], axis=1)
        canvas[c, pl.ds(base, F + 8), :] = pltpu.roll(value, o1, 1)
        copies += store(
            ((canvas.at[c, :edge], gu.at[c]), (canvas.at[c, SPAN - edge:SPAN], gd.at[c]),
             (canvas.at[c, edge:SPAN - edge], gm.at[c])), outs.at[3 * c:3 * c + 3])
    finish(copies)


def new_probe(core, probe, mine, other, out):
    coeff = probe_step / (lax.axis_size("row") * lax.axis_size("col"))
    for q in range(4):
        s = slice(q * F, (q + 1) * F)
        x, y = mine[s, :], other[s, :]
        total = jnp.concatenate(
            [jnp.where(core == 0, x, y), jnp.where(core == 0, y, x)], axis=1)
        out[q // 2, q % 2] = probe[q // 2, q % 2] - coeff * total


def chunk_sum(parts, out):
    rows = out.shape[0]
    total = parts[:rows, :]
    for k in range(1, parts.shape[0] // rows):
        total = total + parts[k * rows:(k + 1) * rows, :]
    out[...] = total


def bands_kernel(parts, gu, gm, gd, ru, rd, total, cl, cm, cr, tl, tm, tr, outs, *inner):
    *inner, sems = inner
    wait = fetch((gu, gm, gd, ru, rd), inner, sems)
    gu, gm, gd, ru, rd = inner
    chunk_sum(parts, total)
    wait(*range(5))
    for c in range(2):
        for k, out in enumerate((tl, tm, tr)):
            s = slice(k * B, (k + 1) * B)
            out[c, :B] = gu[c, :, s] + ru[c, :, s]
            out[c, B:2 * B] = gm[c, :, s]
            out[c, 2 * B:] = gd[c, :, s] + rd[c, :, s]
    finish(store(zip((tl, tm, tr), (cl, cm, cr)), outs))


def last_bands_kernel(parts, gm, ru, rd, total, grad_out, left, right, grad, outs, *inner):
    *inner, sems = inner
    wait = fetch((gm, ru, rd), inner, sems)
    gm, ru, rd = inner
    chunk_sum(parts, total)
    low = lanes()
    wait(*range(3))
    for c in range(2):
        grad[c, :H] = gm[c, :H] + ru[c]
        grad[c, H:TILE - H] = gm[c, H:TILE - H]
        grad[c, TILE - H:] = gm[c, TILE - H:] + rd[c]
    copies = store(((grad, grad_out),), outs)
    left[...] = jnp.where(low, grad[0, :, :LANE], half_turn(grad[1, :, :LANE]))
    right[...] = jnp.where(low, half_turn(grad[0, :, 2 * LANE:]), grad[1, :, 2 * LANE:])
    finish(copies)


def spread_kernel(a, b, c, d, out):
    total = (a[...] + b[...]) + (c[...] + d[...])
    rows = a.shape[0]
    for k in range(out.shape[0] // rows):
        out[k * rows:(k + 1) * rows, :] = total


def last_kernel(obj, grad, probe, west, east, mine, other, out, out_probe, *inner):
    *inner, sems = inner
    wait = fetch((obj, grad, probe), inner, sems)
    obj, grad, probe = inner
    low = lanes()
    wait(*range(3))
    for c in range(2):
        w = half_turn(west[...]) if c == 0 else west[...]
        e = east[...] if c == 0 else half_turn(east[...])
        x = obj[c, :, :LANE] - object_step * (grad[c, :, :LANE] + w)
        y = obj[c, :, LANE:2 * LANE] - object_step * grad[c, :, LANE:2 * LANE]
        z = obj[c, :, 2 * LANE:] - object_step * (grad[c, :, 2 * LANE:] + e)
        x, y, z = half_turn(x), half_turn(y), half_turn(z)
        out[c, :, :LANE] = jnp.where(low, x, y)
        out[c, :, LANE:] = jnp.where(low, y, z)
    new_probe(lax.rem(lax.axis_index("col"), 2), probe, mine, other, out_probe)


VM = pl.BlockSpec(memory_space=pltpu.VMEM)
HBM = pl.BlockSpec(memory_space=pltpu.HBM)


def call(kernel, outs, name, limit=SMALL_LIMIT, specs=(), places=(), scratch=()):
    def run(*args):
        held = list(specs) or [VM] * len(args)
        inner = [
            (pltpu.VMEM if x.dtype != jnp.int32 else pltpu.SMEM)(x.shape, x.dtype)
            for x, s in zip(args, held) if s is HBM
        ]
        if inner:
            inner.append(pltpu.SemaphoreType.DMA((len(inner),)))
        return pl.pallas_call(
            kernel,
            out_shape=[jax.ShapeDtypeStruct(s, f32) for s in outs],
            in_specs=held,
            out_specs=list(places) or [VM] * len(outs),
            scratch_shapes=list(scratch) + inner,
            compiler_params=pltpu.CompilerParams(vmem_limit_bytes=limit),
            name=name,
        )(*args)

    return run


def shift(x, axis, step):
    count = lax.axis_size(axis)
    pairs = [(i, i + step) for i in range(count) if 0 <= i + step < count]
    return lax.ppermute(x, axis, pairs)


def exchange(x, mask):
    return lax.ppermute(x, RC, [(i, i ^ mask) for i in range(256)])


def groups(mask):
    members = [i for i in range(256) if i & ~mask == 0]
    return [[base | i for i in members] for base in range(256) if base & mask == 0]


WIDE = BIT_Y | BIT_ZLO | BIT_X
COUNT = 32
CHUNK = 1024 // COUNT


def scatter(keep, send):
    x = keep + exchange(send, BIT_CORE)
    return lax.all_to_all(x, RC, 0, 0, axis_index_groups=groups(WIDE), tiled=True)


def gather(x, *early):
    parts = (x, exchange(x, 2), exchange(x, 4), exchange(x, 6))
    (x,) = call(spread_kernel, [(1024, LANE)], "spread")(*parts)
    x = lax.all_to_all(x, RC, 0, 0, axis_index_groups=groups(WIDE), tiled=True)
    x, *early = lax.optimization_barrier((x, *early))
    return x, exchange(x, BIT_CORE), *early


def local(object_field, probe, amplitudes, offsets):
    table = tables()
    left, right = call(sides_kernel, [(TILE, LANE)] * 2, "sides")(object_field)
    west = shift(right, "col", 1)
    east = shift(left, "col", -1)
    mid, top, bottom = call(
        rows_kernel, [(2, TILE, SPAN)] + [(2, H, SPAN)] * 2, "rows"
    )(object_field, west, east)
    up = shift(bottom, "row", 1)
    down = shift(top, "row", -1)

    halves = [(1024, LANE)] * 2
    canvases = [pltpu.VMEM((2, SPAN + 8, SPAN), f32)] * 2
    keep, send, gu, gm, gd = call(
        functools.partial(frame_kernel, True),
        halves + [(2, B, SPAN)] * 3,
        "frame1",
        VMEM_LIMIT,
        [HBM] * 7,
        [VM] * 2 + [HBM] * 3,
        canvases + [pltpu.SemaphoreType.DMA((6,))],
    )(up, mid, down, offsets, probe, amplitudes, table)
    ru = shift(gd, "row", 1)
    rd = shift(gu, "row", -1)
    total, cl, cm, cr = call(
        bands_kernel,
        [(CHUNK, LANE)] + [(2, SPAN, B)] * 3,
        "bands",
        specs=[VM] + [HBM] * 5,
        places=[VM] + [HBM] * 3,
        scratch=[pltpu.VMEM((2, SPAN, B), f32)] * 3 + [pltpu.SemaphoreType.DMA((3,))],
    )(scatter(keep, send), gu, gm, gd, ru, rd)
    dl = shift(cr, "col", 1)
    dr = shift(cl, "col", -1)
    mine, other, dl, dr = gather(total, dl, dr)

    keep, send, gu, gm, gd, obj, probe = call(
        functools.partial(frame_kernel, False),
        halves + [(2, H, SPAN), (2, TILE, SPAN), (2, H, SPAN), (2, TILE, SPAN), (2, M, F, F)],
        "frame2",
        VMEM_LIMIT,
        [HBM] * 14,
        [VM] * 2 + [HBM] * 5,
        canvases + [pltpu.SemaphoreType.DMA((9,)), pltpu.VMEM((2, M, F, F), f32)],
    )(up, mid, down, offsets, cl, cm, cr, dl, dr, probe, mine, other, amplitudes, table)
    ru = shift(gd, "row", 1)
    rd = shift(gu, "row", -1)
    total, grad, left, right = call(
        last_bands_kernel,
        [(CHUNK, LANE), (2, TILE, SPAN)] + [(TILE, LANE)] * 2,
        "last_bands",
        specs=[VM] + [HBM] * 3,
        places=[VM, HBM, VM, VM],
        scratch=[pltpu.VMEM((2, TILE, SPAN), f32), pltpu.SemaphoreType.DMA((1,))],
    )(scatter(keep, send), gm, ru, rd)
    west = shift(right, "col", 1)
    east = shift(left, "col", -1)
    mine, other, west, east = gather(total, west, east)
    return tuple(
        call(
            last_kernel,
            [(2, TILE, TILE), (2, M, F, F)],
            "last",
            specs=[HBM] * 3 + [VM] * 4,
        )(obj, grad, probe, west, east, mine, other)
    )


def solution(mesh):
    return jax.shard_map(
        local,
        mesh=mesh,
        in_specs=(
            P(None, "row", "col"),
            P(),
            P("row", "col", None, None, None),
            P("row", "col", None, None),
        ),
        out_specs=(P(None, "row", "col"), P()),
        check_vma=False,
    )
```

time: 693 us -> 195 us (0.28); the launches traced: 682 us -> 194 us
  waiting for transfers between devices: 510 us -> 55.9 us
  matrix products: 61.9 us -> 0 us
  starting transfers between devices: 50.1 us -> 104 us
  Pallas kernels: 0 us -> 24.5 us
  local copies, waits for them, and re-layouts: 28 us -> 4.15 us
  between operations: 19 us -> 1.1 us
  other arithmetic: 12.6 us -> 3.91 us
    psum x2 -> x0, waiting for transfers between devices: 469 us -> none  [local(): total = lax.psum(probe_grad, ('row', 'col'))]
    dot_general x32 -> x0, matrix products: 61.9 us -> none  [the longest x4 8.84 us: transform(): jnp.einsum('mjk,kl->mjl', left_im, table_im, precision=highest)]
    all_to_all x0 -> x4, starting transfers between devices: none -> 47.8 us  [the longest x2 24.4 us: scatter(): lax.all_to_all(x, RC, 0, 0, axis_index_groups=groups(WIDE), tiled=True)]
    pallas_call x0 -> x9, Pallas kernels: none -> 24.5 us  [run(): pl.pallas_call(kernel, out_shape=[jax.ShapeDtypeStruct(s, f32) for s in o...]
    ppermute x16 -> x22, waiting for transfers between devices: 40.9 us -> 55.9 us  [the longest x12 43.4 us: shift(): return lax.ppermute(x, axis, pairs)]
    dynamic_update_slice x2 -> x0, local copies, waits for them, and re-layouts: 13.8 us -> none  [local_gradients(): grad = lax.dynamic_update_slice(grad, term_object, start)]
    slice x13 -> x0, local copies, waits for them, and re-layouts: 7.14 us -> none  [the longest x3 2.18 us: extended_2(): lax.slice_in_dim(block, 0, width, axis=dim)]
    ppermute x16 -> x22, starting transfers between devices: 50 us -> 56.5 us  [the longest x12 41 us: shift(): return lax.ppermute(x, axis, pairs)]
  transfers between devices with their start and end apart: 18 -> 26, of which waited for: 14 -> 16; matrix products, arithmetic and copies ran while one was open for 2% -> 0% of each run, Pallas kernels for 0% -> 0%
where the time goes in v1:
time: 195 us; the launch traced here: 194 us
  starting transfers between devices  104 us (53%)
  waiting for transfers between devices  55.9 us (29%)
  Pallas kernels  24.5 us (13%)
  local copies, waits for them, and re-layouts  4.15 us (2%)
  other arithmetic  3.91 us (2%)
    ppermute x12, waiting for transfers between devices, shift(): return lax.ppermute(x, axis, pairs)  43.4 us
    ppermute x12, starting transfers between devices, shift(): return lax.ppermute(x, axis, pairs)  41 us
    pallas_call x9, Pallas kernels, run(): pl.pallas_call(kernel, out_shape=[jax.ShapeDtypeStruct(s, f32) for s in o...  24.5 us
    all_to_all x2, starting transfers between devices, scatter(): lax.all_to_all(x, RC, 0, 0, axis_index_groups=groups(WIDE), tiled=True)  24.4 us
    all_to_all x2, starting transfers between devices, gather(): x = lax.all_to_all(x, RC, 0, 0, axis_index_groups=groups(WIDE), tiled=True)  23.4 us
    ppermute x10, starting transfers between devices, exchange(): return lax.ppermute(x, RC, [(i, i ^ mask) for i in range(256)])  15.5 us
    ppermute x10, waiting for transfers between devices, exchange(): return lax.ppermute(x, RC, [(i, i ^ mask) for i in range(256)])  12.5 us
    unnamed x38, local copies, waits for them, and re-layouts  4.15 us
  transfers between devices with their start and end apart: 26, of which 16 were waited for; matrix products, arithmetic and copies ran while one was open for 0% of the time, Pallas kernels for 0%

profile of v1, /device:TPU:1, one launch (start us, length us, event | category | flops | bytes accessed | tf_op | source)
XLA Modules:
  0.0 193.8 jit_solution(6013505141395757334)
XLA Ops:
  1.8 6.3 %collective-permute-start = (f32[256,128]{1,0:T(8,128)S(1)}, f32[256,128]{1,0:T(8,128)S(1)}, u32[]{:S(2)}, u32[]{:S(2)}) collective-permute-start(f32[256,128]{1,0:T(8,128)S(1)} %get-tuple-element.33), channel_id=1, source_target_pairs={{0,1},{1,2},{2,3},{3,4},{4,5},{5,6},{6,7},{7,8},{8,9},{9,10},{10,1... | collective-permute-start | bytes 393224 | tf_op jit(solution)/shard_map/ppermute | solution.py:317
  10.0 5.3 %collective-permute-done.1.east = f32[256,128]{1,0:T(8,128)S(1)} collective-permute-done((f32[256,128]{1,0:T(8,128)S(1)}, f32[256,128]{1,0:T(8,128)S(1)}, u32[]{:S(2)}, u32[]{:S(2)}) %collective-permute-start.1) | collective-permute-done | bytes 131104 | tf_op jit(solution)/shard_map/ppermute | solution.py:317
  16.5 3.6 %collective-permute-start.2 = (f32[2,64,384]{2,1,0:T(8,128)S(1)}, f32[2,64,384]{2,1,0:T(8,128)S(1)}, u32[]{:S(2)}, u32[]{:S(2)}) collective-permute-start(f32[2,64,384]{2,1,0:T(8,128)S(1)} %get-tuple-element.35), channel_id=1, source_target_pairs={{0,32},{32,64},{64,96},{96,128},{128,160},{160,192},{192,224},{1,3... | collective-permute-start | bytes 589832 | tf_op jit(solution)/shard_map/ppermute | solution.py:317
  22.6 4.8 %collective-permute-done.3.refs_2_ = f32[2,64,384]{2,1,0:T(8,128)S(1)} collective-permute-done((f32[2,64,384]{2,1,0:T(8,128)S(1)}, f32[2,64,384]{2,1,0:T(8,128)S(1)}, u32[]{:S(2)}, u32[]{:S(2)}) %collective-permute-start.3) | collective-permute-done | bytes 196640 | tf_op jit(solution)/shard_map/ppermute | solution.py:317
  28.1 8.1 %frame1.1 = (f32[1024,128]{1,0:T(8,128)}, f32[1024,128]{1,0:T(8,128)}, f32[2,128,384]{2,1,0:T(8,128)}, f32[2,128,384]{2,1,0:T(8,128)}, f32[2,128,384]{2,1,0:T(8,128)}) custom-call(f32[2,64,384]{2,1,0:T(8,128)} %copy-done.12, f32[2,256,384]{2,1,0:T(8,128)} %copy-done, f32[2,64,384]{2,1,0:T(8,128)} %copy-done.13, s32[1,1,1,2]{3,2,1,0:T(1,128)} %refs_3_.3, ...), custom_call_target="tpu_custom_call" | custom-call | tf_op jit(solution)/shard_map/frame1/pallas_call | solution.py:301
  40.4 11.4 %all-to-all-start = ((f32[32,32,128]{2,1,0:T(8,128)}), f32[32,32,128]{2,1,0:T(8,128)S(1)}, u32[]{:S(2)}, u32[]{:S(2)}) async-start(f32[32,32,128]{2,1,0:T(8,128)} %bitcast), calls=%async_computation | async-start | bytes 1048576 | tf_op jit(solution)/shard_map/all_to_all | solution.py:336
  53.1 4.0 %collective-permute-start.5 = (f32[2,128,384]{2,1,0:T(8,128)S(1)}, f32[2,128,384]{2,1,0:T(8,128)S(1)}, u32[]{:S(2)}, u32[]{:S(2)}) collective-permute-start(f32[2,128,384]{2,1,0:T(8,128)S(1)} %copy-done.10), channel_id=1, source_target_pairs={{0,32},{32,64},{64,96},{96,128},{128,160},{160,192},{192,224},{1,3... | collective-permute-start | bytes 1179656 | tf_op jit(solution)/shard_map/ppermute | solution.py:317
  57.1 10.1 %collective-permute-done.6.rd = f32[2,128,384]{2,1,0:T(8,128)S(1)} collective-permute-done((f32[2,128,384]{2,1,0:T(8,128)S(1)}, f32[2,128,384]{2,1,0:T(8,128)S(1)}, u32[]{:S(2)}, u32[]{:S(2)}) %collective-permute-start.6) | collective-permute-done | bytes 393248 | tf_op jit(solution)/shard_map/ppermute | solution.py:317
  69.7 3.5 %collective-permute-start.9 = (f32[32,128]{1,0:T(8,128)S(1)}, f32[32,128]{1,0:T(8,128)S(1)}, u32[]{:S(2)}, u32[]{:S(2)}) collective-permute-start(f32[32,128]{1,0:T(8,128)S(1)} %get-tuple-element.46.a), channel_id=1, source_target_pairs={{0,6},{1,7},{2,4},{3,5},{4,2},{5,3},{6,0},{7,1},{8,14},{9,15},{10,... | collective-permute-start | bytes 49160 | tf_op jit(solution)/shard_map/ppermute | solution.py:321
  73.2 2.9 %collective-permute-start.8 = (f32[32,128]{1,0:T(8,128)S(1)}, f32[32,128]{1,0:T(8,128)S(1)}, u32[]{:S(2)}, u32[]{:S(2)}) collective-permute-start(f32[32,128]{1,0:T(8,128)S(1)} %get-tuple-element.46.a), channel_id=1, source_target_pairs={{0,4},{1,5},{2,6},{3,7},{4,0},{5,1},{6,2},{7,3},{8,12},{9,13},{10,... | collective-permute-start | bytes 49160 | tf_op jit(solution)/shard_map/ppermute | solution.py:321
  76.0 3.7 %collective-permute-done.8.c = f32[32,128]{1,0:T(8,128)S(1)} collective-permute-done((f32[32,128]{1,0:T(8,128)S(1)}, f32[32,128]{1,0:T(8,128)S(1)}, u32[]{:S(2)}, u32[]{:S(2)}) %collective-permute-start.8) | collective-permute-done | bytes 16416 | tf_op jit(solution)/shard_map/ppermute | solution.py:321
  80.6 16.2 %all-to-all-start.1 = ((f32[32,32,128]{2,1,0:T(8,128)}), f32[32,32,128]{2,1,0:T(8,128)S(1)}, u32[]{:S(2)}, u32[]{:S(2)}) async-start(f32[32,32,128]{2,1,0:T(8,128)} %bitcast.2), calls=%async_computation.1 | async-start | bytes 1048576 | tf_op jit(solution)/shard_map/all_to_all | solution.py:342
  96.8 5.0 %collective-permute-start.11 = (f32[2,384,128]{2,1,0:T(8,128)S(1)}, f32[2,384,128]{2,1,0:T(8,128)S(1)}, u32[]{:S(2)}, u32[]{:S(2)}) collective-permute-start(f32[2,384,128]{2,1,0:T(8,128)S(1)} %get-tuple-element.43.refs_4_), channel_id=1, source_target_pairs={{1,0},{2,1},{3,2},{4,3},{5,4},{6,5},{7,6},{8,7},{9,8},{10,9},{11,1... | collective-permute-start | bytes 1179656 | tf_op jit(solution)/shard_map/ppermute | solution.py:317
  101.9 3.9 %collective-permute-start.10 = (f32[2,384,128]{2,1,0:T(8,128)S(1)}, f32[2,384,128]{2,1,0:T(8,128)S(1)}, u32[]{:S(2)}, u32[]{:S(2)}) collective-permute-start(f32[2,384,128]{2,1,0:T(8,128)S(1)} %get-tuple-element.45.refs_6_), channel_id=1, source_target_pairs={{0,1},{1,2},{2,3},{3,4},{4,5},{5,6},{6,7},{7,8},{8,9},{9,10},{10,1... | collective-permute-start | bytes 1179656 | tf_op jit(solution)/shard_map/ppermute | solution.py:317
  105.8 3.8 %collective-permute-done.11.refs_8_ = f32[2,384,128]{2,1,0:T(8,128)S(1)} collective-permute-done((f32[2,384,128]{2,1,0:T(8,128)S(1)}, f32[2,384,128]{2,1,0:T(8,128)S(1)}, u32[]{:S(2)}, u32[]{:S(2)}) %collective-permute-start.11) | collective-permute-done | bytes 393248 | tf_op jit(solution)/shard_map/ppermute | solution.py:317
  110.7 2.9 %collective-permute-start.12 = (f32[1024,128]{1,0:T(8,128)S(1)}, f32[1024,128]{1,0:T(8,128)S(1)}, u32[]{:S(2)}, u32[]{:S(2)}) collective-permute-start(f32[1024,128]{1,0:T(8,128)S(1)} %bitcast.12), channel_id=1, source_target_pairs={{0,1},{1,0},{2,3},{3,2},{4,5},{5,4},{6,7},{7,6},{8,9},{9,8},{10,11... | collective-permute-start | bytes 1572872 | tf_op jit(solution)/shard_map/ppermute | solution.py:321
  115.8 9.2 %frame2.1 = (f32[1024,128]{1,0:T(8,128)}, f32[1024,128]{1,0:T(8,128)}, f32[2,64,384]{2,1,0:T(8,128)}, f32[2,256,384]{2,1,0:T(8,128)}, f32[2,64,384]{2,1,0:T(8,12...) custom-call(f32[2,64,384]{2,1,0:T(8,128)} %copy-done.12, f32[2,256,384]{2,1,0:T(8,128)} %copy-done, ...), custom_call_target="tpu_custom_call" | custom-call | tf_op jit(solution)/shard_map/frame2/pallas_call | solution.py:301
  129.2 13.1 %all-to-all-start.2 = ((f32[32,32,128]{2,1,0:T(8,128)}), f32[32,32,128]{2,1,0:T(8,128)S(1)}, u32[]{:S(2)}, u32[]{:S(2)}) async-start(f32[32,32,128]{2,1,0:T(8,128)} %bitcast.4), calls=%async_computation.2 | async-start | bytes 1048576 | tf_op jit(solution)/shard_map/all_to_all | solution.py:336
  142.3 3.1 %collective-permute-start.14 = (f32[2,64,384]{2,1,0:T(8,128)S(1)}, f32[2,64,384]{2,1,0:T(8,128)S(1)}, u32[]{:S(2)}, u32[]{:S(2)}) collective-permute-start(f32[2,64,384]{2,1,0:T(8,128)S(1)} %copy-done.18), channel_id=1, source_target_pairs={{0,32},{32,64},{64,96},{96,128},{128,160},{160,192},{192,224},{1,3... | collective-permute-start | bytes 589832 | tf_op jit(solution)/shard_map/ppermute | solution.py:317
  146.8 5.0 %collective-permute-done.14.ru = f32[2,64,384]{2,1,0:T(8,128)S(1)} collective-permute-done((f32[2,64,384]{2,1,0:T(8,128)S(1)}, f32[2,64,384]{2,1,0:T(8,128)S(1)}, u32[]{:S(2)}, u32[]{:S(2)}) %collective-permute-start.14) | collective-permute-done | bytes 196640 | tf_op jit(solution)/shard_map/ppermute | solution.py:317
  151.8 6.3 %collective-permute-done.15.rd = f32[2,64,384]{2,1,0:T(8,128)S(1)} collective-permute-done((f32[2,64,384]{2,1,0:T(8,128)S(1)}, f32[2,64,384]{2,1,0:T(8,128)S(1)}, u32[]{:S(2)}, u32[]{:S(2)}) %collective-permute-start.15) | collective-permute-done | bytes 196640 | tf_op jit(solution)/shard_map/ppermute | solution.py:317
  167.7 7.2 %all-to-all-start.3 = ((f32[32,32,128]{2,1,0:T(8,128)}), f32[32,32,128]{2,1,0:T(8,128)S(1)}, u32[]{:S(2)}, u32[]{:S(2)}) async-start(f32[32,32,128]{2,1,0:T(8,128)} %bitcast.6), calls=%async_computation.3 | async-start | bytes 1048576 | tf_op jit(solution)/shard_map/all_to_all | solution.py:342
  174.9 7.3 %collective-permute-start.19 = (f32[256,128]{1,0:T(8,128)}, f32[256,128]{1,0:T(8,128)S(1)}, u32[]{:S(2)}, u32[]{:S(2)}) collective-permute-start(f32[256,128]{1,0:T(8,128)} %get-tuple-element.59), channel_id=1, source_target_pairs={{0,1},{1,2},{2,3},{3,4},{4,5},{5,6},{6,7},{7,8},{8,9},{9,10},{10,1... | collective-permute-start | bytes 393224 | tf_op jit(solution)/shard_map/ppermute | solution.py:317
  184.5 5.5 %collective-permute-done.20.east = f32[256,128]{1,0:T(8,128)S(1)} collective-permute-done((f32[256,128]{1,0:T(8,128)S(1)}, f32[256,128]{1,0:T(8,128)S(1)}, u32[]{:S(2)}, u32[]{:S(2)}) %collective-permute-start.20) | collective-permute-done | bytes 131104 | tf_op jit(solution)/shard_map/ppermute | solution.py:317
  (77 shorter events, 40.6 us)
Async XLA Ops:
  1.8 8.2 %collective-permute-start = (f32[256,128]{1,0:T(8,128)S(1)}, f32[256,128]{1,0:T(8,128)S(1)}, u32[]{:S(2)}, u32[]{:S(2)}) collective-permute-start(f32[256,128]{1,0:T(8,128)S(1)} %get-tuple-element.33), channel_id=1, source_target_pairs={{0,1},{1,2},{2,3},{3,4},{4,5},{5,6},{6,7},{7,8},{8,9},{9,10},{10,1... | collective-permute-start | bytes 393224 | tf_op jit(solution)/shard_map/ppermute | solution.py:317
  8.1 7.2 %collective-permute-start.1 = (f32[256,128]{1,0:T(8,128)S(1)}, f32[256,128]{1,0:T(8,128)S(1)}, u32[]{:S(2)}, u32[]{:S(2)}) collective-permute-start(f32[256,128]{1,0:T(8,128)S(1)} %get-tuple-element.34), channel_id=1, source_target_pairs={{1,0},{2,1},{3,2},{4,3},{5,4},{6,5},{7,6},{8,7},{9,8},{10,9},{11,1... | collective-permute-start | bytes 393224 | tf_op jit(solution)/shard_map/ppermute | solution.py:317
  16.5 6.2 %collective-permute-start.2 = (f32[2,64,384]{2,1,0:T(8,128)S(1)}, f32[2,64,384]{2,1,0:T(8,128)S(1)}, u32[]{:S(2)}, u32[]{:S(2)}) collective-permute-start(f32[2,64,384]{2,1,0:T(8,128)S(1)} %get-tuple-element.35), channel_id=1, source_target_pairs={{0,32},{32,64},{64,96},{96,128},{128,160},{160,192},{192,224},{1,3... | collective-permute-start | bytes 589832 | tf_op jit(solution)/shard_map/ppermute | solution.py:317
  20.1 7.4 %collective-permute-start.3 = (f32[2,64,384]{2,1,0:T(8,128)S(1)}, f32[2,64,384]{2,1,0:T(8,128)S(1)}, u32[]{:S(2)}, u32[]{:S(2)}) collective-permute-start(f32[2,64,384]{2,1,0:T(8,128)S(1)} %get-tuple-element.37), channel_id=1, source_target_pairs={{32,0},{64,32},{96,64},{128,96},{160,128},{192,160},{224,192},{33,... | collective-permute-start | bytes 589832 | tf_op jit(solution)/shard_map/ppermute | solution.py:317
  40.4 26.9 %all-to-all-start = ((f32[32,32,128]{2,1,0:T(8,128)}), f32[32,32,128]{2,1,0:T(8,128)S(1)}, u32[]{:S(2)}, u32[]{:S(2)}) async-start(f32[32,32,128]{2,1,0:T(8,128)} %bitcast), calls=%async_computation | async-start | bytes 1048576 | tf_op jit(solution)/shard_map/all_to_all | solution.py:336
  51.7 15.5 %collective-permute-start.6 = (f32[2,128,384]{2,1,0:T(8,128)S(1)}, f32[2,128,384]{2,1,0:T(8,128)S(1)}, u32[]{:S(2)}, u32[]{:S(2)}) collective-permute-start(f32[2,128,384]{2,1,0:T(8,128)S(1)} %copy-done.8), channel_id=1, source_target_pairs={{32,0},{64,32},{96,64},{128,96},{160,128},{192,160},{224,192},{33,... | collective-permute-start | bytes 1179656 | tf_op jit(solution)/shard_map/ppermute | solution.py:317
  53.1 14.2 %collective-permute-start.5 = (f32[2,128,384]{2,1,0:T(8,128)S(1)}, f32[2,128,384]{2,1,0:T(8,128)S(1)}, u32[]{:S(2)}, u32[]{:S(2)}) collective-permute-start(f32[2,128,384]{2,1,0:T(8,128)S(1)} %copy-done.10), channel_id=1, source_target_pairs={{0,32},{32,64},{64,96},{96,128},{128,160},{160,192},{192,224},{1,3... | collective-permute-start | bytes 1179656 | tf_op jit(solution)/shard_map/ppermute | solution.py:317
  69.7 6.3 %collective-permute-start.9 = (f32[32,128]{1,0:T(8,128)S(1)}, f32[32,128]{1,0:T(8,128)S(1)}, u32[]{:S(2)}, u32[]{:S(2)}) collective-permute-start(f32[32,128]{1,0:T(8,128)S(1)} %get-tuple-element.46.a), channel_id=1, source_target_pairs={{0,6},{1,7},{2,4},{3,5},{4,2},{5,3},{6,0},{7,1},{8,14},{9,15},{10,... | collective-permute-start | bytes 49160 | tf_op jit(solution)/shard_map/ppermute | solution.py:321
  73.2 6.6 %collective-permute-start.8 = (f32[32,128]{1,0:T(8,128)S(1)}, f32[32,128]{1,0:T(8,128)S(1)}, u32[]{:S(2)}, u32[]{:S(2)}) collective-permute-start(f32[32,128]{1,0:T(8,128)S(1)} %get-tuple-element.46.a), channel_id=1, source_target_pairs={{0,4},{1,5},{2,6},{3,7},{4,0},{5,1},{6,2},{7,3},{8,12},{9,13},{10,... | collective-permute-start | bytes 49160 | tf_op jit(solution)/shard_map/ppermute | solution.py:321
  76.0 3.8 %collective-permute-start.7 = (f32[32,128]{1,0:T(8,128)S(1)}, f32[32,128]{1,0:T(8,128)S(1)}, u32[]{:S(2)}, u32[]{:S(2)}) collective-permute-start(f32[32,128]{1,0:T(8,128)S(1)} %get-tuple-element.46.a), channel_id=1, source_target_pairs={{0,2},{1,3},{2,0},{3,1},{4,6},{5,7},{6,4},{7,5},{8,10},{9,11},{10,... | collective-permute-start | bytes 49160 | tf_op jit(solution)/shard_map/ppermute | solution.py:321
  80.6 30.0 %all-to-all-start.1 = ((f32[32,32,128]{2,1,0:T(8,128)}), f32[32,32,128]{2,1,0:T(8,128)S(1)}, u32[]{:S(2)}, u32[]{:S(2)}) async-start(f32[32,32,128]{2,1,0:T(8,128)} %bitcast.2), calls=%async_computation.1 | async-start | bytes 1048576 | tf_op jit(solution)/shard_map/all_to_all | solution.py:342
  96.8 12.9 %collective-permute-start.11 = (f32[2,384,128]{2,1,0:T(8,128)S(1)}, f32[2,384,128]{2,1,0:T(8,128)S(1)}, u32[]{:S(2)}, u32[]{:S(2)}) collective-permute-start(f32[2,384,128]{2,1,0:T(8,128)S(1)} %get-tuple-element.43.refs_4_), channel_id=1, source_target_pairs={{1,0},{2,1},{3,2},{4,3},{5,4},{6,5},{7,6},{8,7},{9,8},{10,9},{11,1... | collective-permute-start | bytes 1179656 | tf_op jit(solution)/shard_map/ppermute | solution.py:317
  101.9 8.8 %collective-permute-start.10 = (f32[2,384,128]{2,1,0:T(8,128)S(1)}, f32[2,384,128]{2,1,0:T(8,128)S(1)}, u32[]{:S(2)}, u32[]{:S(2)}) collective-permute-start(f32[2,384,128]{2,1,0:T(8,128)S(1)} %get-tuple-element.45.refs_6_), channel_id=1, source_target_pairs={{0,1},{1,2},{2,3},{3,4},{4,5},{5,6},{6,7},{7,8},{8,9},{9,10},{10,1... | collective-permute-start | bytes 1179656 | tf_op jit(solution)/shard_map/ppermute | solution.py:317
  110.7 4.4 %collective-permute-start.12 = (f32[1024,128]{1,0:T(8,128)S(1)}, f32[1024,128]{1,0:T(8,128)S(1)}, u32[]{:S(2)}, u32[]{:S(2)}) collective-permute-start(f32[1024,128]{1,0:T(8,128)S(1)} %bitcast.12), channel_id=1, source_target_pairs={{0,1},{1,0},{2,3},{3,2},{4,5},{5,4},{6,7},{7,6},{8,9},{9,8},{10,11... | collective-permute-start | bytes 1572872 | tf_op jit(solution)/shard_map/ppermute | solution.py:321
  125.0 2.2 %collective-permute-start.13 = (f32[1024,128]{1,0:T(8,128)}, f32[1024,128]{1,0:T(8,128)S(1)}, u32[]{:S(2)}, u32[]{:S(2)}) collective-permute-start(f32[1024,128]{1,0:T(8,128)} %get-tuple-element.52), channel_id=1, source_target_pairs={{0,1},{1,0},{2,3},{3,2},{4,5},{5,4},{6,7},{7,6},{8,9},{9,8},{10,11... | collective-permute-start | bytes 1572872 | tf_op jit(solution)/shard_map/ppermute | solution.py:321
  129.2 28.8 %all-to-all-start.2 = ((f32[32,32,128]{2,1,0:T(8,128)}), f32[32,32,128]{2,1,0:T(8,128)S(1)}, u32[]{:S(2)}, u32[]{:S(2)}) async-start(f32[32,32,128]{2,1,0:T(8,128)} %bitcast.4), calls=%async_computation.2 | async-start | bytes 1048576 | tf_op jit(solution)/shard_map/all_to_all | solution.py:336
  142.3 9.5 %collective-permute-start.14 = (f32[2,64,384]{2,1,0:T(8,128)S(1)}, f32[2,64,384]{2,1,0:T(8,128)S(1)}, u32[]{:S(2)}, u32[]{:S(2)}) collective-permute-start(f32[2,64,384]{2,1,0:T(8,128)S(1)} %copy-done.18), channel_id=1, source_target_pairs={{0,32},{32,64},{64,96},{96,128},{128,160},{160,192},{192,224},{1,3... | collective-permute-start | bytes 589832 | tf_op jit(solution)/shard_map/ppermute | solution.py:317
  145.5 12.6 %collective-permute-start.15 = (f32[2,64,384]{2,1,0:T(8,128)S(1)}, f32[2,64,384]{2,1,0:T(8,128)S(1)}, u32[]{:S(2)}, u32[]{:S(2)}) collective-permute-start(f32[2,64,384]{2,1,0:T(8,128)S(1)} %copy-done.17), channel_id=1, source_target_pairs={{32,0},{64,32},{96,64},{128,96},{160,128},{192,160},{224,192},{33,... | collective-permute-start | bytes 589832 | tf_op jit(solution)/shard_map/ppermute | solution.py:317
  159.6 5.7 %collective-permute-start.18 = (f32[32,128]{1,0:T(8,128)S(1)}, f32[32,128]{1,0:T(8,128)S(1)}, u32[]{:S(2)}, u32[]{:S(2)}) collective-permute-start(f32[32,128]{1,0:T(8,128)S(1)} %get-tuple-element.58.a), channel_id=1, source_target_pairs={{0,6},{1,7},{2,4},{3,5},{4,2},{5,3},{6,0},{7,1},{8,14},{9,15},{10,... | collective-permute-start | bytes 49160 | tf_op jit(solution)/shard_map/ppermute | solution.py:321
  160.3 6.5 %collective-permute-start.17 = (f32[32,128]{1,0:T(8,128)S(1)}, f32[32,128]{1,0:T(8,128)S(1)}, u32[]{:S(2)}, u32[]{:S(2)}) collective-permute-start(f32[32,128]{1,0:T(8,128)S(1)} %get-tuple-element.58.a), channel_id=1, source_target_pairs={{0,4},{1,5},{2,6},{3,7},{4,0},{5,1},{6,2},{7,3},{8,12},{9,13},{10,... | collective-permute-start | bytes 49160 | tf_op jit(solution)/shard_map/ppermute | solution.py:321
  163.0 3.8 %collective-permute-start.16 = (f32[32,128]{1,0:T(8,128)S(1)}, f32[32,128]{1,0:T(8,128)S(1)}, u32[]{:S(2)}, u32[]{:S(2)}) collective-permute-start(f32[32,128]{1,0:T(8,128)S(1)} %get-tuple-element.58.a), channel_id=1, source_target_pairs={{0,2},{1,3},{2,0},{3,1},{4,6},{5,7},{6,4},{7,5},{8,10},{9,11},{10,... | collective-permute-start | bytes 49160 | tf_op jit(solution)/shard_map/ppermute | solution.py:321
  167.7 22.3 %all-to-all-start.3 = ((f32[32,32,128]{2,1,0:T(8,128)}), f32[32,32,128]{2,1,0:T(8,128)S(1)}, u32[]{:S(2)}, u32[]{:S(2)}) async-start(f32[32,32,128]{2,1,0:T(8,128)} %bitcast.6), calls=%async_computation.3 | async-start | bytes 1048576 | tf_op jit(solution)/shard_map/all_to_all | solution.py:342
  174.9 9.6 %collective-permute-start.19 = (f32[256,128]{1,0:T(8,128)}, f32[256,128]{1,0:T(8,128)S(1)}, u32[]{:S(2)}, u32[]{:S(2)}) collective-permute-start(f32[256,128]{1,0:T(8,128)} %get-tuple-element.59), channel_id=1, source_target_pairs={{0,1},{1,2},{2,3},{3,4},{4,5},{5,6},{6,7},{7,8},{8,9},{9,10},{10,1... | collective-permute-start | bytes 393224 | tf_op jit(solution)/shard_map/ppermute | solution.py:317
  182.2 7.7 %collective-permute-start.20 = (f32[256,128]{1,0:T(8,128)S(1)}, f32[256,128]{1,0:T(8,128)S(1)}, u32[]{:S(2)}, u32[]{:S(2)}) collective-permute-start(f32[256,128]{1,0:T(8,128)S(1)} %get-tuple-element.60), channel_id=1, source_target_pairs={{1,0},{2,1},{3,2},{4,3},{5,4},{6,5},{7,6},{8,7},{9,8},{10,9},{11,1... | collective-permute-start | bytes 393224 | tf_op jit(solution)/shard_map/ppermute | solution.py:317
  (21 other events, 265.6 us)

commit v2 on v1

--- a/solution.py
+++ b/solution.py
@@ -119,10 +119,12 @@
     count = 7 if first else 14
     arrays, refs = refs[:count], refs[count:]
     if first:
-        keep, send, gu, gm, gd, ext, canvas, outs, *inner, sems = refs
+        *stores, su, sd, own = refs[:5]
+        ext, canvas, raw, head, keep, send, outs, *inner, sems = refs[5:]
         up, mid, down, off, probe, amps, table = inner
     else:
-        keep, send, gu, gm, gd, obj, probe_out, ext, canvas, outs, probe, *inner, sems = refs
+        *stores, su, sd, own, obj, probe_out = refs[:7]
+        ext, canvas, raw, head, keep, send, outs, probe, *inner, sems = refs[7:]
         up, mid, down, off, cl, cm, cr, dl, dr, probe_in, mine, other, amps, table = inner
     wait = fetch(arrays, inner, sems)
     wait(*range(4 if first else 9))
@@ -156,7 +158,7 @@
         new_probe(core, probe_in, mine, other, probe)
         copies += store(
             ((ext.at[0, H:H + TILE], obj.at[0]), (ext.at[1, H:H + TILE], obj.at[1]),
-             (probe, probe_out)), outs.at[6:9])
+             (probe, probe_out)), outs.at[10:13])
     right, left = blocks(table)
     wave = jnp.concatenate(
         [
@@ -197,17 +199,35 @@
             s = slice((p * M + m) * F, (p * M + m + 1) * F)
             keep[s, :] = jnp.where(core == 0, term[:, :LANE], term[:, LANE:])
             send[s, :] = jnp.where(core == 0, term[:, LANE:], term[:, :LANE])
-    edge = gu.shape[1]
+    copies += store(zip((keep, send), stores), outs.at[8:10])
+    edge = (su.shape[0] - 8) // 2
+    skip = (SPAN - own.shape[1]) // 2
+    head[...] = jnp.full((8, F), o1.astype(f32))
     for c, value in enumerate((ore, oim)):
         canvas[c] = jnp.zeros((SPAN + 8, SPAN), f32)
+        raw[c] = jnp.zeros((SPAN + 8, F), f32)
         value = jnp.concatenate([value, jnp.zeros((8, F), f32)], axis=0)
         value = pltpu.roll(value, rest, 0)
-        value = jnp.concatenate([value, jnp.zeros((F + 8, SPAN - F), f32)], axis=1)
-        canvas[c, pl.ds(base, F + 8), :] = pltpu.roll(value, o1, 1)
+        raw[c, pl.ds(base, F + 8), :] = value
+        s = slice(c * edge, (c + 1) * edge)
         copies += store(
-            ((canvas.at[c, :edge], gu.at[c]), (canvas.at[c, SPAN - edge:SPAN], gd.at[c]),
-             (canvas.at[c, edge:SPAN - edge], gm.at[c])), outs.at[3 * c:3 * c + 3])
+            ((raw.at[c, :edge], su.at[s]), (raw.at[c, SPAN - edge:SPAN], sd.at[s])),
+            outs.at[2 * c:2 * c + 2])
+        canvas[c, pl.ds(base, F + 8), :] = shifted(value, o1)
+        copies += store(((canvas.at[c, skip:SPAN - skip], own.at[c]),), outs.at[4 + c:5 + c])
+    copies += store(((head, su.at[2 * edge:]), (head, sd.at[2 * edge:])), outs.at[6:8])
     finish(copies)
+
+
+def shifted(value, columns):
+    value = jnp.concatenate([value, jnp.zeros((value.shape[0], SPAN - F), f32)], axis=1)
+    return pltpu.roll(value, columns, 1)
+
+
+def arrived(strip, c):
+    edge = (strip.shape[0] - 8) // 2
+    columns = jnp.max(strip[2 * edge:, :LANE]).astype(jnp.int32)
+    return shifted(strip[c * edge:(c + 1) * edge, :], columns)
 
 
 def new_probe(core, probe, mine, other, out):
@@ -228,32 +248,33 @@
     out[...] = total
 
 
-def bands_kernel(parts, gu, gm, gd, ru, rd, total, cl, cm, cr, tl, tm, tr, outs, *inner):
+def bands_kernel(parts, own, ru, rd, total, cl, cm, cr, tl, tm, tr, outs, *inner):
     *inner, sems = inner
-    wait = fetch((gu, gm, gd, ru, rd), inner, sems)
-    gu, gm, gd, ru, rd = inner
+    wait = fetch((own, ru, rd), inner, sems)
+    own, ru, rd = inner
     chunk_sum(parts, total)
-    wait(*range(5))
+    wait(*range(3))
     for c in range(2):
+        above, below = arrived(ru, c), arrived(rd, c)
         for k, out in enumerate((tl, tm, tr)):
             s = slice(k * B, (k + 1) * B)
-            out[c, :B] = gu[c, :, s] + ru[c, :, s]
-            out[c, B:2 * B] = gm[c, :, s]
-            out[c, 2 * B:] = gd[c, :, s] + rd[c, :, s]
+            out[c, :B] = own[c, :B, s] + above[:, s]
+            out[c, B:2 * B] = own[c, B:2 * B, s]
+            out[c, 2 * B:] = own[c, 2 * B:, s] + below[:, s]
     finish(store(zip((tl, tm, tr), (cl, cm, cr)), outs))
 
 
-def last_bands_kernel(parts, gm, ru, rd, total, grad_out, left, right, grad, outs, *inner):
+def last_bands_kernel(parts, own, ru, rd, total, grad_out, left, right, grad, outs, *inner):
     *inner, sems = inner
-    wait = fetch((gm, ru, rd), inner, sems)
-    gm, ru, rd = inner
+    wait = fetch((own, ru, rd), inner, sems)
+    own, ru, rd = inner
     chunk_sum(parts, total)
     low = lanes()
     wait(*range(3))
     for c in range(2):
-        grad[c, :H] = gm[c, :H] + ru[c]
-        grad[c, H:TILE - H] = gm[c, H:TILE - H]
-        grad[c, TILE - H:] = gm[c, TILE - H:] + rd[c]
+        grad[c, :H] = own[c, :H] + arrived(ru, c)
+        grad[c, H:TILE - H] = own[c, H:TILE - H]
+        grad[c, TILE - H:] = own[c, TILE - H:] + arrived(rd, c)
     copies = store(((grad, grad_out),), outs)
     left[...] = jnp.where(low, grad[0, :, :LANE], half_turn(grad[1, :, :LANE]))
     right[...] = jnp.where(low, half_turn(grad[0, :, 2 * LANE:]), grad[1, :, 2 * LANE:])
@@ -338,9 +359,9 @@
 
 def gather(x, *early):
     parts = (x, exchange(x, 2), exchange(x, 4), exchange(x, 6))
+    parts, early = lax.optimization_barrier((parts, early))
     (x,) = call(spread_kernel, [(1024, LANE)], "spread")(*parts)
     x = lax.all_to_all(x, RC, 0, 0, axis_index_groups=groups(WIDE), tiled=True)
-    x, *early = lax.optimization_barrier((x, *early))
     return x, exchange(x, BIT_CORE), *early
 
 
@@ -356,41 +377,42 @@
     down = shift(top, "row", -1)
 
     halves = [(1024, LANE)] * 2
-    canvases = [pltpu.VMEM((2, SPAN + 8, SPAN), f32)] * 2
-    keep, send, gu, gm, gd = call(
+    held = [pltpu.VMEM((2, SPAN + 8, SPAN), f32)] * 2 + [pltpu.VMEM((2, SPAN + 8, F), f32)]
+    held += [pltpu.VMEM((8, F), f32)] + [pltpu.VMEM((1024, LANE), f32)] * 2
+    keep, send, su, sd, own = call(
         functools.partial(frame_kernel, True),
-        halves + [(2, B, SPAN)] * 3,
+        halves + [(2 * B + 8, F)] * 2 + [(2, SPAN, SPAN)],
         "frame1",
         VMEM_LIMIT,
         [HBM] * 7,
-        [VM] * 2 + [HBM] * 3,
-        canvases + [pltpu.SemaphoreType.DMA((6,))],
+        [HBM] * 5,
+        held + [pltpu.SemaphoreType.DMA((10,))],
     )(up, mid, down, offsets, probe, amplitudes, table)
-    ru = shift(gd, "row", 1)
-    rd = shift(gu, "row", -1)
+    ru = shift(sd, "row", 1)
+    rd = shift(su, "row", -1)
     total, cl, cm, cr = call(
         bands_kernel,
         [(CHUNK, LANE)] + [(2, SPAN, B)] * 3,
         "bands",
-        specs=[VM] + [HBM] * 5,
+        specs=[VM] + [HBM] * 3,
         places=[VM] + [HBM] * 3,
         scratch=[pltpu.VMEM((2, SPAN, B), f32)] * 3 + [pltpu.SemaphoreType.DMA((3,))],
-    )(scatter(keep, send), gu, gm, gd, ru, rd)
+    )(scatter(keep, send), own, ru, rd)
     dl = shift(cr, "col", 1)
     dr = shift(cl, "col", -1)
     mine, other, dl, dr = gather(total, dl, dr)
 
-    keep, send, gu, gm, gd, obj, probe = call(
+    keep, send, su, sd, own, obj, probe = call(
         functools.partial(frame_kernel, False),
-        halves + [(2, H, SPAN), (2, TILE, SPAN), (2, H, SPAN), (2, TILE, SPAN), (2, M, F, F)],
+        halves + [(2 * H + 8, F)] * 2 + [(2, TILE, SPAN)] * 2 + [(2, M, F, F)],
         "frame2",
         VMEM_LIMIT,
         [HBM] * 14,
-        [VM] * 2 + [HBM] * 5,
-        canvases + [pltpu.SemaphoreType.DMA((9,)), pltpu.VMEM((2, M, F, F), f32)],
+        [HBM] * 7,
+        held + [pltpu.SemaphoreType.DMA((13,)), pltpu.VMEM((2, M, F, F), f32)],
     )(up, mid, down, offsets, cl, cm, cr, dl, dr, probe, mine, other, amplitudes, table)
-    ru = shift(gd, "row", 1)
-    rd = shift(gu, "row", -1)
+    ru = shift(sd, "row", 1)
+    rd = shift(su, "row", -1)
     total, grad, left, right = call(
         last_bands_kernel,
         [(CHUNK, LANE), (2, TILE, SPAN)] + [(TILE, LANE)] * 2,
@@ -398,7 +420,7 @@
         specs=[VM] + [HBM] * 3,
         places=[VM, HBM, VM, VM],
         scratch=[pltpu.VMEM((2, TILE, SPAN), f32), pltpu.SemaphoreType.DMA((1,))],
-    )(scatter(keep, send), gm, ru, rd)
+    )(scatter(keep, send), own, ru, rd)
     west = shift(right, "col", 1)
     east = shift(left, "col", -1)
     mine, other, west, east = gather(total, west, east)

time: 195 us -> 187 us (0.959)
  starting transfers between devices: 104 us -> 70.3 us
  blocking collectives: 0 us -> 32.8 us
  Pallas kernels: 24.5 us -> 20.6 us
    all_to_all x0 -> x2, blocking collectives: none -> 32.8 us  [gather(): x = lax.all_to_all(x, RC, 0, 0, axis_index_groups=groups(WIDE), tiled=True)]
    all_to_all x2 -> x0, starting transfers between devices: 23.4 us -> none  [gather(): x = lax.all_to_all(x, RC, 0, 0, axis_index_groups=groups(WIDE), tiled=True)]
    ppermute x12, waiting for transfers between devices: 43.4 us -> 34.4 us  [shift(): return lax.ppermute(x, axis, pairs)]
    all_to_all x2, starting transfers between devices: 24.4 us -> 15.6 us  [scatter(): lax.all_to_all(x, RC, 0, 0, axis_index_groups=groups(WIDE), tiled=True)]
    ppermute x10, waiting for transfers between devices: 12.5 us -> 19.8 us  [exchange(): return lax.ppermute(x, RC, [(i, i ^ mask) for i in range(256)])]
    ppermute x12, starting transfers between devices: 41 us -> 34.8 us  [shift(): return lax.ppermute(x, axis, pairs)]
    ppermute x10, starting transfers between devices: 15.5 us -> 19.9 us  [exchange(): return lax.ppermute(x, RC, [(i, i ^ mask) for i in range(256)])]
    pallas_call x9, Pallas kernels: 24.5 us -> 20.6 us  [run(): pl.pallas_call(kernel, out_shape=[jax.ShapeDtypeStruct(s, f32) for s in o...]
  transfers between devices with their start and end apart: 26 -> 24, of which waited for: 16 -> 13; matrix products, arithmetic and copies ran while one was open for 0% -> 0% of each run, Pallas kernels for 0% -> 0%
where the time goes in v2:
time: 187 us; the launch traced here: 186 us
  starting transfers between devices  70.3 us (38%)
  waiting for transfers between devices  54.2 us (29%)
  blocking collectives  32.8 us (18%)
  Pallas kernels  20.6 us (11%)
  other arithmetic  4.04 us (2%)
  local copies, waits for them, and re-layouts  3.41 us (2%)
    ppermute x12, starting transfers between devices, shift(): return lax.ppermute(x, axis, pairs)  34.8 us
    ppermute x12, waiting for transfers between devices, shift(): return lax.ppermute(x, axis, pairs)  34.4 us
    all_to_all x2, blocking collectives, gather(): x = lax.all_to_all(x, RC, 0, 0, axis_index_groups=groups(WIDE), tiled=True)  32.8 us
    pallas_call x9, Pallas kernels, run(): pl.pallas_call(kernel, out_shape=[jax.ShapeDtypeStruct(s, f32) for s in o...  20.6 us
    ppermute x10, starting transfers between devices, exchange(): return lax.ppermute(x, RC, [(i, i ^ mask) for i in range(256)])  19.9 us
    ppermute x10, waiting for transfers between devices, exchange(): return lax.ppermute(x, RC, [(i, i ^ mask) for i in range(256)])  19.8 us
    all_to_all x2, starting transfers between devices, scatter(): lax.all_to_all(x, RC, 0, 0, axis_index_groups=groups(WIDE), tiled=True)  15.6 us
    add x2, other arithmetic, scatter(): x = keep + exchange(send, BIT_CORE)  4.04 us
  transfers between devices with their start and end apart: 24, of which 13 were waited for; matrix products, arithmetic and copies ran while one was open for 0% of the time, Pallas kernels for 0%

profile of v2, /device:TPU:1, one launch (start us, length us, event | category | flops | bytes accessed | tf_op | source)
XLA Modules:
  0.0 186.4 jit_solution(2600377398129079588)
XLA Ops:
  1.8 6.3 %collective-permute-start = (f32[256,128]{1,0:T(8,128)S(1)}, f32[256,128]{1,0:T(8,128)S(1)}, u32[]{:S(2)}, u32[]{:S(2)}) collective-permute-start(f32[256,128]{1,0:T(8,128)S(1)} %get-tuple-element.39), channel_id=1, source_target_pairs={{0,1},{1,2},{2,3},{3,4},{4,5},{5,6},{6,7},{7,8},{8,9},{9,10},{10,1... | collective-permute-start | bytes 393224 | tf_op jit(solution)/shard_map/ppermute | solution.py:338
  10.0 5.3 %collective-permute-done.1.east = f32[256,128]{1,0:T(8,128)S(1)} collective-permute-done((f32[256,128]{1,0:T(8,128)S(1)}, f32[256,128]{1,0:T(8,128)S(1)}, u32[]{:S(2)}, u32[]{:S(2)}) %collective-permute-start.1) | collective-permute-done | bytes 131104 | tf_op jit(solution)/shard_map/ppermute | solution.py:338
  16.5 3.6 %collective-permute-start.2 = (f32[2,64,384]{2,1,0:T(8,128)S(1)}, f32[2,64,384]{2,1,0:T(8,128)S(1)}, u32[]{:S(2)}, u32[]{:S(2)}) collective-permute-start(f32[2,64,384]{2,1,0:T(8,128)S(1)} %get-tuple-element.41), channel_id=1, source_target_pairs={{0,32},{32,64},{64,96},{96,128},{128,160},{160,192},{192,224},{1,3... | collective-permute-start | bytes 589832 | tf_op jit(solution)/shard_map/ppermute | solution.py:338
  22.6 4.8 %collective-permute-done.3.refs_2_ = f32[2,64,384]{2,1,0:T(8,128)S(1)} collective-permute-done((f32[2,64,384]{2,1,0:T(8,128)S(1)}, f32[2,64,384]{2,1,0:T(8,128)S(1)}, u32[]{:S(2)}, u32[]{:S(2)}) %collective-permute-start.3) | collective-permute-done | bytes 196640 | tf_op jit(solution)/shard_map/ppermute | solution.py:338
  28.1 7.5 %frame1.1 = (f32[1024,128]{1,0:T(8,128)}, f32[1024,128]{1,0:T(8,128)}, f32[264,256]{1,0:T(8,128)}, f32[264,256]{1,0:T(8,128)}, f32[2,384,384]{2,1,0:T(8,128)}) custom-call(f32[2,64,384]{2,1,0:T(8,128)} %copy-done.10, f32[2,256,384]{2,1,0:T(8,128)} %copy-done, f32[2,64,384]{2,1,0:T(8,128)} %copy-done.11, s32[1,1,1,2]{3,2,1,0:T(1,128)} %refs_3_.3, ...), custom_call_target="tpu_custom_call" | custom-call | tf_op jit(solution)/shard_map/frame1/pallas_call | solution.py:322
  39.9 11.2 %all-to-all-start = ((f32[32,32,128]{2,1,0:T(8,128)}), f32[32,32,128]{2,1,0:T(8,128)S(1)}, u32[]{:S(2)}, u32[]{:S(2)}) async-start(f32[32,32,128]{2,1,0:T(8,128)} %bitcast), calls=%async_computation | async-start | bytes 1048576 | tf_op jit(solution)/shard_map/all_to_all | solution.py:357
  51.1 3.2 %collective-permute-start.5 = (f32[264,256]{1,0:T(8,128)S(1)}, f32[264,256]{1,0:T(8,128)S(1)}, u32[]{:S(2)}, u32[]{:S(2)}) collective-permute-start(f32[264,256]{1,0:T(8,128)S(1)} %copy-done.16), channel_id=1, source_target_pairs={{0,32},{32,64},{64,96},{96,128},{128,160},{160,192},{192,224},{1,3... | collective-permute-start | bytes 811016 | tf_op jit(solution)/shard_map/ppermute | solution.py:338
  55.6 6.6 %collective-permute-done.5.ru = f32[264,256]{1,0:T(8,128)S(1)} collective-permute-done((f32[264,256]{1,0:T(8,128)S(1)}, f32[264,256]{1,0:T(8,128)S(1)}, u32[]{:S(2)}, u32[]{:S(2)}) %collective-permute-start.5) | collective-permute-done | bytes 270368 | tf_op jit(solution)/shard_map/ppermute | solution.py:338
  62.2 7.8 %collective-permute-done.6.rd = f32[264,256]{1,0:T(8,128)S(1)} collective-permute-done((f32[264,256]{1,0:T(8,128)S(1)}, f32[264,256]{1,0:T(8,128)S(1)}, u32[]{:S(2)}, u32[]{:S(2)}) %collective-permute-start.6) | collective-permute-done | bytes 270368 | tf_op jit(solution)/shard_map/ppermute | solution.py:338
  71.4 3.4 %collective-permute-start.11 = (f32[2,384,128]{2,1,0:T(8,128)S(1)}, f32[2,384,128]{2,1,0:T(8,128)S(1)}, u32[]{:S(2)}, u32[]{:S(2)}) collective-permute-start(f32[2,384,128]{2,1,0:T(8,128)S(1)} %get-tuple-element.49.refs_4_), channel_id=1, source_target_pairs={{1,0},{2,1},{3,2},{4,3},{5,4},{6,5},{7,6},{8,7},{9,8},{10,9},{11,1... | collective-permute-start | bytes 1179656 | tf_op jit(solution)/shard_map/ppermute | solution.py:338
  74.9 4.6 %collective-permute-start.10 = (f32[2,384,128]{2,1,0:T(8,128)S(1)}, f32[2,384,128]{2,1,0:T(8,128)S(1)}, u32[]{:S(2)}, u32[]{:S(2)}) collective-permute-start(f32[2,384,128]{2,1,0:T(8,128)S(1)} %get-tuple-element.51.refs_6_), channel_id=1, source_target_pairs={{0,1},{1,2},{2,3},{3,4},{4,5},{5,6},{6,7},{7,8},{8,9},{9,10},{10,1... | collective-permute-start | bytes 1179656 | tf_op jit(solution)/shard_map/ppermute | solution.py:338
  79.5 4.1 %collective-permute-start.9 = (f32[32,128]{1,0:T(8,128)S(1)}, f32[32,128]{1,0:T(8,128)S(1)}, u32[]{:S(2)}, u32[]{:S(2)}) collective-permute-start(f32[32,128]{1,0:T(8,128)S(1)} %get-tuple-element.55.a), channel_id=1, source_target_pairs={{0,6},{1,7},{2,4},{3,5},{4,2},{5,3},{6,0},{7,1},{8,14},{9,15},{10,... | collective-permute-start | bytes 49160 | tf_op jit(solution)/shard_map/ppermute | solution.py:342
  85.7 7.8 %collective-permute-done.9.d = f32[32,128]{1,0:T(8,128)S(1)} collective-permute-done((f32[32,128]{1,0:T(8,128)S(1)}, f32[32,128]{1,0:T(8,128)S(1)}, u32[]{:S(2)}, u32[]{:S(2)}) %collective-permute-start.9) | collective-permute-done | bytes 16416 | tf_op jit(solution)/shard_map/ppermute | solution.py:342
  93.7 17.4 %all_to_all.44 = f32[32,32,128]{2,1,0:T(8,128)S(1)} all-to-all(f32[32,32,128]{2,1,0:T(8,128)S(1)} %bitcast.12), channel_id=1, replica_groups={{0,8,16,24,32,40,48,56,64,72,80,88,96,104,112,120,128,136,144,152,160,1..., dimensions={0} | all-to-all | bytes 1048576 | tf_op jit(solution)/shard_map/all_to_all | solution.py:364
  115.6 8.4 %frame2.1 = (f32[1024,128]{1,0:T(8,128)}, f32[1024,128]{1,0:T(8,128)}, f32[136,256]{1,0:T(8,128)}, f32[136,256]{1,0:T(8,128)}, f32[2,256,384]{2,1,0:T(8,128)}, /...) custom-call(f32[2,64,384]{2,1,0:T(8,128)} %copy-done.10, f32[2,256,384]{2,1,0:T(8,128)} %copy-done, ...), custom_call_target="tpu_custom_call" | custom-call | tf_op jit(solution)/shard_map/frame2/pallas_call | solution.py:322
  128.3 4.3 %all-to-all-start.2 = ((f32[32,32,128]{2,1,0:T(8,128)}), f32[32,32,128]{2,1,0:T(8,128)S(1)}, u32[]{:S(2)}, u32[]{:S(2)}) async-start(f32[32,32,128]{2,1,0:T(8,128)} %bitcast.4), calls=%async_computation.2 | async-start | bytes 1048576 | tf_op jit(solution)/shard_map/all_to_all | solution.py:357
  132.6 3.1 %collective-permute-start.14 = (f32[136,256]{1,0:T(8,128)S(1)}, f32[136,256]{1,0:T(8,128)S(1)}, u32[]{:S(2)}, u32[]{:S(2)}) collective-permute-start(f32[136,256]{1,0:T(8,128)S(1)} %copy-done.18), channel_id=1, source_target_pairs={{0,32},{32,64},{64,96},{96,128},{128,160},{160,192},{192,224},{1,3... | collective-permute-start | bytes 417800 | tf_op jit(solution)/shard_map/ppermute | solution.py:338
  137.1 3.8 %collective-permute-done.14.ru = f32[136,256]{1,0:T(8,128)S(1)} collective-permute-done((f32[136,256]{1,0:T(8,128)S(1)}, f32[136,256]{1,0:T(8,128)S(1)}, u32[]{:S(2)}, u32[]{:S(2)}) %collective-permute-start.14) | collective-permute-done | bytes 139296 | tf_op jit(solution)/shard_map/ppermute | solution.py:338
  140.9 4.8 %collective-permute-done.15.rd = f32[136,256]{1,0:T(8,128)S(1)} collective-permute-done((f32[136,256]{1,0:T(8,128)S(1)}, f32[136,256]{1,0:T(8,128)S(1)}, u32[]{:S(2)}, u32[]{:S(2)}) %collective-permute-start.15) | collective-permute-done | bytes 139296 | tf_op jit(solution)/shard_map/ppermute | solution.py:338
  146.7 2.8 %collective-permute-start.19 = (f32[256,128]{1,0:T(8,128)S(1)}, f32[256,128]{1,0:T(8,128)S(1)}, u32[]{:S(2)}, u32[]{:S(2)}) collective-permute-start(f32[256,128]{1,0:T(8,128)S(1)} %get-tuple-element.68), channel_id=1, source_target_pairs={{0,1},{1,2},{2,3},{3,4},{4,5},{5,6},{6,7},{7,8},{8,9},{9,10},{10,1... | collective-permute-start | bytes 393224 | tf_op jit(solution)/shard_map/ppermute | solution.py:338
  151.5 5.1 %collective-permute-start.18 = (f32[32,128]{1,0:T(8,128)S(1)}, f32[32,128]{1,0:T(8,128)S(1)}, u32[]{:S(2)}, u32[]{:S(2)}) collective-permute-start(f32[32,128]{1,0:T(8,128)S(1)} %get-tuple-element.72.a), channel_id=1, source_target_pairs={{0,6},{1,7},{2,4},{3,5},{4,2},{5,3},{6,0},{7,1},{8,14},{9,15},{10,... | collective-permute-start | bytes 49160 | tf_op jit(solution)/shard_map/ppermute | solution.py:342
  158.8 5.1 %collective-permute-done.17.c = f32[32,128]{1,0:T(8,128)S(1)} collective-permute-done((f32[32,128]{1,0:T(8,128)S(1)}, f32[32,128]{1,0:T(8,128)S(1)}, u32[]{:S(2)}, u32[]{:S(2)}) %collective-permute-start.17) | collective-permute-done | bytes 16416 | tf_op jit(solution)/shard_map/ppermute | solution.py:342
  164.0 15.4 %all_to_all.45 = f32[32,32,128]{2,1,0:T(8,128)S(1)} all-to-all(f32[32,32,128]{2,1,0:T(8,128)S(1)} %bitcast.13), channel_id=1, replica_groups={{0,8,16,24,32,40,48,56,64,72,80,88,96,104,112,120,128,136,144,152,160,1..., dimensions={0} | all-to-all | bytes 1048576 | tf_op jit(solution)/shard_map/all_to_all | solution.py:364
  179.3 3.6 %collective-permute-start.21 = (f32[1024,128]{1,0:T(8,128)S(1)}, f32[1024,128]{1,0:T(8,128)S(1)}, u32[]{:S(2)}, u32[]{:S(2)}) collective-permute-start(f32[1024,128]{1,0:T(8,128)S(1)} %bitcast.10), channel_id=1, source_target_pairs={{0,1},{1,0},{2,3},{3,2},{4,5},{5,4},{6,7},{7,6},{8,9},{9,8},{10,11... | collective-permute-start | bytes 1572872 | tf_op jit(solution)/shard_map/ppermute | solution.py:342
  (75 shorter events, 35.3 us)
Async XLA Ops:
  1.8 8.2 %collective-permute-start = (f32[256,128]{1,0:T(8,128)S(1)}, f32[256,128]{1,0:T(8,128)S(1)}, u32[]{:S(2)}, u32[]{:S(2)}) collective-permute-start(f32[256,128]{1,0:T(8,128)S(1)} %get-tuple-element.39), channel_id=1, source_target_pairs={{0,1},{1,2},{2,3},{3,4},{4,5},{5,6},{6,7},{7,8},{8,9},{9,10},{10,1... | collective-permute-start | bytes 393224 | tf_op jit(solution)/shard_map/ppermute | solution.py:338
  8.1 7.2 %collective-permute-start.1 = (f32[256,128]{1,0:T(8,128)S(1)}, f32[256,128]{1,0:T(8,128)S(1)}, u32[]{:S(2)}, u32[]{:S(2)}) collective-permute-start(f32[256,128]{1,0:T(8,128)S(1)} %get-tuple-element.40), channel_id=1, source_target_pairs={{1,0},{2,1},{3,2},{4,3},{5,4},{6,5},{7,6},{8,7},{9,8},{10,9},{11,1... | collective-permute-start | bytes 393224 | tf_op jit(solution)/shard_map/ppermute | solution.py:338
  16.5 6.2 %collective-permute-start.2 = (f32[2,64,384]{2,1,0:T(8,128)S(1)}, f32[2,64,384]{2,1,0:T(8,128)S(1)}, u32[]{:S(2)}, u32[]{:S(2)}) collective-permute-start(f32[2,64,384]{2,1,0:T(8,128)S(1)} %get-tuple-element.41), channel_id=1, source_target_pairs={{0,32},{32,64},{64,96},{96,128},{128,160},{160,192},{192,224},{1,3... | collective-permute-start | bytes 589832 | tf_op jit(solution)/shard_map/ppermute | solution.py:338
  20.1 7.4 %collective-permute-start.3 = (f32[2,64,384]{2,1,0:T(8,128)S(1)}, f32[2,64,384]{2,1,0:T(8,128)S(1)}, u32[]{:S(2)}, u32[]{:S(2)}) collective-permute-start(f32[2,64,384]{2,1,0:T(8,128)S(1)} %get-tuple-element.43), channel_id=1, source_target_pairs={{32,0},{64,32},{96,64},{128,96},{160,128},{192,160},{224,192},{33,... | collective-permute-start | bytes 589832 | tf_op jit(solution)/shard_map/ppermute | solution.py:338
  35.7 2.2 %collective-permute-start.4 = (f32[1024,128]{1,0:T(8,128)}, f32[1024,128]{1,0:T(8,128)S(1)}, u32[]{:S(2)}, u32[]{:S(2)}) collective-permute-start(f32[1024,128]{1,0:T(8,128)} %get-tuple-element.45), channel_id=1, source_target_pairs={{0,1},{1,0},{2,3},{3,2},{4,5},{5,4},{6,7},{7,6},{8,9},{9,8},{10,11... | collective-permute-start | bytes 1572872 | tf_op jit(solution)/shard_map/ppermute | solution.py:342
  39.9 30.1 %all-to-all-start = ((f32[32,32,128]{2,1,0:T(8,128)}), f32[32,32,128]{2,1,0:T(8,128)S(1)}, u32[]{:S(2)}, u32[]{:S(2)}) async-start(f32[32,32,128]{2,1,0:T(8,128)} %bitcast), calls=%async_computation | async-start | bytes 1048576 | tf_op jit(solution)/shard_map/all_to_all | solution.py:357
  51.1 11.1 %collective-permute-start.5 = (f32[264,256]{1,0:T(8,128)S(1)}, f32[264,256]{1,0:T(8,128)S(1)}, u32[]{:S(2)}, u32[]{:S(2)}) collective-permute-start(f32[264,256]{1,0:T(8,128)S(1)} %copy-done.16), channel_id=1, source_target_pairs={{0,32},{32,64},{64,96},{96,128},{128,160},{160,192},{192,224},{1,3... | collective-permute-start | bytes 811016 | tf_op jit(solution)/shard_map/ppermute | solution.py:338
  54.3 15.7 %collective-permute-start.6 = (f32[264,256]{1,0:T(8,128)S(1)}, f32[264,256]{1,0:T(8,128)S(1)}, u32[]{:S(2)}, u32[]{:S(2)}) collective-permute-start(f32[264,256]{1,0:T(8,128)S(1)} %copy-done.15), channel_id=1, source_target_pairs={{32,0},{64,32},{96,64},{128,96},{160,128},{192,160},{224,192},{33,... | collective-permute-start | bytes 811016 | tf_op jit(solution)/shard_map/ppermute | solution.py:338
  71.4 22.1 %collective-permute-start.11 = (f32[2,384,128]{2,1,0:T(8,128)S(1)}, f32[2,384,128]{2,1,0:T(8,128)S(1)}, u32[]{:S(2)}, u32[]{:S(2)}) collective-permute-start(f32[2,384,128]{2,1,0:T(8,128)S(1)} %get-tuple-element.49.refs_4_), channel_id=1, source_target_pairs={{1,0},{2,1},{3,2},{4,3},{5,4},{6,5},{7,6},{8,7},{9,8},{10,9},{11,1... | collective-permute-start | bytes 1179656 | tf_op jit(solution)/shard_map/ppermute | solution.py:338
  74.9 18.7 %collective-permute-start.10 = (f32[2,384,128]{2,1,0:T(8,128)S(1)}, f32[2,384,128]{2,1,0:T(8,128)S(1)}, u32[]{:S(2)}, u32[]{:S(2)}) collective-permute-start(f32[2,384,128]{2,1,0:T(8,128)S(1)} %get-tuple-element.51.refs_6_), channel_id=1, source_target_pairs={{0,1},{1,2},{2,3},{3,4},{4,5},{5,6},{6,7},{7,8},{8,9},{9,10},{10,1... | collective-permute-start | bytes 1179656 | tf_op jit(solution)/shard_map/ppermute | solution.py:338
  79.5 14.1 %collective-permute-start.9 = (f32[32,128]{1,0:T(8,128)S(1)}, f32[32,128]{1,0:T(8,128)S(1)}, u32[]{:S(2)}, u32[]{:S(2)}) collective-permute-start(f32[32,128]{1,0:T(8,128)S(1)} %get-tuple-element.55.a), channel_id=1, source_target_pairs={{0,6},{1,7},{2,4},{3,5},{4,2},{5,3},{6,0},{7,1},{8,14},{9,15},{10,... | collective-permute-start | bytes 49160 | tf_op jit(solution)/shard_map/ppermute | solution.py:342
  83.5 10.0 %collective-permute-start.8 = (f32[32,128]{1,0:T(8,128)S(1)}, f32[32,128]{1,0:T(8,128)S(1)}, u32[]{:S(2)}, u32[]{:S(2)}) collective-permute-start(f32[32,128]{1,0:T(8,128)S(1)} %get-tuple-element.55.a), channel_id=1, source_target_pairs={{0,4},{1,5},{2,6},{3,7},{4,0},{5,1},{6,2},{7,3},{8,12},{9,13},{10,... | collective-permute-start | bytes 49160 | tf_op jit(solution)/shard_map/ppermute | solution.py:342
  85.5 8.0 %collective-permute-start.7 = (f32[32,128]{1,0:T(8,128)S(1)}, f32[32,128]{1,0:T(8,128)S(1)}, u32[]{:S(2)}, u32[]{:S(2)}) collective-permute-start(f32[32,128]{1,0:T(8,128)S(1)} %get-tuple-element.55.a), channel_id=1, source_target_pairs={{0,2},{1,3},{2,0},{3,1},{4,6},{5,7},{6,4},{7,5},{8,10},{9,11},{10,... | collective-permute-start | bytes 49160 | tf_op jit(solution)/shard_map/ppermute | solution.py:342
  111.1 3.7 %collective-permute-start.12 = (f32[1024,128]{1,0:T(8,128)S(1)}, f32[1024,128]{1,0:T(8,128)S(1)}, u32[]{:S(2)}, u32[]{:S(2)}) collective-permute-start(f32[1024,128]{1,0:T(8,128)S(1)} %bitcast.14), channel_id=1, source_target_pairs={{0,1},{1,0},{2,3},{3,2},{4,5},{5,4},{6,7},{7,6},{8,9},{9,8},{10,11... | collective-permute-start | bytes 1572872 | tf_op jit(solution)/shard_map/ppermute | solution.py:342
  124.0 2.2 %collective-permute-start.13 = (f32[1024,128]{1,0:T(8,128)}, f32[1024,128]{1,0:T(8,128)S(1)}, u32[]{:S(2)}, u32[]{:S(2)}) collective-permute-start(f32[1024,128]{1,0:T(8,128)} %get-tuple-element.61), channel_id=1, source_target_pairs={{0,1},{1,0},{2,3},{3,2},{4,5},{5,4},{6,7},{7,6},{8,9},{9,8},{10,11... | collective-permute-start | bytes 1572872 | tf_op jit(solution)/shard_map/ppermute | solution.py:342
  128.3 17.4 %all-to-all-start.2 = ((f32[32,32,128]{2,1,0:T(8,128)}), f32[32,32,128]{2,1,0:T(8,128)S(1)}, u32[]{:S(2)}, u32[]{:S(2)}) async-start(f32[32,32,128]{2,1,0:T(8,128)} %bitcast.4), calls=%async_computation.2 | async-start | bytes 1048576 | tf_op jit(solution)/shard_map/all_to_all | solution.py:357
  132.6 8.3 %collective-permute-start.14 = (f32[136,256]{1,0:T(8,128)S(1)}, f32[136,256]{1,0:T(8,128)S(1)}, u32[]{:S(2)}, u32[]{:S(2)}) collective-permute-start(f32[136,256]{1,0:T(8,128)S(1)} %copy-done.18), channel_id=1, source_target_pairs={{0,32},{32,64},{64,96},{96,128},{128,160},{160,192},{192,224},{1,3... | collective-permute-start | bytes 417800 | tf_op jit(solution)/shard_map/ppermute | solution.py:338
  135.8 9.9 %collective-permute-start.15 = (f32[136,256]{1,0:T(8,128)S(1)}, f32[136,256]{1,0:T(8,128)S(1)}, u32[]{:S(2)}, u32[]{:S(2)}) collective-permute-start(f32[136,256]{1,0:T(8,128)S(1)} %copy-done.17), channel_id=1, source_target_pairs={{32,0},{64,32},{96,64},{128,96},{160,128},{192,160},{224,192},{33,... | collective-permute-start | bytes 417800 | tf_op jit(solution)/shard_map/ppermute | solution.py:338
  146.7 17.2 %collective-permute-start.19 = (f32[256,128]{1,0:T(8,128)S(1)}, f32[256,128]{1,0:T(8,128)S(1)}, u32[]{:S(2)}, u32[]{:S(2)}) collective-permute-start(f32[256,128]{1,0:T(8,128)S(1)} %get-tuple-element.68), channel_id=1, source_target_pairs={{0,1},{1,2},{2,3},{3,4},{4,5},{5,6},{6,7},{7,8},{8,9},{9,10},{10,1... | collective-permute-start | bytes 393224 | tf_op jit(solution)/shard_map/ppermute | solution.py:338
  149.5 14.4 %collective-permute-start.20 = (f32[256,128]{1,0:T(8,128)S(1)}, f32[256,128]{1,0:T(8,128)S(1)}, u32[]{:S(2)}, u32[]{:S(2)}) collective-permute-start(f32[256,128]{1,0:T(8,128)S(1)} %get-tuple-element.69), channel_id=1, source_target_pairs={{1,0},{2,1},{3,2},{4,3},{5,4},{6,5},{7,6},{8,7},{9,8},{10,9},{11,1... | collective-permute-start | bytes 393224 | tf_op jit(solution)/shard_map/ppermute | solution.py:338
  151.5 7.3 %collective-permute-start.18 = (f32[32,128]{1,0:T(8,128)S(1)}, f32[32,128]{1,0:T(8,128)S(1)}, u32[]{:S(2)}, u32[]{:S(2)}) collective-permute-start(f32[32,128]{1,0:T(8,128)S(1)} %get-tuple-element.72.a), channel_id=1, source_target_pairs={{0,6},{1,7},{2,4},{3,5},{4,2},{5,3},{6,0},{7,1},{8,14},{9,15},{10,... | collective-permute-start | bytes 49160 | tf_op jit(solution)/shard_map/ppermute | solution.py:342
  156.6 7.3 %collective-permute-start.17 = (f32[32,128]{1,0:T(8,128)S(1)}, f32[32,128]{1,0:T(8,128)S(1)}, u32[]{:S(2)}, u32[]{:S(2)}) collective-permute-start(f32[32,128]{1,0:T(8,128)S(1)} %get-tuple-element.72.a), channel_id=1, source_target_pairs={{0,4},{1,5},{2,6},{3,7},{4,0},{5,1},{6,2},{7,3},{8,12},{9,13},{10,... | collective-permute-start | bytes 49160 | tf_op jit(solution)/shard_map/ppermute | solution.py:342
  157.5 6.4 %collective-permute-start.16 = (f32[32,128]{1,0:T(8,128)S(1)}, f32[32,128]{1,0:T(8,128)S(1)}, u32[]{:S(2)}, u32[]{:S(2)}) collective-permute-start(f32[32,128]{1,0:T(8,128)S(1)} %get-tuple-element.72.a), channel_id=1, source_target_pairs={{0,2},{1,3},{2,0},{3,1},{4,6},{5,7},{6,4},{7,5},{8,10},{9,11},{10,... | collective-permute-start | bytes 49160 | tf_op jit(solution)/shard_map/ppermute | solution.py:342
  179.3 5.2 %collective-permute-start.21 = (f32[1024,128]{1,0:T(8,128)S(1)}, f32[1024,128]{1,0:T(8,128)S(1)}, u32[]{:S(2)}, u32[]{:S(2)}) collective-permute-start(f32[1024,128]{1,0:T(8,128)S(1)} %bitcast.10), channel_id=1, source_target_pairs={{0,1},{1,0},{2,3},{3,2},{4,5},{5,4},{6,7},{7,6},{8,9},{9,8},{10,11... | collective-permute-start | bytes 1572872 | tf_op jit(solution)/shard_map/ppermute | solution.py:342
  (19 other events, 354.8 us)

commit v3 on v2

--- a/solution.py
+++ b/solution.py
@@ -240,20 +240,14 @@
         out[q // 2, q % 2] = probe[q // 2, q % 2] - coeff * total
 
 
-def chunk_sum(parts, out):
-    rows = out.shape[0]
-    total = parts[:rows, :]
-    for k in range(1, parts.shape[0] // rows):
-        total = total + parts[k * rows:(k + 1) * rows, :]
-    out[...] = total
-
-
-def bands_kernel(parts, own, ru, rd, total, cl, cm, cr, tl, tm, tr, outs, *inner):
+def bands_kernel(keep, recv, own, ru, rd, half, cl, cm, cr, th, tl, tm, tr, outs, *inner):
     *inner, sems = inner
-    wait = fetch((own, ru, rd), inner, sems)
-    own, ru, rd = inner
-    chunk_sum(parts, total)
-    wait(*range(3))
+    wait = fetch((keep, recv, own, ru, rd), inner, sems)
+    keep, recv, own, ru, rd = inner
+    wait(0, 1)
+    th[...] = keep[...] + recv[...]
+    copies = store(((th, half),), outs)
+    wait(2, 3, 4)
     for c in range(2):
         above, below = arrived(ru, c), arrived(rd, c)
         for k, out in enumerate((tl, tm, tr)):
@@ -261,21 +255,23 @@
             out[c, :B] = own[c, :B, s] + above[:, s]
             out[c, B:2 * B] = own[c, B:2 * B, s]
             out[c, 2 * B:] = own[c, 2 * B:, s] + below[:, s]
-    finish(store(zip((tl, tm, tr), (cl, cm, cr)), outs))
-
-
-def last_bands_kernel(parts, own, ru, rd, total, grad_out, left, right, grad, outs, *inner):
+    finish(copies + store(zip((tl, tm, tr), (cl, cm, cr)), outs.at[1:4]))
+
+
+def last_bands_kernel(keep, recv, own, ru, rd, half, grad_out, left, right, th, grad, outs, *inner):
     *inner, sems = inner
-    wait = fetch((own, ru, rd), inner, sems)
-    own, ru, rd = inner
-    chunk_sum(parts, total)
+    wait = fetch((keep, recv, own, ru, rd), inner, sems)
+    keep, recv, own, ru, rd = inner
+    wait(0, 1)
+    th[...] = keep[...] + recv[...]
+    copies = store(((th, half),), outs)
     low = lanes()
-    wait(*range(3))
+    wait(2, 3, 4)
     for c in range(2):
         grad[c, :H] = own[c, :H] + arrived(ru, c)
         grad[c, H:TILE - H] = own[c, H:TILE - H]
         grad[c, TILE - H:] = own[c, TILE - H:] + arrived(rd, c)
-    copies = store(((grad, grad_out),), outs)
+    copies += store(((grad, grad_out),), outs.at[1:2])
     left[...] = jnp.where(low, grad[0, :, :LANE], half_turn(grad[1, :, :LANE]))
     right[...] = jnp.where(low, half_turn(grad[0, :, 2 * LANE:]), grad[1, :, 2 * LANE:])
     finish(copies)
@@ -352,14 +348,11 @@
 CHUNK = 1024 // COUNT
 
 
-def scatter(keep, send):
-    x = keep + exchange(send, BIT_CORE)
-    return lax.all_to_all(x, RC, 0, 0, axis_index_groups=groups(WIDE), tiled=True)
-
-
-def gather(x, *early):
+def total_of(x, *early):
+    x = lax.all_to_all(x, RC, 0, 0, axis_index_groups=groups(WIDE), tiled=True)
+    x, early = lax.optimization_barrier((x, early))
+    x = x.reshape(COUNT, CHUNK, LANE).sum(axis=0)
     parts = (x, exchange(x, 2), exchange(x, 4), exchange(x, 6))
-    parts, early = lax.optimization_barrier((parts, early))
     (x,) = call(spread_kernel, [(1024, LANE)], "spread")(*parts)
     x = lax.all_to_all(x, RC, 0, 0, axis_index_groups=groups(WIDE), tiled=True)
     return x, exchange(x, BIT_CORE), *early
@@ -390,17 +383,20 @@
     )(up, mid, down, offsets, probe, amplitudes, table)
     ru = shift(sd, "row", 1)
     rd = shift(su, "row", -1)
-    total, cl, cm, cr = call(
+    half, cl, cm, cr = call(
         bands_kernel,
-        [(CHUNK, LANE)] + [(2, SPAN, B)] * 3,
+        [(1024, LANE)] + [(2, SPAN, B)] * 3,
         "bands",
-        specs=[VM] + [HBM] * 3,
-        places=[VM] + [HBM] * 3,
-        scratch=[pltpu.VMEM((2, SPAN, B), f32)] * 3 + [pltpu.SemaphoreType.DMA((3,))],
-    )(scatter(keep, send), own, ru, rd)
+        VMEM_LIMIT,
+        specs=[HBM] * 5,
+        places=[HBM] * 4,
+        scratch=[pltpu.VMEM((1024, LANE), f32)]
+        + [pltpu.VMEM((2, SPAN, B), f32)] * 3
+        + [pltpu.SemaphoreType.DMA((4,))],
+    )(keep, exchange(send, BIT_CORE), own, ru, rd)
     dl = shift(cr, "col", 1)
     dr = shift(cl, "col", -1)
-    mine, other, dl, dr = gather(total, dl, dr)
+    mine, other, dl, dr = total_of(half, dl, dr)
 
     keep, send, su, sd, own, obj, probe = call(
         functools.partial(frame_kernel, False),
@@ -413,17 +409,19 @@
     )(up, mid, down, offsets, cl, cm, cr, dl, dr, probe, mine, other, amplitudes, table)
     ru = shift(sd, "row", 1)
     rd = shift(su, "row", -1)
-    total, grad, left, right = call(
+    half, grad, left, right = call(
         last_bands_kernel,
-        [(CHUNK, LANE), (2, TILE, SPAN)] + [(TILE, LANE)] * 2,
+        [(1024, LANE), (2, TILE, SPAN)] + [(TILE, LANE)] * 2,
         "last_bands",
-        specs=[VM] + [HBM] * 3,
-        places=[VM, HBM, VM, VM],
-        scratch=[pltpu.VMEM((2, TILE, SPAN), f32), pltpu.SemaphoreType.DMA((1,))],
-    )(scatter(keep, send), own, ru, rd)
+        VMEM_LIMIT,
+        specs=[HBM] * 5,
+        places=[HBM, HBM, VM, VM],
+        scratch=[pltpu.VMEM((1024, LANE), f32), pltpu.VMEM((2, TILE, SPAN), f32)]
+        + [pltpu.SemaphoreType.DMA((2,))],
+    )(keep, exchange(send, BIT_CORE), own, ru, rd)
     west = shift(right, "col", 1)
     east = shift(left, "col", -1)
-    mine, other, west, east = gather(total, west, east)
+    mine, other, west, east = total_of(half, west, east)
     return tuple(
         call(
             last_kernel,

time: 187 us -> 194 us (1.037)
  starting transfers between devices: 70.3 us -> 75.1 us
  Pallas kernels: 20.6 us -> 24.8 us
  other arithmetic: 4.04 us -> 0.09 us
  waiting for transfers between devices: 54.2 us -> 52.1 us
    ppermute x10, waiting for transfers between devices: 19.8 us -> 11.4 us  [exchange(): return lax.ppermute(x, RC, [(i, i ^ mask) for i in range(256)])]
    ppermute x12, waiting for transfers between devices: 34.4 us -> 40.7 us  [shift(): return lax.ppermute(x, axis, pairs)]
    pallas_call x9, Pallas kernels: 20.6 us -> 24.8 us  [run(): pl.pallas_call(kernel, out_shape=[jax.ShapeDtypeStruct(s, f32) for s in o...]
    add x2 -> x0, other arithmetic: 4.04 us -> none  [scatter(): x = keep + exchange(send, BIT_CORE)]
    ppermute x10, starting transfers between devices: 19.9 us -> 22.9 us  [exchange(): return lax.ppermute(x, RC, [(i, i ^ mask) for i in range(256)])]
    unnamed x38 -> x34, local copies, waits for them, and re-layouts: 3.41 us -> 5.1 us
  transfers between devices with their start and end apart: 24 -> 24, of which waited for: 13 -> 16; matrix products, arithmetic and copies ran while one was open for 0% -> 0% of each run, Pallas kernels for 0% -> 0%
where the time goes in v3:
time: 194 us; the launch traced here: 193 us
  starting transfers between devices  75.1 us (39%)
  waiting for transfers between devices  52.1 us (27%)
  blocking collectives  34.6 us (18%)
  Pallas kernels  24.8 us (13%)
  local copies, waits for them, and re-layouts  5.1 us (3%)
    ppermute x12, waiting for transfers between devices, shift(): return lax.ppermute(x, axis, pairs)  40.7 us
    ppermute x12, starting transfers between devices, shift(): return lax.ppermute(x, axis, pairs)  36.5 us
    all_to_all x2, blocking collectives, total_of(): x = lax.all_to_all(x, RC, 0, 0, axis_index_groups=groups(WIDE), tiled=True)  34.6 us
    pallas_call x9, Pallas kernels, run(): pl.pallas_call(kernel, out_shape=[jax.ShapeDtypeStruct(s, f32) for s in o...  24.8 us
    ppermute x10, starting transfers between devices, exchange(): return lax.ppermute(x, RC, [(i, i ^ mask) for i in range(256)])  22.9 us
    all_to_all x2, starting transfers between devices, total_of(): x = lax.all_to_all(x, RC, 0, 0, axis_index_groups=groups(WIDE), tiled=True)  15.7 us
    ppermute x10, waiting for transfers between devices, exchange(): return lax.ppermute(x, RC, [(i, i ^ mask) for i in range(256)])  11.4 us
    unnamed x34, local copies, waits for them, and re-layouts  5.1 us
  transfers between devices with their start and end apart: 24, of which 16 were waited for; matrix products, arithmetic and copies ran while one was open for 0% of the time, Pallas kernels for 0%

profile of v3, /device:TPU:1, one launch (start us, length us, event | category | flops | bytes accessed | tf_op | source)
XLA Modules:
  0.0 192.9 jit_solution(782847876670980272)
XLA Ops:
  1.8 6.3 %collective-permute-start = (f32[256,128]{1,0:T(8,128)S(1)}, f32[256,128]{1,0:T(8,128)S(1)}, u32[]{:S(2)}, u32[]{:S(2)}) collective-permute-start(f32[256,128]{1,0:T(8,128)S(1)} %get-tuple-element.33), channel_id=1, source_target_pairs={{0,1},{1,2},{2,3},{3,4},{4,5},{5,6},{6,7},{7,8},{8,9},{9,10},{10,1... | collective-permute-start | bytes 393224 | tf_op jit(solution)/shard_map/ppermute | solution.py:334
  10.0 5.3 %collective-permute-done.1.east = f32[256,128]{1,0:T(8,128)S(1)} collective-permute-done((f32[256,128]{1,0:T(8,128)S(1)}, f32[256,128]{1,0:T(8,128)S(1)}, u32[]{:S(2)}, u32[]{:S(2)}) %collective-permute-start.1) | collective-permute-done | bytes 131104 | tf_op jit(solution)/shard_map/ppermute | solution.py:334
  16.5 3.6 %collective-permute-start.2 = (f32[2,64,384]{2,1,0:T(8,128)S(1)}, f32[2,64,384]{2,1,0:T(8,128)S(1)}, u32[]{:S(2)}, u32[]{:S(2)}) collective-permute-start(f32[2,64,384]{2,1,0:T(8,128)S(1)} %get-tuple-element.35), channel_id=1, source_target_pairs={{0,32},{32,64},{64,96},{96,128},{128,160},{160,192},{192,224},{1,3... | collective-permute-start | bytes 589832 | tf_op jit(solution)/shard_map/ppermute | solution.py:334
  22.6 4.8 %collective-permute-done.3.refs_2_ = f32[2,64,384]{2,1,0:T(8,128)S(1)} collective-permute-done((f32[2,64,384]{2,1,0:T(8,128)S(1)}, f32[2,64,384]{2,1,0:T(8,128)S(1)}, u32[]{:S(2)}, u32[]{:S(2)}) %collective-permute-start.3) | collective-permute-done | bytes 196640 | tf_op jit(solution)/shard_map/ppermute | solution.py:334
  28.1 7.5 %frame1.1 = (f32[1024,128]{1,0:T(8,128)}, f32[1024,128]{1,0:T(8,128)}, f32[264,256]{1,0:T(8,128)}, f32[264,256]{1,0:T(8,128)}, f32[2,384,384]{2,1,0:T(8,128)}) custom-call(f32[2,64,384]{2,1,0:T(8,128)} %copy-done.6, f32[2,256,384]{2,1,0:T(8,128)} %copy-done, f32[2,64,384]{2,1,0:T(8,128)} %copy-done.7, s32[1,1,1,2]{3,2,1,0:T(1,128)} %refs_3_.3, ...), custom_call_target="tpu_custom_call" | custom-call | tf_op jit(solution)/shard_map/frame1/pallas_call | solution.py:318
  35.7 3.7 %collective-permute-start.5 = (f32[264,256]{1,0:T(8,128)}, f32[264,256]{1,0:T(8,128)S(1)}, u32[]{:S(2)}, u32[]{:S(2)}) collective-permute-start(f32[264,256]{1,0:T(8,128)} %get-tuple-element.41), channel_id=1, source_target_pairs={{0,32},{32,64},{64,96},{96,128},{128,160},{160,192},{192,224},{1,3... | collective-permute-start | bytes 811016 | tf_op jit(solution)/shard_map/ppermute | solution.py:334
  40.7 4.3 %collective-permute-done.5.ru = f32[264,256]{1,0:T(8,128)S(1)} collective-permute-done((f32[264,256]{1,0:T(8,128)}, f32[264,256]{1,0:T(8,128)S(1)}, u32[]{:S(2)}, u32[]{:S(2)}) %collective-permute-start.5) | collective-permute-done | bytes 270368 | tf_op jit(solution)/shard_map/ppermute | solution.py:334
  45.0 7.2 %collective-permute-done.6.rd = f32[264,256]{1,0:T(8,128)S(1)} collective-permute-done((f32[264,256]{1,0:T(8,128)}, f32[264,256]{1,0:T(8,128)S(1)}, u32[]{:S(2)}, u32[]{:S(2)}) %collective-permute-start.6) | collective-permute-done | bytes 270368 | tf_op jit(solution)/shard_map/ppermute | solution.py:334
  56.3 10.5 %all-to-all-start = ((f32[32,32,128]{2,1,0:T(8,128)}), f32[32,32,128]{2,1,0:T(8,128)S(1)}, u32[]{:S(2)}, u32[]{:S(2)}) async-start(f32[32,32,128]{2,1,0:T(8,128)} %bitcast.16), calls=%async_computation | async-start | bytes 1048576 | tf_op jit(solution)/shard_map/all_to_all | solution.py:352
  69.8 4.2 %collective-permute-start.7 = (f32[2,384,128]{2,1,0:T(8,128)}, f32[2,384,128]{2,1,0:T(8,128)S(1)}, u32[]{:S(2)}, u32[]{:S(2)}) collective-permute-start(f32[2,384,128]{2,1,0:T(8,128)} %get-tuple-element.45.refs_6_), channel_id=1, source_target_pairs={{0,1},{1,2},{2,3},{3,4},{4,5},{5,6},{6,7},{7,8},{8,9},{9,10},{10,1... | collective-permute-start | bytes 1179656 | tf_op jit(solution)/shard_map/ppermute | solution.py:334
  74.0 4.2 %collective-permute-done.8.refs_8_ = f32[2,384,128]{2,1,0:T(8,128)S(1)} collective-permute-done((f32[2,384,128]{2,1,0:T(8,128)}, f32[2,384,128]{2,1,0:T(8,128)S(1)}, u32[]{:S(2)}, u32[]{:S(2)}) %collective-permute-start.8) | collective-permute-done | bytes 393248 | tf_op jit(solution)/shard_map/ppermute | solution.py:334
  79.2 3.8 %collective-permute-start.11 = (f32[32,128]{1,0:T(8,128)S(1)}, f32[32,128]{1,0:T(8,128)S(1)}, u32[]{:S(2)}, u32[]{:S(2)}) collective-permute-start(f32[32,128]{1,0:T(8,128)S(1)} %reduce_sum.18.a), channel_id=1, source_target_pairs={{0,6},{1,7},{2,4},{3,5},{4,2},{5,3},{6,0},{7,1},{8,14},{9,15},{10,... | collective-permute-start | bytes 49160 | tf_op jit(solution)/shard_map/ppermute | solution.py:338
  83.0 6.7 %collective-permute-start.10 = (f32[32,128]{1,0:T(8,128)S(1)}, f32[32,128]{1,0:T(8,128)S(1)}, u32[]{:S(2)}, u32[]{:S(2)}) collective-permute-start(f32[32,128]{1,0:T(8,128)S(1)} %reduce_sum.18.a), channel_id=1, source_target_pairs={{0,4},{1,5},{2,6},{3,7},{4,0},{5,1},{6,2},{7,3},{8,12},{9,13},{10,... | collective-permute-start | bytes 49160 | tf_op jit(solution)/shard_map/ppermute | solution.py:338
  93.4 17.7 %all_to_all.46 = f32[32,32,128]{2,1,0:T(8,128)S(1)} all-to-all(f32[32,32,128]{2,1,0:T(8,128)S(1)} %bitcast.12), channel_id=1, replica_groups={{0,8,16,24,32,40,48,56,64,72,80,88,96,104,112,120,128,136,144,152,160,1..., dimensions={0} | all-to-all | bytes 1048576 | tf_op jit(solution)/shard_map/all_to_all | solution.py:357
  111.0 4.0 %collective-permute-start.12 = (f32[1024,128]{1,0:T(8,128)S(1)}, f32[1024,128]{1,0:T(8,128)S(1)}, u32[]{:S(2)}, u32[]{:S(2)}) collective-permute-start(f32[1024,128]{1,0:T(8,128)S(1)} %bitcast.14), channel_id=1, source_target_pairs={{0,1},{1,0},{2,3},{3,2},{4,5},{5,4},{6,7},{7,6},{8,9},{9,8},{10,11... | collective-permute-start | bytes 1572872 | tf_op jit(solution)/shard_map/ppermute | solution.py:338
  117.4 8.4 %frame2.1 = (f32[1024,128]{1,0:T(8,128)}, f32[1024,128]{1,0:T(8,128)}, f32[136,256]{1,0:T(8,128)}, f32[136,256]{1,0:T(8,128)}, f32[2,256,384]{2,1,0:T(8,128)}, /...) custom-call(f32[2,64,384]{2,1,0:T(8,128)} %copy-done.6, f32[2,256,384]{2,1,0:T(8,128)} %copy-done, ...), custom_call_target="tpu_custom_call" | custom-call | tf_op jit(solution)/shard_map/frame2/pallas_call | solution.py:318
  132.0 4.5 %collective-permute-done.15.rd = f32[136,256]{1,0:T(8,128)S(1)} collective-permute-done((f32[136,256]{1,0:T(8,128)}, f32[136,256]{1,0:T(8,128)S(1)}, u32[]{:S(2)}, u32[]{:S(2)}) %collective-permute-start.15) | collective-permute-done | bytes 139296 | tf_op jit(solution)/shard_map/ppermute | solution.py:334
  137.4 3.4 %last_bands.1 = (f32[1024,128]{1,0:T(8,128)}, f32[2,256,384]{2,1,0:T(8,128)}, f32[256,128]{1,0:T(8,128)}, f32[256,128]{1,0:T(8,128)}) custom-call(f32[1024,128]{1,0:T(8,128)} %get-tuple-element.51.keep, f32[1024,128]{1,0:T(8,128)} %copy-done.10, f32[2,256,384]{2,1,0:T(8,128)} %get-tuple-element.53.own, f32[136,256]{1,0:T(8,128)} %copy-done.15, ...), custom_call_target="tpu_custom_call" | custom-call | tf_op jit(solution)/shard_map/last_bands/pallas_call | solution.py:318
  140.9 5.2 %all-to-all-start.2 = ((f32[32,32,128]{2,1,0:T(8,128)}), f32[32,32,128]{2,1,0:T(8,128)S(1)}, u32[]{:S(2)}, u32[]{:S(2)}) async-start(f32[32,32,128]{2,1,0:T(8,128)} %bitcast.17), calls=%async_computation.2 | async-start | bytes 1048576 | tf_op jit(solution)/shard_map/all_to_all | solution.py:352
  146.1 5.4 %collective-permute-start.16 = (f32[256,128]{1,0:T(8,128)}, f32[256,128]{1,0:T(8,128)S(1)}, u32[]{:S(2)}, u32[]{:S(2)}) collective-permute-start(f32[256,128]{1,0:T(8,128)} %get-tuple-element.59), channel_id=1, source_target_pairs={{0,1},{1,2},{2,3},{3,4},{4,5},{5,6},{6,7},{7,8},{8,9},{9,10},{10,1... | collective-permute-start | bytes 393224 | tf_op jit(solution)/shard_map/ppermute | solution.py:334
  153.8 5.9 %collective-permute-done.17.east = f32[256,128]{1,0:T(8,128)S(1)} collective-permute-done((f32[256,128]{1,0:T(8,128)}, f32[256,128]{1,0:T(8,128)S(1)}, u32[]{:S(2)}, u32[]{:S(2)}) %collective-permute-start.17) | collective-permute-done | bytes 131104 | tf_op jit(solution)/shard_map/ppermute | solution.py:334
  159.7 5.7 %collective-permute-start.20 = (f32[32,128]{1,0:T(8,128)S(1)}, f32[32,128]{1,0:T(8,128)S(1)}, u32[]{:S(2)}, u32[]{:S(2)}) collective-permute-start(f32[32,128]{1,0:T(8,128)S(1)} %reduce_sum.19.a), channel_id=1, source_target_pairs={{0,6},{1,7},{2,4},{3,5},{4,2},{5,3},{6,0},{7,1},{8,14},{9,15},{10,... | collective-permute-start | bytes 49160 | tf_op jit(solution)/shard_map/ppermute | solution.py:338
  167.6 4.4 %collective-permute-done.19.c = f32[32,128]{1,0:T(8,128)S(1)} collective-permute-done((f32[32,128]{1,0:T(8,128)S(1)}, f32[32,128]{1,0:T(8,128)S(1)}, u32[]{:S(2)}, u32[]{:S(2)}) %collective-permute-start.19) | collective-permute-done | bytes 16416 | tf_op jit(solution)/shard_map/ppermute | solution.py:338
  172.0 17.0 %all_to_all.47 = f32[32,32,128]{2,1,0:T(8,128)S(1)} all-to-all(f32[32,32,128]{2,1,0:T(8,128)S(1)} %bitcast.13), channel_id=1, replica_groups={{0,8,16,24,32,40,48,56,64,72,80,88,96,104,112,120,128,136,144,152,160,1..., dimensions={0} | all-to-all | bytes 1048576 | tf_op jit(solution)/shard_map/all_to_all | solution.py:357
  (71 shorter events, 38.3 us)
Async XLA Ops:
  1.8 8.2 %collective-permute-start = (f32[256,128]{1,0:T(8,128)S(1)}, f32[256,128]{1,0:T(8,128)S(1)}, u32[]{:S(2)}, u32[]{:S(2)}) collective-permute-start(f32[256,128]{1,0:T(8,128)S(1)} %get-tuple-element.33), channel_id=1, source_target_pairs={{0,1},{1,2},{2,3},{3,4},{4,5},{5,6},{6,7},{7,8},{8,9},{9,10},{10,1... | collective-permute-start | bytes 393224 | tf_op jit(solution)/shard_map/ppermute | solution.py:334
  8.1 7.2 %collective-permute-start.1 = (f32[256,128]{1,0:T(8,128)S(1)}, f32[256,128]{1,0:T(8,128)S(1)}, u32[]{:S(2)}, u32[]{:S(2)}) collective-permute-start(f32[256,128]{1,0:T(8,128)S(1)} %get-tuple-element.34), channel_id=1, source_target_pairs={{1,0},{2,1},{3,2},{4,3},{5,4},{6,5},{7,6},{8,7},{9,8},{10,9},{11,1... | collective-permute-start | bytes 393224 | tf_op jit(solution)/shard_map/ppermute | solution.py:334
  16.5 6.2 %collective-permute-start.2 = (f32[2,64,384]{2,1,0:T(8,128)S(1)}, f32[2,64,384]{2,1,0:T(8,128)S(1)}, u32[]{:S(2)}, u32[]{:S(2)}) collective-permute-start(f32[2,64,384]{2,1,0:T(8,128)S(1)} %get-tuple-element.35), channel_id=1, source_target_pairs={{0,32},{32,64},{64,96},{96,128},{128,160},{160,192},{192,224},{1,3... | collective-permute-start | bytes 589832 | tf_op jit(solution)/shard_map/ppermute | solution.py:334
  20.0 7.4 %collective-permute-start.3 = (f32[2,64,384]{2,1,0:T(8,128)S(1)}, f32[2,64,384]{2,1,0:T(8,128)S(1)}, u32[]{:S(2)}, u32[]{:S(2)}) collective-permute-start(f32[2,64,384]{2,1,0:T(8,128)S(1)} %get-tuple-element.37), channel_id=1, source_target_pairs={{32,0},{64,32},{96,64},{128,96},{160,128},{192,160},{224,192},{33,... | collective-permute-start | bytes 589832 | tf_op jit(solution)/shard_map/ppermute | solution.py:334
  35.6 16.6 %collective-permute-start.4 = (f32[1024,128]{1,0:T(8,128)}, f32[1024,128]{1,0:T(8,128)S(1)}, u32[]{:S(2)}, u32[]{:S(2)}) collective-permute-start(f32[1024,128]{1,0:T(8,128)} %get-tuple-element.39), channel_id=1, source_target_pairs={{0,1},{1,0},{2,3},{3,2},{4,5},{5,4},{6,7},{7,6},{8,9},{9,8},{10,11... | collective-permute-start | bytes 1572872 | tf_op jit(solution)/shard_map/ppermute | solution.py:338
  35.7 9.3 %collective-permute-start.5 = (f32[264,256]{1,0:T(8,128)}, f32[264,256]{1,0:T(8,128)S(1)}, u32[]{:S(2)}, u32[]{:S(2)}) collective-permute-start(f32[264,256]{1,0:T(8,128)} %get-tuple-element.41), channel_id=1, source_target_pairs={{0,32},{32,64},{64,96},{96,128},{128,160},{160,192},{192,224},{1,3... | collective-permute-start | bytes 811016 | tf_op jit(solution)/shard_map/ppermute | solution.py:334
  39.4 12.8 %collective-permute-start.6 = (f32[264,256]{1,0:T(8,128)}, f32[264,256]{1,0:T(8,128)S(1)}, u32[]{:S(2)}, u32[]{:S(2)}) collective-permute-start(f32[264,256]{1,0:T(8,128)} %get-tuple-element.42), channel_id=1, source_target_pairs={{32,0},{64,32},{96,64},{128,96},{160,128},{192,160},{224,192},{33,... | collective-permute-start | bytes 811016 | tf_op jit(solution)/shard_map/ppermute | solution.py:334
  56.3 22.9 %all-to-all-start = ((f32[32,32,128]{2,1,0:T(8,128)}), f32[32,32,128]{2,1,0:T(8,128)S(1)}, u32[]{:S(2)}, u32[]{:S(2)}) async-start(f32[32,32,128]{2,1,0:T(8,128)} %bitcast.16), calls=%async_computation | async-start | bytes 1048576 | tf_op jit(solution)/shard_map/all_to_all | solution.py:352
  66.8 11.4 %collective-permute-start.8 = (f32[2,384,128]{2,1,0:T(8,128)}, f32[2,384,128]{2,1,0:T(8,128)S(1)}, u32[]{:S(2)}, u32[]{:S(2)}) collective-permute-start(f32[2,384,128]{2,1,0:T(8,128)} %get-tuple-element.43.refs_4_), channel_id=1, source_target_pairs={{1,0},{2,1},{3,2},{4,3},{5,4},{6,5},{7,6},{8,7},{9,8},{10,9},{11,1... | collective-permute-start | bytes 1179656 | tf_op jit(solution)/shard_map/ppermute | solution.py:334
  69.8 9.4 %collective-permute-start.7 = (f32[2,384,128]{2,1,0:T(8,128)}, f32[2,384,128]{2,1,0:T(8,128)S(1)}, u32[]{:S(2)}, u32[]{:S(2)}) collective-permute-start(f32[2,384,128]{2,1,0:T(8,128)} %get-tuple-element.45.refs_6_), channel_id=1, source_target_pairs={{0,1},{1,2},{2,3},{3,4},{4,5},{5,6},{6,7},{7,8},{8,9},{9,10},{10,1... | collective-permute-start | bytes 1179656 | tf_op jit(solution)/shard_map/ppermute | solution.py:334
  79.2 10.5 %collective-permute-start.11 = (f32[32,128]{1,0:T(8,128)S(1)}, f32[32,128]{1,0:T(8,128)S(1)}, u32[]{:S(2)}, u32[]{:S(2)}) collective-permute-start(f32[32,128]{1,0:T(8,128)S(1)} %reduce_sum.18.a), channel_id=1, source_target_pairs={{0,6},{1,7},{2,4},{3,5},{4,2},{5,3},{6,0},{7,1},{8,14},{9,15},{10,... | collective-permute-start | bytes 49160 | tf_op jit(solution)/shard_map/ppermute | solution.py:338
  83.0 7.8 %collective-permute-start.10 = (f32[32,128]{1,0:T(8,128)S(1)}, f32[32,128]{1,0:T(8,128)S(1)}, u32[]{:S(2)}, u32[]{:S(2)}) collective-permute-start(f32[32,128]{1,0:T(8,128)S(1)} %reduce_sum.18.a), channel_id=1, source_target_pairs={{0,4},{1,5},{2,6},{3,7},{4,0},{5,1},{6,2},{7,3},{8,12},{9,13},{10,... | collective-permute-start | bytes 49160 | tf_op jit(solution)/shard_map/ppermute | solution.py:338
  89.7 3.6 %collective-permute-start.9 = (f32[32,128]{1,0:T(8,128)S(1)}, f32[32,128]{1,0:T(8,128)S(1)}, u32[]{:S(2)}, u32[]{:S(2)}) collective-permute-start(f32[32,128]{1,0:T(8,128)S(1)} %reduce_sum.18.a), channel_id=1, source_target_pairs={{0,2},{1,3},{2,0},{3,1},{4,6},{5,7},{6,4},{7,5},{8,10},{9,11},{10,... | collective-permute-start | bytes 49160 | tf_op jit(solution)/shard_map/ppermute | solution.py:338
  111.0 5.5 %collective-permute-start.12 = (f32[1024,128]{1,0:T(8,128)S(1)}, f32[1024,128]{1,0:T(8,128)S(1)}, u32[]{:S(2)}, u32[]{:S(2)}) collective-permute-start(f32[1024,128]{1,0:T(8,128)S(1)} %bitcast.14), channel_id=1, source_target_pairs={{0,1},{1,0},{2,3},{3,2},{4,5},{5,4},{6,7},{7,6},{8,9},{9,8},{10,11... | collective-permute-start | bytes 1572872 | tf_op jit(solution)/shard_map/ppermute | solution.py:338
  125.7 10.8 %collective-permute-start.13 = (f32[1024,128]{1,0:T(8,128)}, f32[1024,128]{1,0:T(8,128)S(1)}, u32[]{:S(2)}, u32[]{:S(2)}) collective-permute-start(f32[1024,128]{1,0:T(8,128)} %get-tuple-element.52), channel_id=1, source_target_pairs={{0,1},{1,0},{2,3},{3,2},{4,5},{5,4},{6,7},{7,6},{8,9},{9,8},{10,11... | collective-permute-start | bytes 1572872 | tf_op jit(solution)/shard_map/ppermute | solution.py:338
  126.2 5.8 %collective-permute-start.14 = (f32[136,256]{1,0:T(8,128)}, f32[136,256]{1,0:T(8,128)S(1)}, u32[]{:S(2)}, u32[]{:S(2)}) collective-permute-start(f32[136,256]{1,0:T(8,128)} %get-tuple-element.54), channel_id=1, source_target_pairs={{0,32},{32,64},{64,96},{96,128},{128,160},{160,192},{192,224},{1,3... | collective-permute-start | bytes 417800 | tf_op jit(solution)/shard_map/ppermute | solution.py:334
  128.8 7.8 %collective-permute-start.15 = (f32[136,256]{1,0:T(8,128)}, f32[136,256]{1,0:T(8,128)S(1)}, u32[]{:S(2)}, u32[]{:S(2)}) collective-permute-start(f32[136,256]{1,0:T(8,128)} %get-tuple-element.55), channel_id=1, source_target_pairs={{32,0},{64,32},{96,64},{128,96},{160,128},{192,160},{224,192},{33,... | collective-permute-start | bytes 417800 | tf_op jit(solution)/shard_map/ppermute | solution.py:334
  140.9 18.8 %all-to-all-start.2 = ((f32[32,32,128]{2,1,0:T(8,128)}), f32[32,32,128]{2,1,0:T(8,128)S(1)}, u32[]{:S(2)}, u32[]{:S(2)}) async-start(f32[32,32,128]{2,1,0:T(8,128)} %bitcast.17), calls=%async_computation.2 | async-start | bytes 1048576 | tf_op jit(solution)/shard_map/all_to_all | solution.py:352
  146.1 7.7 %collective-permute-start.16 = (f32[256,128]{1,0:T(8,128)}, f32[256,128]{1,0:T(8,128)S(1)}, u32[]{:S(2)}, u32[]{:S(2)}) collective-permute-start(f32[256,128]{1,0:T(8,128)} %get-tuple-element.59), channel_id=1, source_target_pairs={{0,1},{1,2},{2,3},{3,4},{4,5},{5,6},{6,7},{7,8},{8,9},{9,10},{10,1... | collective-permute-start | bytes 393224 | tf_op jit(solution)/shard_map/ppermute | solution.py:334
  151.6 8.1 %collective-permute-start.17 = (f32[256,128]{1,0:T(8,128)}, f32[256,128]{1,0:T(8,128)S(1)}, u32[]{:S(2)}, u32[]{:S(2)}) collective-permute-start(f32[256,128]{1,0:T(8,128)} %get-tuple-element.60), channel_id=1, source_target_pairs={{1,0},{2,1},{3,2},{4,3},{5,4},{6,5},{7,6},{8,7},{9,8},{10,9},{11,1... | collective-permute-start | bytes 393224 | tf_op jit(solution)/shard_map/ppermute | solution.py:334
  159.7 7.9 %collective-permute-start.20 = (f32[32,128]{1,0:T(8,128)S(1)}, f32[32,128]{1,0:T(8,128)S(1)}, u32[]{:S(2)}, u32[]{:S(2)}) collective-permute-start(f32[32,128]{1,0:T(8,128)S(1)} %reduce_sum.19.a), channel_id=1, source_target_pairs={{0,6},{1,7},{2,4},{3,5},{4,2},{5,3},{6,0},{7,1},{8,14},{9,15},{10,... | collective-permute-start | bytes 49160 | tf_op jit(solution)/shard_map/ppermute | solution.py:338
  165.4 6.5 %collective-permute-start.19 = (f32[32,128]{1,0:T(8,128)S(1)}, f32[32,128]{1,0:T(8,128)S(1)}, u32[]{:S(2)}, u32[]{:S(2)}) collective-permute-start(f32[32,128]{1,0:T(8,128)S(1)} %reduce_sum.19.a), channel_id=1, source_target_pairs={{0,4},{1,5},{2,6},{3,7},{4,0},{5,1},{6,2},{7,3},{8,12},{9,13},{10,... | collective-permute-start | bytes 49160 | tf_op jit(solution)/shard_map/ppermute | solution.py:338
  165.4 6.5 %collective-permute-start.18 = (f32[32,128]{1,0:T(8,128)S(1)}, f32[32,128]{1,0:T(8,128)S(1)}, u32[]{:S(2)}, u32[]{:S(2)}) collective-permute-start(f32[32,128]{1,0:T(8,128)S(1)} %reduce_sum.19.a), channel_id=1, source_target_pairs={{0,2},{1,3},{2,0},{3,1},{4,6},{5,7},{6,4},{7,5},{8,10},{9,11},{10,... | collective-permute-start | bytes 49160 | tf_op jit(solution)/shard_map/ppermute | solution.py:338
  189.0 1.9 collective-permute-start.21
  (17 other events, 243.9 us)

commit v4 on v2

--- a/solution.py
+++ b/solution.py
@@ -72,18 +72,29 @@
     return pltpu.roll(x, H, 1)
 
 
-def sides_kernel(obj, left, right):
+def core_index():
+    return lax.rem(lax.axis_index("col"), 2)
+
+
+def choose(x, y):
+    return jnp.where(core_index() == 0, x, y)
+
+
+def sides_kernel(obj, inner, outer):
     low = lanes()
-    left[...] = jnp.where(low, obj[0, :, :LANE], half_turn(obj[1, :, :LANE]))
-    right[...] = jnp.where(low, half_turn(obj[0, :, LANE:]), obj[1, :, LANE:])
-
-
-def rows_kernel(obj, west, east, mid, top, bottom):
+    left = jnp.where(low, obj[0, :, :LANE], half_turn(obj[1, :, :LANE]))
+    right = jnp.where(low, half_turn(obj[0, :, LANE:]), obj[1, :, LANE:])
+    inner[...] = choose(right, left)
+    outer[...] = choose(left, right)
+
+
+def rows_kernel(obj, inner, outer, mid, top, bottom):
     low = lanes()
+    west, east = choose(outer[...], inner[...]), choose(inner[...], outer[...])
     for c in range(2):
         x, y = half_turn(obj[c, :, :LANE]), half_turn(obj[c, :, LANE:])
-        w = west[...] if c == 0 else half_turn(west[...])
-        e = half_turn(east[...]) if c == 0 else east[...]
+        w = west if c == 0 else half_turn(west)
+        e = half_turn(east) if c == 0 else east
         for k, part in enumerate((jnp.where(low, w, x), jnp.where(low, x, y), jnp.where(low, y, e))):
             s = slice(k * LANE, (k + 1) * LANE)
             mid[c, :, s] = part
@@ -125,7 +136,7 @@
     else:
         *stores, su, sd, own, obj, probe_out = refs[:7]
         ext, canvas, raw, head, keep, send, outs, probe, *inner, sems = refs[7:]
-        up, mid, down, off, cl, cm, cr, dl, dr, probe_in, mine, other, amps, table = inner
+        up, mid, down, off, ci, cm, co, di, do, probe_in, mine, other, amps, table = inner
     wait = fetch(arrays, inner, sems)
     wait(*range(4 if first else 9))
     o0 = off[0, 0, 0, 0]
@@ -140,7 +151,8 @@
     for c in range(2):
         whole = jnp.concatenate([up[c], mid[c], down[c]], axis=0)
         if not first:
-            grad = jnp.concatenate([cl[c] + dl[c], cm[c], cr[c] + dr[c]], axis=1)
+            near, far = ci[c] + di[c], co[c] + do[c]
+            grad = jnp.concatenate([choose(far, near), cm[c], choose(near, far)], axis=1)
             i = lax.broadcasted_iota(jnp.int32, (SPAN, SPAN), 0) + (row * TILE - H)
             j = lax.broadcasted_iota(jnp.int32, (SPAN, SPAN), 1) + (col * TILE - H)
             inside = (i >= 0) & (i < lax.axis_size("row") * TILE) & (j >= 0) & (
@@ -248,23 +260,22 @@
     out[...] = total
 
 
-def bands_kernel(parts, own, ru, rd, total, cl, cm, cr, tl, tm, tr, outs, *inner):
+def bands_kernel(parts, own, ru, rd, total, ci, cm, co, ti, tm, to, outs, *inner):
     *inner, sems = inner
     wait = fetch((own, ru, rd), inner, sems)
     own, ru, rd = inner
     chunk_sum(parts, total)
     wait(*range(3))
     for c in range(2):
-        above, below = arrived(ru, c), arrived(rd, c)
-        for k, out in enumerate((tl, tm, tr)):
-            s = slice(k * B, (k + 1) * B)
-            out[c, :B] = own[c, :B, s] + above[:, s]
-            out[c, B:2 * B] = own[c, B:2 * B, s]
-            out[c, 2 * B:] = own[c, 2 * B:, s] + below[:, s]
-    finish(store(zip((tl, tm, tr), (cl, cm, cr)), outs))
-
-
-def last_bands_kernel(parts, own, ru, rd, total, grad_out, left, right, grad, outs, *inner):
+        rows = jnp.concatenate(
+            [own[c, :B] + arrived(ru, c), own[c, B:2 * B], own[c, 2 * B:] + arrived(rd, c)], axis=0)
+        left, tm[c], right = rows[:, :B], rows[:, B:2 * B], rows[:, 2 * B:]
+        ti[c] = choose(right, left)
+        to[c] = choose(left, right)
+    finish(store(zip((ti, to, tm), (ci, co, cm)), outs))
+
+
+def last_bands_kernel(parts, own, ru, rd, total, grad_out, near, far, grad, outs, *inner):
     *inner, sems = inner
     wait = fetch((own, ru, rd), inner, sems)
     own, ru, rd = inner
@@ -276,8 +287,10 @@
         grad[c, H:TILE - H] = own[c, H:TILE - H]
         grad[c, TILE - H:] = own[c, TILE - H:] + arrived(rd, c)
     copies = store(((grad, grad_out),), outs)
-    left[...] = jnp.where(low, grad[0, :, :LANE], half_turn(grad[1, :, :LANE]))
-    right[...] = jnp.where(low, half_turn(grad[0, :, 2 * LANE:]), grad[1, :, 2 * LANE:])
+    left = jnp.where(low, grad[0, :, :LANE], half_turn(grad[1, :, :LANE]))
+    right = jnp.where(low, half_turn(grad[0, :, 2 * LANE:]), grad[1, :, 2 * LANE:])
+    near[...] = choose(right, left)
+    far[...] = choose(left, right)
     finish(copies)
 
 
@@ -288,15 +301,16 @@
         out[k * rows:(k + 1) * rows, :] = total
 
 
-def last_kernel(obj, grad, probe, west, east, mine, other, out, out_probe, *inner):
+def last_kernel(obj, grad, probe, near, far, mine, other, out, out_probe, *inner):
     *inner, sems = inner
     wait = fetch((obj, grad, probe), inner, sems)
     obj, grad, probe = inner
     low = lanes()
+    west, east = choose(far[...], near[...]), choose(near[...], far[...])
     wait(*range(3))
     for c in range(2):
-        w = half_turn(west[...]) if c == 0 else west[...]
-        e = east[...] if c == 0 else half_turn(east[...])
+        w = half_turn(west) if c == 0 else west
+        e = east if c == 0 else half_turn(east)
         x = obj[c, :, :LANE] - object_step * (grad[c, :, :LANE] + w)
         y = obj[c, :, LANE:2 * LANE] - object_step * grad[c, :, LANE:2 * LANE]
         z = obj[c, :, 2 * LANE:] - object_step * (grad[c, :, 2 * LANE:] + e)
@@ -342,6 +356,13 @@
     return lax.ppermute(x, RC, [(i, i ^ mask) for i in range(256)])
 
 
+def columns(near, far):
+    count = lax.axis_size("col")
+    pairs = [(i, i + 1) for i in range(1, count - 1, 2)]
+    pairs += [(j, i) for i, j in pairs]
+    return exchange(near, BIT_CORE), lax.ppermute(far, "col", pairs)
+
+
 def groups(mask):
     members = [i for i in range(256) if i & ~mask == 0]
     return [[base | i for i in members] for base in range(256) if base & mask == 0]
@@ -367,12 +388,10 @@
 
 def local(object_field, probe, amplitudes, offsets):
     table = tables()
-    left, right = call(sides_kernel, [(TILE, LANE)] * 2, "sides")(object_field)
-    west = shift(right, "col", 1)
-    east = shift(left, "col", -1)
+    sides = call(sides_kernel, [(TILE, LANE)] * 2, "sides")(object_field)
     mid, top, bottom = call(
         rows_kernel, [(2, TILE, SPAN)] + [(2, H, SPAN)] * 2, "rows"
-    )(object_field, west, east)
+    )(object_field, *columns(*sides))
     up = shift(bottom, "row", 1)
     down = shift(top, "row", -1)
 
@@ -390,7 +409,7 @@
     )(up, mid, down, offsets, probe, amplitudes, table)
     ru = shift(sd, "row", 1)
     rd = shift(su, "row", -1)
-    total, cl, cm, cr = call(
+    total, ci, cm, co = call(
         bands_kernel,
         [(CHUNK, LANE)] + [(2, SPAN, B)] * 3,
         "bands",
@@ -398,9 +417,7 @@
         places=[VM] + [HBM] * 3,
         scratch=[pltpu.VMEM((2, SPAN, B), f32)] * 3 + [pltpu.SemaphoreType.DMA((3,))],
     )(scatter(keep, send), own, ru, rd)
-    dl = shift(cr, "col", 1)
-    dr = shift(cl, "col", -1)
-    mine, other, dl, dr = gather(total, dl, dr)
+    mine, other, di, do = gather(total, *columns(ci, co))
 
     keep, send, su, sd, own, obj, probe = call(
         functools.partial(frame_kernel, False),
@@ -410,10 +427,10 @@
         [HBM] * 14,
         [HBM] * 7,
         held + [pltpu.SemaphoreType.DMA((13,)), pltpu.VMEM((2, M, F, F), f32)],
-    )(up, mid, down, offsets, cl, cm, cr, dl, dr, probe, mine, other, amplitudes, table)
+    )(up, mid, down, offsets, ci, cm, co, di, do, probe, mine, other, amplitudes, table)
     ru = shift(sd, "row", 1)
     rd = shift(su, "row", -1)
-    total, grad, left, right = call(
+    total, grad, near, far = call(
         last_bands_kernel,
         [(CHUNK, LANE), (2, TILE, SPAN)] + [(TILE, LANE)] * 2,
         "last_bands",
@@ -421,16 +438,14 @@
         places=[VM, HBM, VM, VM],
         scratch=[pltpu.VMEM((2, TILE, SPAN), f32), pltpu.SemaphoreType.DMA((1,))],
     )(scatter(keep, send), own, ru, rd)
-    west = shift(right, "col", 1)
-    east = shift(left, "col", -1)
-    mine, other, west, east = gather(total, west, east)
+    mine, other, near, far = gather(total, *columns(near, far))
     return tuple(
         call(
             last_kernel,
             [(2, TILE, TILE), (2, M, F, F)],
             "last",
             specs=[HBM] * 3 + [VM] * 4,
-        )(obj, grad, probe, west, east, mine, other)
+        )(obj, grad, probe, near, far, mine, other)
     )
 
 

time: 187 us -> 179 us (0.957)
  starting transfers between devices: 70.3 us -> 64.4 us
  waiting for transfers between devices: 54.2 us -> 49.3 us
  blocking collectives: 32.8 us -> 35.5 us
    ppermute x12 -> x6, starting transfers between devices: 34.8 us -> 11.5 us  [shift(): return lax.ppermute(x, axis, pairs)]
    ppermute x0 -> x3, starting transfers between devices: none -> 10.3 us  [columns(): return (exchange(near, BIT_CORE), lax.ppermute(far, 'col', pairs))]
    ppermute x12 -> x6, waiting for transfers between devices: 34.4 us -> 28.1 us  [shift(): return lax.ppermute(x, axis, pairs)]
    ppermute x0 -> x3, waiting for transfers between devices: none -> 5.76 us  [columns(): return (exchange(near, BIT_CORE), lax.ppermute(far, 'col', pairs))]
    ppermute x10 -> x13, starting transfers between devices: 19.9 us -> 25 us  [exchange(): return lax.ppermute(x, RC, [(i, i ^ mask) for i in range(256)])]
    ppermute x10 -> x13, waiting for transfers between devices: 19.8 us -> 15.5 us  [exchange(): return lax.ppermute(x, RC, [(i, i ^ mask) for i in range(256)])]
    all_to_all x2, blocking collectives: 32.8 us -> 35.5 us  [gather(): x = lax.all_to_all(x, RC, 0, 0, axis_index_groups=groups(WIDE), tiled=True)]
    all_to_all x2, starting transfers between devices: 15.6 us -> 17.7 us  [scatter(): lax.all_to_all(x, RC, 0, 0, axis_index_groups=groups(WIDE), tiled=True)]
  transfers between devices with their start and end apart: 24 -> 24, of which waited for: 13 -> 16; matrix products, arithmetic and copies ran while one was open for 0% -> 0% of each run, Pallas kernels for 0% -> 0%
where the time goes in v4:
time: 179 us; the launch traced here: 178 us
  starting transfers between devices  64.4 us (36%)
  waiting for transfers between devices  49.3 us (28%)
  blocking collectives  35.5 us (20%)
  Pallas kernels  20.6 us (12%)
  other arithmetic  4.04 us (2%)
  local copies, waits for them, and re-layouts  3.41 us (2%)
    all_to_all x2, blocking collectives, gather(): x = lax.all_to_all(x, RC, 0, 0, axis_index_groups=groups(WIDE), tiled=True)  35.5 us
    ppermute x6, waiting for transfers between devices, shift(): return lax.ppermute(x, axis, pairs)  28.1 us
    ppermute x13, starting transfers between devices, exchange(): return lax.ppermute(x, RC, [(i, i ^ mask) for i in range(256)])  25 us
    pallas_call x9, Pallas kernels, run(): pl.pallas_call(kernel, out_shape=[jax.ShapeDtypeStruct(s, f32) for s in o...  20.6 us
    all_to_all x2, starting transfers between devices, scatter(): lax.all_to_all(x, RC, 0, 0, axis_index_groups=groups(WIDE), tiled=True)  17.7 us
    ppermute x13, waiting for transfers between devices, exchange(): return lax.ppermute(x, RC, [(i, i ^ mask) for i in range(256)])  15.5 us
    ppermute x6, starting transfers between devices, shift(): return lax.ppermute(x, axis, pairs)  11.5 us
    ppermute x3, starting transfers between devices, columns(): return (exchange(near, BIT_CORE), lax.ppermute(far, 'col', pairs))  10.3 us
  transfers between devices with their start and end apart: 24, of which 16 were waited for; matrix products, arithmetic and copies ran while one was open for 0% of the time, Pallas kernels for 0%

profile of v4, /device:TPU:1, one launch (start us, length us, event | category | flops | bytes accessed | tf_op | source)
XLA Modules:
  0.0 178.3 jit_solution(18133218507740550376)
XLA Ops:
  1.8 3.3 %collective-permute-start = (f32[256,128]{1,0:T(8,128)S(1)}, f32[256,128]{1,0:T(8,128)S(1)}, u32[]{:S(2)}, u32[]{:S(2)}) collective-permute-start(f32[256,128]{1,0:T(8,128)S(1)} %get-tuple-element.39), channel_id=1, source_target_pairs={{0,1},{1,0},{2,3},{3,2},{4,5},{5,4},{6,7},{7,6},{8,9},{9,8},{10,11... | collective-permute-start | bytes 393224 | tf_op jit(solution)/shard_map/ppermute | solution.py:356
  5.1 3.1 %collective-permute-start.1 = (f32[256,128]{1,0:T(8,128)S(1)}, f32[256,128]{1,0:T(8,128)S(1)}, u32[]{:S(2)}, u32[]{:S(2)}) collective-permute-start(f32[256,128]{1,0:T(8,128)S(1)} %get-tuple-element.40), channel_id=1, source_target_pairs={{1,2},{3,4},{5,6},{7,8},{9,10},{11,12},{13,14},{15,16},{17,18},{19... | collective-permute-start | bytes 393224 | tf_op jit(solution)/shard_map/ppermute | solution.py:363
  8.2 5.5 %collective-permute-done.1.outer = f32[256,128]{1,0:T(8,128)S(1)} collective-permute-done((f32[256,128]{1,0:T(8,128)S(1)}, f32[256,128]{1,0:T(8,128)S(1)}, u32[]{:S(2)}, u32[]{:S(2)}) %collective-permute-start.1) | collective-permute-done | bytes 131104 | tf_op jit(solution)/shard_map/ppermute | solution.py:363
  18.7 3.8 %collective-permute-done.3.refs_2_ = f32[2,64,384]{2,1,0:T(8,128)S(1)} collective-permute-done((f32[2,64,384]{2,1,0:T(8,128)S(1)}, f32[2,64,384]{2,1,0:T(8,128)S(1)}, u32[]{:S(2)}, u32[]{:S(2)}) %collective-permute-start.3) | collective-permute-done | bytes 196640 | tf_op jit(solution)/shard_map/ppermute | solution.py:352
  23.2 7.5 %frame1.1 = (f32[1024,128]{1,0:T(8,128)}, f32[1024,128]{1,0:T(8,128)}, f32[264,256]{1,0:T(8,128)}, f32[264,256]{1,0:T(8,128)}, f32[2,384,384]{2,1,0:T(8,128)}) custom-call(f32[2,64,384]{2,1,0:T(8,128)} %copy-done.10, f32[2,256,384]{2,1,0:T(8,128)} %copy-done, f32[2,64,384]{2,1,0:T(8,128)} %copy-done.11, s32[1,1,1,2]{3,2,1,0:T(1,128)} %refs_3_.3, ...), custom_call_target="tpu_custom_call" | custom-call | tf_op jit(solution)/shard_map/frame1/pallas_call | solution.py:336
  35.0 13.4 %all-to-all-start = ((f32[32,32,128]{2,1,0:T(8,128)}), f32[32,32,128]{2,1,0:T(8,128)S(1)}, u32[]{:S(2)}, u32[]{:S(2)}) async-start(f32[32,32,128]{2,1,0:T(8,128)} %bitcast), calls=%async_computation | async-start | bytes 1048576 | tf_op jit(solution)/shard_map/all_to_all | solution.py:378
  48.5 3.2 %collective-permute-start.5 = (f32[264,256]{1,0:T(8,128)S(1)}, f32[264,256]{1,0:T(8,128)S(1)}, u32[]{:S(2)}, u32[]{:S(2)}) collective-permute-start(f32[264,256]{1,0:T(8,128)S(1)} %copy-done.16), channel_id=1, source_target_pairs={{0,32},{32,64},{64,96},{96,128},{128,160},{160,192},{192,224},{1,3... | collective-permute-start | bytes 811016 | tf_op jit(solution)/shard_map/ppermute | solution.py:352
  52.9 6.6 %collective-permute-done.5.ru = f32[264,256]{1,0:T(8,128)S(1)} collective-permute-done((f32[264,256]{1,0:T(8,128)S(1)}, f32[264,256]{1,0:T(8,128)S(1)}, u32[]{:S(2)}, u32[]{:S(2)}) %collective-permute-start.5) | collective-permute-done | bytes 270368 | tf_op jit(solution)/shard_map/ppermute | solution.py:352
  59.5 7.8 %collective-permute-done.6.rd = f32[264,256]{1,0:T(8,128)S(1)} collective-permute-done((f32[264,256]{1,0:T(8,128)S(1)}, f32[264,256]{1,0:T(8,128)S(1)}, u32[]{:S(2)}, u32[]{:S(2)}) %collective-permute-start.6) | collective-permute-done | bytes 270368 | tf_op jit(solution)/shard_map/ppermute | solution.py:352
  70.4 3.9 %collective-permute-start.11 = (f32[2,384,128]{2,1,0:T(8,128)S(1)}, f32[2,384,128]{2,1,0:T(8,128)S(1)}, u32[]{:S(2)}, u32[]{:S(2)}) collective-permute-start(f32[2,384,128]{2,1,0:T(8,128)S(1)} %get-tuple-element.51.refs_6_), channel_id=1, source_target_pairs={{1,2},{3,4},{5,6},{7,8},{9,10},{11,12},{13,14},{15,16},{17,18},{19... | collective-permute-start | bytes 1179656 | tf_op jit(solution)/shard_map/ppermute | solution.py:363
  74.3 2.7 %collective-permute-start.9 = (f32[32,128]{1,0:T(8,128)S(1)}, f32[32,128]{1,0:T(8,128)S(1)}, u32[]{:S(2)}, u32[]{:S(2)}) collective-permute-start(f32[32,128]{1,0:T(8,128)S(1)} %get-tuple-element.55.a), channel_id=1, source_target_pairs={{0,6},{1,7},{2,4},{3,5},{4,2},{5,3},{6,0},{7,1},{8,14},{9,15},{10,... | collective-permute-start | bytes 49160 | tf_op jit(solution)/shard_map/ppermute | solution.py:356
  77.0 3.9 %collective-permute-start.8 = (f32[32,128]{1,0:T(8,128)S(1)}, f32[32,128]{1,0:T(8,128)S(1)}, u32[]{:S(2)}, u32[]{:S(2)}) collective-permute-start(f32[32,128]{1,0:T(8,128)S(1)} %get-tuple-element.55.a), channel_id=1, source_target_pairs={{0,4},{1,5},{2,6},{3,7},{4,0},{5,1},{6,2},{7,3},{8,12},{9,13},{10,... | collective-permute-start | bytes 49160 | tf_op jit(solution)/shard_map/ppermute | solution.py:356
  86.0 18.8 %all_to_all.44 = f32[32,32,128]{2,1,0:T(8,128)S(1)} all-to-all(f32[32,32,128]{2,1,0:T(8,128)S(1)} %bitcast.12), channel_id=1, replica_groups={{0,8,16,24,32,40,48,56,64,72,80,88,96,104,112,120,128,136,144,152,160,1..., dimensions={0} | all-to-all | bytes 1048576 | tf_op jit(solution)/shard_map/all_to_all | solution.py:385
  109.4 8.4 %frame2.1 = (f32[1024,128]{1,0:T(8,128)}, f32[1024,128]{1,0:T(8,128)}, f32[136,256]{1,0:T(8,128)}, f32[136,256]{1,0:T(8,128)}, f32[2,256,384]{2,1,0:T(8,128)}, /...) custom-call(f32[2,64,384]{2,1,0:T(8,128)} %copy-done.10, f32[2,256,384]{2,1,0:T(8,128)} %copy-done, ...), custom_call_target="tpu_custom_call" | custom-call | tf_op jit(solution)/shard_map/frame2/pallas_call | solution.py:336
  122.0 4.3 %all-to-all-start.2 = ((f32[32,32,128]{2,1,0:T(8,128)}), f32[32,32,128]{2,1,0:T(8,128)S(1)}, u32[]{:S(2)}, u32[]{:S(2)}) async-start(f32[32,32,128]{2,1,0:T(8,128)} %bitcast.4), calls=%async_computation.2 | async-start | bytes 1048576 | tf_op jit(solution)/shard_map/all_to_all | solution.py:378
  126.3 3.1 %collective-permute-start.14 = (f32[136,256]{1,0:T(8,128)S(1)}, f32[136,256]{1,0:T(8,128)S(1)}, u32[]{:S(2)}, u32[]{:S(2)}) collective-permute-start(f32[136,256]{1,0:T(8,128)S(1)} %copy-done.18), channel_id=1, source_target_pairs={{0,32},{32,64},{64,96},{96,128},{128,160},{160,192},{192,224},{1,3... | collective-permute-start | bytes 417800 | tf_op jit(solution)/shard_map/ppermute | solution.py:352
  130.8 3.8 %collective-permute-done.14.ru = f32[136,256]{1,0:T(8,128)S(1)} collective-permute-done((f32[136,256]{1,0:T(8,128)S(1)}, f32[136,256]{1,0:T(8,128)S(1)}, u32[]{:S(2)}, u32[]{:S(2)}) %collective-permute-start.14) | collective-permute-done | bytes 139296 | tf_op jit(solution)/shard_map/ppermute | solution.py:352
  134.6 4.8 %collective-permute-done.15.rd = f32[136,256]{1,0:T(8,128)S(1)} collective-permute-done((f32[136,256]{1,0:T(8,128)S(1)}, f32[136,256]{1,0:T(8,128)S(1)}, u32[]{:S(2)}, u32[]{:S(2)}) %collective-permute-start.15) | collective-permute-done | bytes 139296 | tf_op jit(solution)/shard_map/ppermute | solution.py:352
  142.0 3.3 %collective-permute-start.20 = (f32[256,128]{1,0:T(8,128)S(1)}, f32[256,128]{1,0:T(8,128)S(1)}, u32[]{:S(2)}, u32[]{:S(2)}) collective-permute-start(f32[256,128]{1,0:T(8,128)S(1)} %get-tuple-element.69), channel_id=1, source_target_pairs={{1,2},{3,4},{5,6},{7,8},{9,10},{11,12},{13,14},{15,16},{17,18},{19... | collective-permute-start | bytes 393224 | tf_op jit(solution)/shard_map/ppermute | solution.py:363
  145.3 3.2 %collective-permute-start.18 = (f32[32,128]{1,0:T(8,128)S(1)}, f32[32,128]{1,0:T(8,128)S(1)}, u32[]{:S(2)}, u32[]{:S(2)}) collective-permute-start(f32[32,128]{1,0:T(8,128)S(1)} %get-tuple-element.72.a), channel_id=1, source_target_pairs={{0,6},{1,7},{2,4},{3,5},{4,2},{5,3},{6,0},{7,1},{8,14},{9,15},{10,... | collective-permute-start | bytes 49160 | tf_op jit(solution)/shard_map/ppermute | solution.py:356
  148.5 2.8 %collective-permute-start.17 = (f32[32,128]{1,0:T(8,128)S(1)}, f32[32,128]{1,0:T(8,128)S(1)}, u32[]{:S(2)}, u32[]{:S(2)}) collective-permute-start(f32[32,128]{1,0:T(8,128)S(1)} %get-tuple-element.72.a), channel_id=1, source_target_pairs={{0,4},{1,5},{2,6},{3,7},{4,0},{5,1},{6,2},{7,3},{8,12},{9,13},{10,... | collective-permute-start | bytes 49160 | tf_op jit(solution)/shard_map/ppermute | solution.py:356
  151.3 3.7 %collective-permute-done.17.c = f32[32,128]{1,0:T(8,128)S(1)} collective-permute-done((f32[32,128]{1,0:T(8,128)S(1)}, f32[32,128]{1,0:T(8,128)S(1)}, u32[]{:S(2)}, u32[]{:S(2)}) %collective-permute-start.17) | collective-permute-done | bytes 16416 | tf_op jit(solution)/shard_map/ppermute | solution.py:356
  155.2 16.7 %all_to_all.45 = f32[32,32,128]{2,1,0:T(8,128)S(1)} all-to-all(f32[32,32,128]{2,1,0:T(8,128)S(1)} %bitcast.13), channel_id=1, replica_groups={{0,8,16,24,32,40,48,56,64,72,80,88,96,104,112,120,128,136,144,152,160,1..., dimensions={0} | all-to-all | bytes 1048576 | tf_op jit(solution)/shard_map/all_to_all | solution.py:385
  171.8 3.0 %collective-permute-start.21 = (f32[1024,128]{1,0:T(8,128)S(1)}, f32[1024,128]{1,0:T(8,128)S(1)}, u32[]{:S(2)}, u32[]{:S(2)}) collective-permute-start(f32[1024,128]{1,0:T(8,128)S(1)} %bitcast.10), channel_id=1, source_target_pairs={{0,1},{1,0},{2,3},{3,2},{4,5},{5,4},{6,7},{7,6},{8,9},{9,8},{10,11... | collective-permute-start | bytes 1572872 | tf_op jit(solution)/shard_map/ppermute | solution.py:356
  (75 shorter events, 36.6 us)
Async XLA Ops:
  1.8 6.4 %collective-permute-start = (f32[256,128]{1,0:T(8,128)S(1)}, f32[256,128]{1,0:T(8,128)S(1)}, u32[]{:S(2)}, u32[]{:S(2)}) collective-permute-start(f32[256,128]{1,0:T(8,128)S(1)} %get-tuple-element.39), channel_id=1, source_target_pairs={{0,1},{1,0},{2,3},{3,2},{4,5},{5,4},{6,7},{7,6},{8,9},{9,8},{10,11... | collective-permute-start | bytes 393224 | tf_op jit(solution)/shard_map/ppermute | solution.py:356
  5.1 8.6 %collective-permute-start.1 = (f32[256,128]{1,0:T(8,128)S(1)}, f32[256,128]{1,0:T(8,128)S(1)}, u32[]{:S(2)}, u32[]{:S(2)}) collective-permute-start(f32[256,128]{1,0:T(8,128)S(1)} %get-tuple-element.40), channel_id=1, source_target_pairs={{1,2},{3,4},{5,6},{7,8},{9,10},{11,12},{13,14},{15,16},{17,18},{19... | collective-permute-start | bytes 393224 | tf_op jit(solution)/shard_map/ppermute | solution.py:363
  14.9 3.9 %collective-permute-start.2 = (f32[2,64,384]{2,1,0:T(8,128)S(1)}, f32[2,64,384]{2,1,0:T(8,128)S(1)}, u32[]{:S(2)}, u32[]{:S(2)}) collective-permute-start(f32[2,64,384]{2,1,0:T(8,128)S(1)} %get-tuple-element.41), channel_id=1, source_target_pairs={{0,32},{32,64},{64,96},{96,128},{128,160},{160,192},{192,224},{1,3... | collective-permute-start | bytes 589832 | tf_op jit(solution)/shard_map/ppermute | solution.py:352
  16.2 6.4 %collective-permute-start.3 = (f32[2,64,384]{2,1,0:T(8,128)S(1)}, f32[2,64,384]{2,1,0:T(8,128)S(1)}, u32[]{:S(2)}, u32[]{:S(2)}) collective-permute-start(f32[2,64,384]{2,1,0:T(8,128)S(1)} %get-tuple-element.43), channel_id=1, source_target_pairs={{32,0},{64,32},{96,64},{128,96},{160,128},{192,160},{224,192},{33,... | collective-permute-start | bytes 589832 | tf_op jit(solution)/shard_map/ppermute | solution.py:352
  30.8 2.2 %collective-permute-start.4 = (f32[1024,128]{1,0:T(8,128)}, f32[1024,128]{1,0:T(8,128)S(1)}, u32[]{:S(2)}, u32[]{:S(2)}) collective-permute-start(f32[1024,128]{1,0:T(8,128)} %get-tuple-element.45), channel_id=1, source_target_pairs={{0,1},{1,0},{2,3},{3,2},{4,5},{5,4},{6,7},{7,6},{8,9},{9,8},{10,11... | collective-permute-start | bytes 1572872 | tf_op jit(solution)/shard_map/ppermute | solution.py:356
  35.0 32.3 %all-to-all-start = ((f32[32,32,128]{2,1,0:T(8,128)}), f32[32,32,128]{2,1,0:T(8,128)S(1)}, u32[]{:S(2)}, u32[]{:S(2)}) async-start(f32[32,32,128]{2,1,0:T(8,128)} %bitcast), calls=%async_computation | async-start | bytes 1048576 | tf_op jit(solution)/shard_map/all_to_all | solution.py:378
  48.5 11.1 %collective-permute-start.5 = (f32[264,256]{1,0:T(8,128)S(1)}, f32[264,256]{1,0:T(8,128)S(1)}, u32[]{:S(2)}, u32[]{:S(2)}) collective-permute-start(f32[264,256]{1,0:T(8,128)S(1)} %copy-done.16), channel_id=1, source_target_pairs={{0,32},{32,64},{64,96},{96,128},{128,160},{160,192},{192,224},{1,3... | collective-permute-start | bytes 811016 | tf_op jit(solution)/shard_map/ppermute | solution.py:352
  51.6 15.7 %collective-permute-start.6 = (f32[264,256]{1,0:T(8,128)S(1)}, f32[264,256]{1,0:T(8,128)S(1)}, u32[]{:S(2)}, u32[]{:S(2)}) collective-permute-start(f32[264,256]{1,0:T(8,128)S(1)} %copy-done.15), channel_id=1, source_target_pairs={{32,0},{64,32},{96,64},{128,96},{160,128},{192,160},{224,192},{33,... | collective-permute-start | bytes 811016 | tf_op jit(solution)/shard_map/ppermute | solution.py:352
  68.8 16.9 %collective-permute-start.10 = (f32[2,384,128]{2,1,0:T(8,128)S(1)}, f32[2,384,128]{2,1,0:T(8,128)S(1)}, u32[]{:S(2)}, u32[]{:S(2)}) collective-permute-start(f32[2,384,128]{2,1,0:T(8,128)S(1)} %get-tuple-element.49.refs_4_), channel_id=1, source_target_pairs={{0,1},{1,0},{2,3},{3,2},{4,5},{5,4},{6,7},{7,6},{8,9},{9,8},{10,11... | collective-permute-start | bytes 1179656 | tf_op jit(solution)/shard_map/ppermute | solution.py:356
  70.4 15.5 %collective-permute-start.11 = (f32[2,384,128]{2,1,0:T(8,128)S(1)}, f32[2,384,128]{2,1,0:T(8,128)S(1)}, u32[]{:S(2)}, u32[]{:S(2)}) collective-permute-start(f32[2,384,128]{2,1,0:T(8,128)S(1)} %get-tuple-element.51.refs_6_), channel_id=1, source_target_pairs={{1,2},{3,4},{5,6},{7,8},{9,10},{11,12},{13,14},{15,16},{17,18},{19... | collective-permute-start | bytes 1179656 | tf_op jit(solution)/shard_map/ppermute | solution.py:363
  74.3 9.0 %collective-permute-start.9 = (f32[32,128]{1,0:T(8,128)S(1)}, f32[32,128]{1,0:T(8,128)S(1)}, u32[]{:S(2)}, u32[]{:S(2)}) collective-permute-start(f32[32,128]{1,0:T(8,128)S(1)} %get-tuple-element.55.a), channel_id=1, source_target_pairs={{0,6},{1,7},{2,4},{3,5},{4,2},{5,3},{6,0},{7,1},{8,14},{9,15},{10,... | collective-permute-start | bytes 49160 | tf_op jit(solution)/shard_map/ppermute | solution.py:356
  77.0 8.7 %collective-permute-start.8 = (f32[32,128]{1,0:T(8,128)S(1)}, f32[32,128]{1,0:T(8,128)S(1)}, u32[]{:S(2)}, u32[]{:S(2)}) collective-permute-start(f32[32,128]{1,0:T(8,128)S(1)} %get-tuple-element.55.a), channel_id=1, source_target_pairs={{0,4},{1,5},{2,6},{3,7},{4,0},{5,1},{6,2},{7,3},{8,12},{9,13},{10,... | collective-permute-start | bytes 49160 | tf_op jit(solution)/shard_map/ppermute | solution.py:356
  80.9 4.7 %collective-permute-start.7 = (f32[32,128]{1,0:T(8,128)S(1)}, f32[32,128]{1,0:T(8,128)S(1)}, u32[]{:S(2)}, u32[]{:S(2)}) collective-permute-start(f32[32,128]{1,0:T(8,128)S(1)} %get-tuple-element.55.a), channel_id=1, source_target_pairs={{0,2},{1,3},{2,0},{3,1},{4,6},{5,7},{6,4},{7,5},{8,10},{9,11},{10,... | collective-permute-start | bytes 49160 | tf_op jit(solution)/shard_map/ppermute | solution.py:356
  104.8 3.8 %collective-permute-start.12 = (f32[1024,128]{1,0:T(8,128)S(1)}, f32[1024,128]{1,0:T(8,128)S(1)}, u32[]{:S(2)}, u32[]{:S(2)}) collective-permute-start(f32[1024,128]{1,0:T(8,128)S(1)} %bitcast.14), channel_id=1, source_target_pairs={{0,1},{1,0},{2,3},{3,2},{4,5},{5,4},{6,7},{7,6},{8,9},{9,8},{10,11... | collective-permute-start | bytes 1572872 | tf_op jit(solution)/shard_map/ppermute | solution.py:356
  117.8 2.2 %collective-permute-start.13 = (f32[1024,128]{1,0:T(8,128)}, f32[1024,128]{1,0:T(8,128)S(1)}, u32[]{:S(2)}, u32[]{:S(2)}) collective-permute-start(f32[1024,128]{1,0:T(8,128)} %get-tuple-element.61), channel_id=1, source_target_pairs={{0,1},{1,0},{2,3},{3,2},{4,5},{5,4},{6,7},{7,6},{8,9},{9,8},{10,11... | collective-permute-start | bytes 1572872 | tf_op jit(solution)/shard_map/ppermute | solution.py:356
  122.0 17.3 %all-to-all-start.2 = ((f32[32,32,128]{2,1,0:T(8,128)}), f32[32,32,128]{2,1,0:T(8,128)S(1)}, u32[]{:S(2)}, u32[]{:S(2)}) async-start(f32[32,32,128]{2,1,0:T(8,128)} %bitcast.4), calls=%async_computation.2 | async-start | bytes 1048576 | tf_op jit(solution)/shard_map/all_to_all | solution.py:378
  126.3 8.3 %collective-permute-start.14 = (f32[136,256]{1,0:T(8,128)S(1)}, f32[136,256]{1,0:T(8,128)S(1)}, u32[]{:S(2)}, u32[]{:S(2)}) collective-permute-start(f32[136,256]{1,0:T(8,128)S(1)} %copy-done.18), channel_id=1, source_target_pairs={{0,32},{32,64},{64,96},{96,128},{128,160},{160,192},{192,224},{1,3... | collective-permute-start | bytes 417800 | tf_op jit(solution)/shard_map/ppermute | solution.py:352
  129.5 9.9 %collective-permute-start.15 = (f32[136,256]{1,0:T(8,128)S(1)}, f32[136,256]{1,0:T(8,128)S(1)}, u32[]{:S(2)}, u32[]{:S(2)}) collective-permute-start(f32[136,256]{1,0:T(8,128)S(1)} %copy-done.17), channel_id=1, source_target_pairs={{32,0},{64,32},{96,64},{128,96},{160,128},{192,160},{224,192},{33,... | collective-permute-start | bytes 417800 | tf_op jit(solution)/shard_map/ppermute | solution.py:352
  140.4 14.7 %collective-permute-start.19 = (f32[256,128]{1,0:T(8,128)S(1)}, f32[256,128]{1,0:T(8,128)S(1)}, u32[]{:S(2)}, u32[]{:S(2)}) collective-permute-start(f32[256,128]{1,0:T(8,128)S(1)} %get-tuple-element.68), channel_id=1, source_target_pairs={{0,1},{1,0},{2,3},{3,2},{4,5},{5,4},{6,7},{7,6},{8,9},{9,8},{10,11... | collective-permute-start | bytes 393224 | tf_op jit(solution)/shard_map/ppermute | solution.py:356
  142.0 13.1 %collective-permute-start.20 = (f32[256,128]{1,0:T(8,128)S(1)}, f32[256,128]{1,0:T(8,128)S(1)}, u32[]{:S(2)}, u32[]{:S(2)}) collective-permute-start(f32[256,128]{1,0:T(8,128)S(1)} %get-tuple-element.69), channel_id=1, source_target_pairs={{1,2},{3,4},{5,6},{7,8},{9,10},{11,12},{13,14},{15,16},{17,18},{19... | collective-permute-start | bytes 393224 | tf_op jit(solution)/shard_map/ppermute | solution.py:363
  145.3 6.0 %collective-permute-start.18 = (f32[32,128]{1,0:T(8,128)S(1)}, f32[32,128]{1,0:T(8,128)S(1)}, u32[]{:S(2)}, u32[]{:S(2)}) collective-permute-start(f32[32,128]{1,0:T(8,128)S(1)} %get-tuple-element.72.a), channel_id=1, source_target_pairs={{0,6},{1,7},{2,4},{3,5},{4,2},{5,3},{6,0},{7,1},{8,14},{9,15},{10,... | collective-permute-start | bytes 49160 | tf_op jit(solution)/shard_map/ppermute | solution.py:356
  148.5 6.5 %collective-permute-start.17 = (f32[32,128]{1,0:T(8,128)S(1)}, f32[32,128]{1,0:T(8,128)S(1)}, u32[]{:S(2)}, u32[]{:S(2)}) collective-permute-start(f32[32,128]{1,0:T(8,128)S(1)} %get-tuple-element.72.a), channel_id=1, source_target_pairs={{0,4},{1,5},{2,6},{3,7},{4,0},{5,1},{6,2},{7,3},{8,12},{9,13},{10,... | collective-permute-start | bytes 49160 | tf_op jit(solution)/shard_map/ppermute | solution.py:356
  151.3 3.8 %collective-permute-start.16 = (f32[32,128]{1,0:T(8,128)S(1)}, f32[32,128]{1,0:T(8,128)S(1)}, u32[]{:S(2)}, u32[]{:S(2)}) collective-permute-start(f32[32,128]{1,0:T(8,128)S(1)} %get-tuple-element.72.a), channel_id=1, source_target_pairs={{0,2},{1,3},{2,0},{3,1},{4,6},{5,7},{6,4},{7,5},{8,10},{9,11},{10,... | collective-permute-start | bytes 49160 | tf_op jit(solution)/shard_map/ppermute | solution.py:356
  171.8 4.5 %collective-permute-start.21 = (f32[1024,128]{1,0:T(8,128)S(1)}, f32[1024,128]{1,0:T(8,128)S(1)}, u32[]{:S(2)}, u32[]{:S(2)}) collective-permute-start(f32[1024,128]{1,0:T(8,128)S(1)} %bitcast.10), channel_id=1, source_target_pairs={{0,1},{1,0},{2,3},{3,2},{4,5},{5,4},{6,7},{7,6},{8,9},{9,8},{10,11... | collective-permute-start | bytes 1572872 | tf_op jit(solution)/shard_map/ppermute | solution.py:356
  (19 other events, 349.1 us)

commit v5 on v4

--- a/solution.py
+++ b/solution.py
@@ -130,14 +130,16 @@
     count = 7 if first else 14
     arrays, refs = refs[:count], refs[count:]
     if first:
-        *stores, su, sd, own = refs[:5]
+        *stores, s1, s2, own = refs[:5]
         ext, canvas, raw, head, keep, send, outs, *inner, sems = refs[5:]
         up, mid, down, off, probe, amps, table = inner
     else:
-        *stores, su, sd, own, obj, probe_out = refs[:7]
+        *stores, s1, s2, own, obj, probe_out = refs[:7]
         ext, canvas, raw, head, keep, send, outs, probe, *inner, sems = refs[7:]
         up, mid, down, off, ci, cm, co, di, do, probe_in, mine, other, amps, table = inner
     wait = fetch(arrays, inner, sems)
+    canvas[...] = jnp.zeros(canvas.shape, f32)
+    raw[...] = jnp.zeros(raw.shape, f32)
     wait(*range(4 if first else 9))
     o0 = off[0, 0, 0, 0]
     o1 = off[0, 0, 0, 1]
@@ -212,22 +214,22 @@
             keep[s, :] = jnp.where(core == 0, term[:, :LANE], term[:, LANE:])
             send[s, :] = jnp.where(core == 0, term[:, LANE:], term[:, :LANE])
     copies += store(zip((keep, send), stores), outs.at[8:10])
-    edge = (su.shape[0] - 8) // 2
+    edge = (s1.shape[0] - 8) // 2
+    at1 = pl.multiple_of(lax.rem(row + 1, 2) * (SPAN - edge), 8)
+    at2 = pl.multiple_of(lax.rem(row, 2) * (SPAN - edge), 8)
     skip = (SPAN - own.shape[1]) // 2
     head[...] = jnp.full((8, F), o1.astype(f32))
     for c, value in enumerate((ore, oim)):
-        canvas[c] = jnp.zeros((SPAN + 8, SPAN), f32)
-        raw[c] = jnp.zeros((SPAN + 8, F), f32)
         value = jnp.concatenate([value, jnp.zeros((8, F), f32)], axis=0)
         value = pltpu.roll(value, rest, 0)
         raw[c, pl.ds(base, F + 8), :] = value
         s = slice(c * edge, (c + 1) * edge)
         copies += store(
-            ((raw.at[c, :edge], su.at[s]), (raw.at[c, SPAN - edge:SPAN], sd.at[s])),
+            ((raw.at[c, pl.ds(at1, edge)], s1.at[s]), (raw.at[c, pl.ds(at2, edge)], s2.at[s])),
             outs.at[2 * c:2 * c + 2])
         canvas[c, pl.ds(base, F + 8), :] = shifted(value, o1)
         copies += store(((canvas.at[c, skip:SPAN - skip], own.at[c]),), outs.at[4 + c:5 + c])
-    copies += store(((head, su.at[2 * edge:]), (head, sd.at[2 * edge:])), outs.at[6:8])
+    copies += store(((head, s1.at[2 * edge:]), (head, s2.at[2 * edge:])), outs.at[6:8])
     finish(copies)
 
 
@@ -240,6 +242,12 @@
     edge = (strip.shape[0] - 8) // 2
     columns = jnp.max(strip[2 * edge:, :LANE]).astype(jnp.int32)
     return shifted(strip[c * edge:(c + 1) * edge, :], columns)
+
+
+def above_below(r1, r2, c):
+    x, y = arrived(r1, c), arrived(r2, c)
+    even = lax.rem(lax.axis_index("row"), 2) == 0
+    return jnp.where(even, y, x), jnp.where(even, x, y)
 
 
 def new_probe(core, probe, mine, other, out):
@@ -260,32 +268,34 @@
     out[...] = total
 
 
-def bands_kernel(parts, own, ru, rd, total, ci, cm, co, ti, tm, to, outs, *inner):
+def bands_kernel(parts, own, r1, r2, total, ci, cm, co, ti, tm, to, outs, *inner):
     *inner, sems = inner
-    wait = fetch((own, ru, rd), inner, sems)
-    own, ru, rd = inner
+    wait = fetch((own, r1, r2), inner, sems)
+    own, r1, r2 = inner
     chunk_sum(parts, total)
     wait(*range(3))
     for c in range(2):
+        above, below = above_below(r1, r2, c)
         rows = jnp.concatenate(
-            [own[c, :B] + arrived(ru, c), own[c, B:2 * B], own[c, 2 * B:] + arrived(rd, c)], axis=0)
+            [own[c, :B] + above, own[c, B:2 * B], own[c, 2 * B:] + below], axis=0)
         left, tm[c], right = rows[:, :B], rows[:, B:2 * B], rows[:, 2 * B:]
         ti[c] = choose(right, left)
         to[c] = choose(left, right)
     finish(store(zip((ti, to, tm), (ci, co, cm)), outs))
 
 
-def last_bands_kernel(parts, own, ru, rd, total, grad_out, near, far, grad, outs, *inner):
+def last_bands_kernel(parts, own, r1, r2, total, grad_out, near, far, grad, outs, *inner):
     *inner, sems = inner
-    wait = fetch((own, ru, rd), inner, sems)
-    own, ru, rd = inner
+    wait = fetch((own, r1, r2), inner, sems)
+    own, r1, r2 = inner
     chunk_sum(parts, total)
     low = lanes()
     wait(*range(3))
     for c in range(2):
-        grad[c, :H] = own[c, :H] + arrived(ru, c)
+        above, below = above_below(r1, r2, c)
+        grad[c, :H] = own[c, :H] + above
         grad[c, H:TILE - H] = own[c, H:TILE - H]
-        grad[c, TILE - H:] = own[c, TILE - H:] + arrived(rd, c)
+        grad[c, TILE - H:] = own[c, TILE - H:] + below
     copies = store(((grad, grad_out),), outs)
     left = jnp.where(low, grad[0, :, :LANE], half_turn(grad[1, :, :LANE]))
     right = jnp.where(low, half_turn(grad[0, :, 2 * LANE:]), grad[1, :, 2 * LANE:])
@@ -356,6 +366,13 @@
     return lax.ppermute(x, RC, [(i, i ^ mask) for i in range(256)])
 
 
+def add_kernel(keep, arrived_half, out, total, outs, *inner):
+    *inner, sems = inner
+    fetch((keep, arrived_half), inner, sems)(0, 1)
+    total[...] = inner[0][...] + inner[1][...]
+    finish(store(((total, out),), outs))
+
+
 def columns(near, far):
     count = lax.axis_size("col")
     pairs = [(i, i + 1) for i in range(1, count - 1, 2)]
@@ -373,9 +390,21 @@
 CHUNK = 1024 // COUNT
 
 
-def scatter(keep, send):
-    x = keep + exchange(send, BIT_CORE)
-    return lax.all_to_all(x, RC, 0, 0, axis_index_groups=groups(WIDE), tiled=True)
+def scatter(keep, send, s1, s2):
+    count = lax.axis_size("row")
+    pairs = [(i, i + 1) for i in range(1, count - 1, 2)]
+    pairs += [(j, i) for i, j in pairs]
+    recv, r1 = lax.optimization_barrier((exchange(send, BIT_CORE), exchange(s1, BIT_ZLO)))
+    (x,) = call(
+        add_kernel,
+        [(1024, LANE)],
+        "add",
+        specs=[HBM] * 2,
+        places=[HBM],
+        scratch=[pltpu.VMEM((1024, LANE), f32), pltpu.SemaphoreType.DMA((1,))],
+    )(keep, recv)
+    x = lax.all_to_all(x, RC, 0, 0, axis_index_groups=groups(WIDE), tiled=True)
+    return x, r1, lax.ppermute(s2, "row", pairs)
 
 
 def gather(x, *early):
@@ -398,7 +427,7 @@
     halves = [(1024, LANE)] * 2
     held = [pltpu.VMEM((2, SPAN + 8, SPAN), f32)] * 2 + [pltpu.VMEM((2, SPAN + 8, F), f32)]
     held += [pltpu.VMEM((8, F), f32)] + [pltpu.VMEM((1024, LANE), f32)] * 2
-    keep, send, su, sd, own = call(
+    keep, send, s1, s2, own = call(
         functools.partial(frame_kernel, True),
         halves + [(2 * B + 8, F)] * 2 + [(2, SPAN, SPAN)],
         "frame1",
@@ -407,8 +436,7 @@
         [HBM] * 5,
         held + [pltpu.SemaphoreType.DMA((10,))],
     )(up, mid, down, offsets, probe, amplitudes, table)
-    ru = shift(sd, "row", 1)
-    rd = shift(su, "row", -1)
+    parts, r1, r2 = scatter(keep, send, s1, s2)
     total, ci, cm, co = call(
         bands_kernel,
         [(CHUNK, LANE)] + [(2, SPAN, B)] * 3,
@@ -416,10 +444,10 @@
         specs=[VM] + [HBM] * 3,
         places=[VM] + [HBM] * 3,
         scratch=[pltpu.VMEM((2, SPAN, B), f32)] * 3 + [pltpu.SemaphoreType.DMA((3,))],
-    )(scatter(keep, send), own, ru, rd)
+    )(parts, own, r1, r2)
     mine, other, di, do = gather(total, *columns(ci, co))
 
-    keep, send, su, sd, own, obj, probe = call(
+    keep, send, s1, s2, own, obj, probe = call(
         functools.partial(frame_kernel, False),
         halves + [(2 * H + 8, F)] * 2 + [(2, TILE, SPAN)] * 2 + [(2, M, F, F)],
         "frame2",
@@ -428,8 +456,7 @@
         [HBM] * 7,
         held + [pltpu.SemaphoreType.DMA((13,)), pltpu.VMEM((2, M, F, F), f32)],
     )(up, mid, down, offsets, ci, cm, co, di, do, probe, mine, other, amplitudes, table)
-    ru = shift(sd, "row", 1)
-    rd = shift(su, "row", -1)
+    parts, r1, r2 = scatter(keep, send, s1, s2)
     total, grad, near, far = call(
         last_bands_kernel,
         [(CHUNK, LANE), (2, TILE, SPAN)] + [(TILE, LANE)] * 2,
@@ -437,7 +464,7 @@
         specs=[VM] + [HBM] * 3,
         places=[VM, HBM, VM, VM],
         scratch=[pltpu.VMEM((2, TILE, SPAN), f32), pltpu.SemaphoreType.DMA((1,))],
-    )(scatter(keep, send), own, ru, rd)
+    )(parts, own, r1, r2)
     mine, other, near, far = gather(total, *columns(near, far))
     return tuple(
         call(

time: 179 us -> 181 us (1.011)
  waiting for transfers between devices: 49.3 us -> 55.8 us
  blocking collectives: 35.5 us -> 30.8 us
  other arithmetic: 4.04 us -> 0 us
  local copies, waits for them, and re-layouts: 3.41 us -> 5.49 us
    ppermute x6 -> x2, waiting for transfers between devices: 28.1 us -> 5.11 us  [shift(): return lax.ppermute(x, axis, pairs)]
    all_to_all x2, waiting for transfers between devices: 0.01 us -> 17.9 us  [scatter(): x = lax.all_to_all(x, RC, 0, 0, axis_index_groups=groups(WIDE), tiled=True)]
    ppermute x13 -> x15, waiting for transfers between devices: 15.5 us -> 27.3 us  [exchange(): return lax.ppermute(x, RC, [(i, i ^ mask) for i in range(256)])]
    ppermute x6 -> x2, starting transfers between devices: 11.5 us -> 2.58 us  [shift(): return lax.ppermute(x, axis, pairs)]
    ppermute x13 -> x15, starting transfers between devices: 25 us -> 31.4 us  [exchange(): return lax.ppermute(x, RC, [(i, i ^ mask) for i in range(256)])]
    all_to_all x2, blocking collectives: 35.5 us -> 30.8 us  [gather(): x = lax.all_to_all(x, RC, 0, 0, axis_index_groups=groups(WIDE), tiled=True)]
    add x2 -> x0, other arithmetic: 4.04 us -> none  [scatter(): x = keep + exchange(send, BIT_CORE)]
    unnamed x38, local copies, waits for them, and re-layouts: 3.41 us -> 5.49 us
  transfers between devices with their start and end apart: 24 -> 24, of which waited for: 16 -> 14; matrix products, arithmetic and copies ran while one was open for 0% -> 0% of each run, Pallas kernels for 0% -> 0%
where the time goes in v5:
time: 181 us; the launch traced here: 180 us
  starting transfers between devices  64.3 us (36%)
  waiting for transfers between devices  55.8 us (31%)
  blocking collectives  30.8 us (17%)
  Pallas kernels  22.4 us (12%)
  local copies, waits for them, and re-layouts  5.49 us (3%)
    ppermute x15, starting transfers between devices, exchange(): return lax.ppermute(x, RC, [(i, i ^ mask) for i in range(256)])  31.4 us
    all_to_all x2, blocking collectives, gather(): x = lax.all_to_all(x, RC, 0, 0, axis_index_groups=groups(WIDE), tiled=True)  30.8 us
    ppermute x15, waiting for transfers between devices, exchange(): return lax.ppermute(x, RC, [(i, i ^ mask) for i in range(256)])  27.3 us
    pallas_call x11, Pallas kernels, run(): pl.pallas_call(kernel, out_shape=[jax.ShapeDtypeStruct(s, f32) for s in o...  22.4 us
    all_to_all x2, starting transfers between devices, scatter(): x = lax.all_to_all(x, RC, 0, 0, axis_index_groups=groups(WIDE), tiled=True)  18.2 us
    all_to_all x2, waiting for transfers between devices, scatter(): x = lax.all_to_all(x, RC, 0, 0, axis_index_groups=groups(WIDE), tiled=True)  17.9 us
    ppermute x3, starting transfers between devices, columns(): return (exchange(near, BIT_CORE), lax.ppermute(far, 'col', pairs))  10.8 us
    ppermute x3, waiting for transfers between devices, columns(): return (exchange(near, BIT_CORE), lax.ppermute(far, 'col', pairs))  5.49 us
  transfers between devices with their start and end apart: 24, of which 14 were waited for; matrix products, arithmetic and copies ran while one was open for 0% of the time, Pallas kernels for 0%

profile of v5, /device:TPU:1, one launch (start us, length us, event | category | flops | bytes accessed | tf_op | source)
XLA Modules:
  0.0 179.9 jit_solution(6113624199450783487)
XLA Ops:
  1.8 3.3 %collective-permute-start = (f32[256,128]{1,0:T(8,128)S(1)}, f32[256,128]{1,0:T(8,128)S(1)}, u32[]{:S(2)}, u32[]{:S(2)}) collective-permute-start(f32[256,128]{1,0:T(8,128)S(1)} %get-tuple-element.43), channel_id=1, source_target_pairs={{0,1},{1,0},{2,3},{3,2},{4,5},{5,4},{6,7},{7,6},{8,9},{9,8},{10,11... | collective-permute-start | bytes 393224 | tf_op jit(solution)/shard_map/ppermute | solution.py:366
  5.1 3.1 %collective-permute-start.1 = (f32[256,128]{1,0:T(8,128)S(1)}, f32[256,128]{1,0:T(8,128)S(1)}, u32[]{:S(2)}, u32[]{:S(2)}) collective-permute-start(f32[256,128]{1,0:T(8,128)S(1)} %get-tuple-element.44), channel_id=1, source_target_pairs={{1,2},{3,4},{5,6},{7,8},{9,10},{11,12},{13,14},{15,16},{17,18},{19... | collective-permute-start | bytes 393224 | tf_op jit(solution)/shard_map/ppermute | solution.py:380
  8.2 5.5 %collective-permute-done.1.outer = f32[256,128]{1,0:T(8,128)S(1)} collective-permute-done((f32[256,128]{1,0:T(8,128)S(1)}, f32[256,128]{1,0:T(8,128)S(1)}, u32[]{:S(2)}, u32[]{:S(2)}) %collective-permute-start.1) | collective-permute-done | bytes 131104 | tf_op jit(solution)/shard_map/ppermute | solution.py:380
  18.7 3.8 %collective-permute-done.3.refs_2_ = f32[2,64,384]{2,1,0:T(8,128)S(1)} collective-permute-done((f32[2,64,384]{2,1,0:T(8,128)S(1)}, f32[2,64,384]{2,1,0:T(8,128)S(1)}, u32[]{:S(2)}, u32[]{:S(2)}) %collective-permute-start.3) | collective-permute-done | bytes 196640 | tf_op jit(solution)/shard_map/ppermute | solution.py:362
  23.2 7.5 %frame1.1 = (f32[1024,128]{1,0:T(8,128)}, f32[1024,128]{1,0:T(8,128)}, f32[264,256]{1,0:T(8,128)}, f32[264,256]{1,0:T(8,128)}, f32[2,384,384]{2,1,0:T(8,128)}) custom-call(f32[2,64,384]{2,1,0:T(8,128)} %copy-done.12, f32[2,256,384]{2,1,0:T(8,128)} %copy-done, f32[2,64,384]{2,1,0:T(8,128)} %copy-done.13, s32[1,1,1,2]{3,2,1,0:T(1,128)} %refs_3_.3, ...), custom_call_target="tpu_custom_call" | custom-call | tf_op jit(solution)/shard_map/frame1/pallas_call | solution.py:346
  32.0 6.7 %collective-permute-done.5.r1 = f32[264,256]{1,0:T(8,128)S(1)} collective-permute-done((f32[264,256]{1,0:T(8,128)}, f32[264,256]{1,0:T(8,128)S(1)}, u32[]{:S(2)}, u32[]{:S(2)}) %collective-permute-start.5) | collective-permute-done | bytes 270368 | tf_op jit(solution)/shard_map/ppermute | solution.py:366
  40.8 14.1 %all-to-all-start = ((f32[32,32,128]{2,1,0:T(8,128)}), f32[32,32,128]{2,1,0:T(8,128)S(1)}, u32[]{:S(2)}, u32[]{:S(2)}) async-start(f32[32,32,128]{2,1,0:T(8,128)} %bitcast), calls=%async_computation | async-start | bytes 1048576 | tf_op jit(solution)/shard_map/all_to_all | solution.py:406
  55.6 9.0 %all-to-all-done = f32[32,32,128]{2,1,0:T(8,128)S(1)} async-done(((f32[32,32,128]{2,1,0:T(8,128)}), f32[32,32,128]{2,1,0:T(8,128)S(1)}, u32[]{:S(2)}, u32[]{:S(2)}) %all-to-all-start) | async-done | bytes 524320 | tf_op jit(solution)/shard_map/all_to_all | solution.py:406
  66.0 3.5 %collective-permute-start.10 = (f32[2,384,128]{2,1,0:T(8,128)S(1)}, f32[2,384,128]{2,1,0:T(8,128)S(1)}, u32[]{:S(2)}, u32[]{:S(2)}) collective-permute-start(f32[2,384,128]{2,1,0:T(8,128)S(1)} %get-tuple-element.55.refs_4_), channel_id=1, source_target_pairs={{0,1},{1,0},{2,3},{3,2},{4,5},{5,4},{6,7},{7,6},{8,9},{9,8},{10,11... | collective-permute-start | bytes 1179656 | tf_op jit(solution)/shard_map/ppermute | solution.py:366
  69.5 3.9 %collective-permute-start.11 = (f32[2,384,128]{2,1,0:T(8,128)S(1)}, f32[2,384,128]{2,1,0:T(8,128)S(1)}, u32[]{:S(2)}, u32[]{:S(2)}) collective-permute-start(f32[2,384,128]{2,1,0:T(8,128)S(1)} %get-tuple-element.57.refs_6_), channel_id=1, source_target_pairs={{1,2},{3,4},{5,6},{7,8},{9,10},{11,12},{13,14},{15,16},{17,18},{19... | collective-permute-start | bytes 1179656 | tf_op jit(solution)/shard_map/ppermute | solution.py:380
  76.1 4.0 %collective-permute-start.8 = (f32[32,128]{1,0:T(8,128)S(1)}, f32[32,128]{1,0:T(8,128)S(1)}, u32[]{:S(2)}, u32[]{:S(2)}) collective-permute-start(f32[32,128]{1,0:T(8,128)S(1)} %get-tuple-element.61.a), channel_id=1, source_target_pairs={{0,4},{1,5},{2,6},{3,7},{4,0},{5,1},{6,2},{7,3},{8,12},{9,13},{10,... | collective-permute-start | bytes 49160 | tf_op jit(solution)/shard_map/ppermute | solution.py:366
  83.2 5.0 %collective-permute-done.7.b = f32[32,128]{1,0:T(8,128)S(1)} collective-permute-done((f32[32,128]{1,0:T(8,128)S(1)}, f32[32,128]{1,0:T(8,128)S(1)}, u32[]{:S(2)}, u32[]{:S(2)}) %collective-permute-start.7) | collective-permute-done | bytes 16416 | tf_op jit(solution)/shard_map/ppermute | solution.py:366
  88.2 16.5 %all_to_all.44 = f32[32,32,128]{2,1,0:T(8,128)S(1)} all-to-all(f32[32,32,128]{2,1,0:T(8,128)S(1)} %bitcast.12), channel_id=1, replica_groups={{0,8,16,24,32,40,48,56,64,72,80,88,96,104,112,120,128,136,144,152,160,1..., dimensions={0} | all-to-all | bytes 1048576 | tf_op jit(solution)/shard_map/all_to_all | solution.py:414
  104.8 3.0 %collective-permute-start.12 = (f32[1024,128]{1,0:T(8,128)S(1)}, f32[1024,128]{1,0:T(8,128)S(1)}, u32[]{:S(2)}, u32[]{:S(2)}) collective-permute-start(f32[1024,128]{1,0:T(8,128)S(1)} %bitcast.14), channel_id=1, source_target_pairs={{0,1},{1,0},{2,3},{3,2},{4,5},{5,4},{6,7},{7,6},{8,9},{9,8},{10,11... | collective-permute-start | bytes 1572872 | tf_op jit(solution)/shard_map/ppermute | solution.py:366
  110.1 8.3 %frame2.1 = (f32[1024,128]{1,0:T(8,128)}, f32[1024,128]{1,0:T(8,128)}, f32[136,256]{1,0:T(8,128)}, f32[136,256]{1,0:T(8,128)}, f32[2,256,384]{2,1,0:T(8,128)}, /...) custom-call(f32[2,64,384]{2,1,0:T(8,128)} %copy-done.12, f32[2,256,384]{2,1,0:T(8,128)} %copy-done, ...), custom_call_target="tpu_custom_call" | custom-call | tf_op jit(solution)/shard_map/frame2/pallas_call | solution.py:346
  119.6 4.7 %collective-permute-done.14.r1 = f32[136,256]{1,0:T(8,128)S(1)} collective-permute-done((f32[136,256]{1,0:T(8,128)}, f32[136,256]{1,0:T(8,128)S(1)}, u32[]{:S(2)}, u32[]{:S(2)}) %collective-permute-start.14) | collective-permute-done | bytes 139296 | tf_op jit(solution)/shard_map/ppermute | solution.py:366
  126.3 4.1 %all-to-all-start.2 = ((f32[32,32,128]{2,1,0:T(8,128)}), f32[32,32,128]{2,1,0:T(8,128)S(1)}, u32[]{:S(2)}, u32[]{:S(2)}) async-start(f32[32,32,128]{2,1,0:T(8,128)} %bitcast.4), calls=%async_computation.2 | async-start | bytes 1048576 | tf_op jit(solution)/shard_map/all_to_all | solution.py:406
  131.1 8.9 %all-to-all-done.2 = f32[32,32,128]{2,1,0:T(8,128)S(1)} async-done(((f32[32,32,128]{2,1,0:T(8,128)}), f32[32,32,128]{2,1,0:T(8,128)S(1)}, u32[]{:S(2)}, u32[]{:S(2)}) %all-to-all-start.2) | async-done | bytes 524320 | tf_op jit(solution)/shard_map/all_to_all | solution.py:406
  141.1 3.7 %collective-permute-start.19 = (f32[256,128]{1,0:T(8,128)S(1)}, f32[256,128]{1,0:T(8,128)S(1)}, u32[]{:S(2)}, u32[]{:S(2)}) collective-permute-start(f32[256,128]{1,0:T(8,128)S(1)} %get-tuple-element.76), channel_id=1, source_target_pairs={{0,1},{1,0},{2,3},{3,2},{4,5},{5,4},{6,7},{7,6},{8,9},{9,8},{10,11... | collective-permute-start | bytes 393224 | tf_op jit(solution)/shard_map/ppermute | solution.py:366
  144.8 3.8 %collective-permute-start.20 = (f32[256,128]{1,0:T(8,128)S(1)}, f32[256,128]{1,0:T(8,128)S(1)}, u32[]{:S(2)}, u32[]{:S(2)}) collective-permute-start(f32[256,128]{1,0:T(8,128)S(1)} %get-tuple-element.77), channel_id=1, source_target_pairs={{1,2},{3,4},{5,6},{7,8},{9,10},{11,12},{13,14},{15,16},{17,18},{19... | collective-permute-start | bytes 393224 | tf_op jit(solution)/shard_map/ppermute | solution.py:380
  148.6 2.9 %collective-permute-start.18 = (f32[32,128]{1,0:T(8,128)S(1)}, f32[32,128]{1,0:T(8,128)S(1)}, u32[]{:S(2)}, u32[]{:S(2)}) collective-permute-start(f32[32,128]{1,0:T(8,128)S(1)} %get-tuple-element.80.a), channel_id=1, source_target_pairs={{0,6},{1,7},{2,4},{3,5},{4,2},{5,3},{6,0},{7,1},{8,14},{9,15},{10,... | collective-permute-start | bytes 49160 | tf_op jit(solution)/shard_map/ppermute | solution.py:366
  154.4 4.6 %collective-permute-done.17.c = f32[32,128]{1,0:T(8,128)S(1)} collective-permute-done((f32[32,128]{1,0:T(8,128)S(1)}, f32[32,128]{1,0:T(8,128)S(1)}, u32[]{:S(2)}, u32[]{:S(2)}) %collective-permute-start.17) | collective-permute-done | bytes 16416 | tf_op jit(solution)/shard_map/ppermute | solution.py:366
  159.1 14.3 %all_to_all.45 = f32[32,32,128]{2,1,0:T(8,128)S(1)} all-to-all(f32[32,32,128]{2,1,0:T(8,128)S(1)} %bitcast.13), channel_id=1, replica_groups={{0,8,16,24,32,40,48,56,64,72,80,88,96,104,112,120,128,136,144,152,160,1..., dimensions={0} | all-to-all | bytes 1048576 | tf_op jit(solution)/shard_map/all_to_all | solution.py:414
  173.4 3.0 %collective-permute-start.21 = (f32[1024,128]{1,0:T(8,128)S(1)}, f32[1024,128]{1,0:T(8,128)S(1)}, u32[]{:S(2)}, u32[]{:S(2)}) collective-permute-start(f32[1024,128]{1,0:T(8,128)S(1)} %bitcast.10), channel_id=1, source_target_pairs={{0,1},{1,0},{2,3},{3,2},{4,5},{5,4},{6,7},{7,6},{8,9},{9,8},{10,11... | collective-permute-start | bytes 1572872 | tf_op jit(solution)/shard_map/ppermute | solution.py:366
  (75 shorter events, 31.7 us)
Async XLA Ops:
  1.8 6.4 %collective-permute-start = (f32[256,128]{1,0:T(8,128)S(1)}, f32[256,128]{1,0:T(8,128)S(1)}, u32[]{:S(2)}, u32[]{:S(2)}) collective-permute-start(f32[256,128]{1,0:T(8,128)S(1)} %get-tuple-element.43), channel_id=1, source_target_pairs={{0,1},{1,0},{2,3},{3,2},{4,5},{5,4},{6,7},{7,6},{8,9},{9,8},{10,11... | collective-permute-start | bytes 393224 | tf_op jit(solution)/shard_map/ppermute | solution.py:366
  5.1 8.6 %collective-permute-start.1 = (f32[256,128]{1,0:T(8,128)S(1)}, f32[256,128]{1,0:T(8,128)S(1)}, u32[]{:S(2)}, u32[]{:S(2)}) collective-permute-start(f32[256,128]{1,0:T(8,128)S(1)} %get-tuple-element.44), channel_id=1, source_target_pairs={{1,2},{3,4},{5,6},{7,8},{9,10},{11,12},{13,14},{15,16},{17,18},{19... | collective-permute-start | bytes 393224 | tf_op jit(solution)/shard_map/ppermute | solution.py:380
  14.9 3.9 %collective-permute-start.2 = (f32[2,64,384]{2,1,0:T(8,128)S(1)}, f32[2,64,384]{2,1,0:T(8,128)S(1)}, u32[]{:S(2)}, u32[]{:S(2)}) collective-permute-start(f32[2,64,384]{2,1,0:T(8,128)S(1)} %get-tuple-element.45), channel_id=1, source_target_pairs={{0,32},{32,64},{64,96},{96,128},{128,160},{160,192},{192,224},{1,3... | collective-permute-start | bytes 589832 | tf_op jit(solution)/shard_map/ppermute | solution.py:362
  16.2 6.4 %collective-permute-start.3 = (f32[2,64,384]{2,1,0:T(8,128)S(1)}, f32[2,64,384]{2,1,0:T(8,128)S(1)}, u32[]{:S(2)}, u32[]{:S(2)}) collective-permute-start(f32[2,64,384]{2,1,0:T(8,128)S(1)} %get-tuple-element.47), channel_id=1, source_target_pairs={{32,0},{64,32},{96,64},{128,96},{160,128},{192,160},{224,192},{33,... | collective-permute-start | bytes 589832 | tf_op jit(solution)/shard_map/ppermute | solution.py:362
  30.7 8.1 %collective-permute-start.4 = (f32[1024,128]{1,0:T(8,128)}, f32[1024,128]{1,0:T(8,128)S(1)}, u32[]{:S(2)}, u32[]{:S(2)}) collective-permute-start(f32[1024,128]{1,0:T(8,128)} %get-tuple-element.49), channel_id=1, source_target_pairs={{0,1},{1,0},{2,3},{3,2},{4,5},{5,4},{6,7},{7,6},{8,9},{9,8},{10,11... | collective-permute-start | bytes 1572872 | tf_op jit(solution)/shard_map/ppermute | solution.py:366
  30.8 7.9 %collective-permute-start.5 = (f32[264,256]{1,0:T(8,128)}, f32[264,256]{1,0:T(8,128)S(1)}, u32[]{:S(2)}, u32[]{:S(2)}) collective-permute-start(f32[264,256]{1,0:T(8,128)} %get-tuple-element.50), channel_id=1, source_target_pairs={{0,32},{1,33},{2,34},{3,35},{4,36},{5,37},{6,38},{7,39},{8,40},{9,... | collective-permute-start | bytes 811016 | tf_op jit(solution)/shard_map/ppermute | solution.py:366
  40.8 23.8 %all-to-all-start = ((f32[32,32,128]{2,1,0:T(8,128)}), f32[32,32,128]{2,1,0:T(8,128)S(1)}, u32[]{:S(2)}, u32[]{:S(2)}) async-start(f32[32,32,128]{2,1,0:T(8,128)} %bitcast), calls=%async_computation | async-start | bytes 1048576 | tf_op jit(solution)/shard_map/all_to_all | solution.py:406
  54.9 0.7 collective-permute-start.6
  66.0 22.2 %collective-permute-start.10 = (f32[2,384,128]{2,1,0:T(8,128)S(1)}, f32[2,384,128]{2,1,0:T(8,128)S(1)}, u32[]{:S(2)}, u32[]{:S(2)}) collective-permute-start(f32[2,384,128]{2,1,0:T(8,128)S(1)} %get-tuple-element.55.refs_4_), channel_id=1, source_target_pairs={{0,1},{1,0},{2,3},{3,2},{4,5},{5,4},{6,7},{7,6},{8,9},{9,8},{10,11... | collective-permute-start | bytes 1179656 | tf_op jit(solution)/shard_map/ppermute | solution.py:366
  69.5 18.6 %collective-permute-start.11 = (f32[2,384,128]{2,1,0:T(8,128)S(1)}, f32[2,384,128]{2,1,0:T(8,128)S(1)}, u32[]{:S(2)}, u32[]{:S(2)}) collective-permute-start(f32[2,384,128]{2,1,0:T(8,128)S(1)} %get-tuple-element.57.refs_6_), channel_id=1, source_target_pairs={{1,2},{3,4},{5,6},{7,8},{9,10},{11,12},{13,14},{15,16},{17,18},{19... | collective-permute-start | bytes 1179656 | tf_op jit(solution)/shard_map/ppermute | solution.py:380
  73.4 8.2 %collective-permute-start.9 = (f32[32,128]{1,0:T(8,128)S(1)}, f32[32,128]{1,0:T(8,128)S(1)}, u32[]{:S(2)}, u32[]{:S(2)}) collective-permute-start(f32[32,128]{1,0:T(8,128)S(1)} %get-tuple-element.61.a), channel_id=1, source_target_pairs={{0,6},{1,7},{2,4},{3,5},{4,2},{5,3},{6,0},{7,1},{8,14},{9,15},{10,... | collective-permute-start | bytes 49160 | tf_op jit(solution)/shard_map/ppermute | solution.py:366
  76.1 7.1 %collective-permute-start.8 = (f32[32,128]{1,0:T(8,128)S(1)}, f32[32,128]{1,0:T(8,128)S(1)}, u32[]{:S(2)}, u32[]{:S(2)}) collective-permute-start(f32[32,128]{1,0:T(8,128)S(1)} %get-tuple-element.61.a), channel_id=1, source_target_pairs={{0,4},{1,5},{2,6},{3,7},{4,0},{5,1},{6,2},{7,3},{8,12},{9,13},{10,... | collective-permute-start | bytes 49160 | tf_op jit(solution)/shard_map/ppermute | solution.py:366
  80.0 8.1 %collective-permute-start.7 = (f32[32,128]{1,0:T(8,128)S(1)}, f32[32,128]{1,0:T(8,128)S(1)}, u32[]{:S(2)}, u32[]{:S(2)}) collective-permute-start(f32[32,128]{1,0:T(8,128)S(1)} %get-tuple-element.61.a), channel_id=1, source_target_pairs={{0,2},{1,3},{2,0},{3,1},{4,6},{5,7},{6,4},{7,5},{8,10},{9,11},{10,... | collective-permute-start | bytes 49160 | tf_op jit(solution)/shard_map/ppermute | solution.py:366
  104.8 4.5 %collective-permute-start.12 = (f32[1024,128]{1,0:T(8,128)S(1)}, f32[1024,128]{1,0:T(8,128)S(1)}, u32[]{:S(2)}, u32[]{:S(2)}) collective-permute-start(f32[1024,128]{1,0:T(8,128)S(1)} %bitcast.14), channel_id=1, source_target_pairs={{0,1},{1,0},{2,3},{3,2},{4,5},{5,4},{6,7},{7,6},{8,9},{9,8},{10,11... | collective-permute-start | bytes 1572872 | tf_op jit(solution)/shard_map/ppermute | solution.py:366
  118.5 5.8 %collective-permute-start.13 = (f32[1024,128]{1,0:T(8,128)}, f32[1024,128]{1,0:T(8,128)S(1)}, u32[]{:S(2)}, u32[]{:S(2)}) collective-permute-start(f32[1024,128]{1,0:T(8,128)} %get-tuple-element.67), channel_id=1, source_target_pairs={{0,1},{1,0},{2,3},{3,2},{4,5},{5,4},{6,7},{7,6},{8,9},{9,8},{10,11... | collective-permute-start | bytes 1572872 | tf_op jit(solution)/shard_map/ppermute | solution.py:366
  119.0 5.3 %collective-permute-start.14 = (f32[136,256]{1,0:T(8,128)}, f32[136,256]{1,0:T(8,128)S(1)}, u32[]{:S(2)}, u32[]{:S(2)}) collective-permute-start(f32[136,256]{1,0:T(8,128)} %get-tuple-element.68), channel_id=1, source_target_pairs={{0,32},{1,33},{2,34},{3,35},{4,36},{5,37},{6,38},{7,39},{8,40},{9,... | collective-permute-start | bytes 417800 | tf_op jit(solution)/shard_map/ppermute | solution.py:366
  126.3 13.7 %all-to-all-start.2 = ((f32[32,32,128]{2,1,0:T(8,128)}), f32[32,32,128]{2,1,0:T(8,128)S(1)}, u32[]{:S(2)}, u32[]{:S(2)}) async-start(f32[32,32,128]{2,1,0:T(8,128)} %bitcast.4), calls=%async_computation.2 | async-start | bytes 1048576 | tf_op jit(solution)/shard_map/all_to_all | solution.py:406
  130.4 0.7 collective-permute-start.15
  141.1 17.9 %collective-permute-start.19 = (f32[256,128]{1,0:T(8,128)S(1)}, f32[256,128]{1,0:T(8,128)S(1)}, u32[]{:S(2)}, u32[]{:S(2)}) collective-permute-start(f32[256,128]{1,0:T(8,128)S(1)} %get-tuple-element.76), channel_id=1, source_target_pairs={{0,1},{1,0},{2,3},{3,2},{4,5},{5,4},{6,7},{7,6},{8,9},{9,8},{10,11... | collective-permute-start | bytes 393224 | tf_op jit(solution)/shard_map/ppermute | solution.py:366
  144.8 14.3 %collective-permute-start.20 = (f32[256,128]{1,0:T(8,128)S(1)}, f32[256,128]{1,0:T(8,128)S(1)}, u32[]{:S(2)}, u32[]{:S(2)}) collective-permute-start(f32[256,128]{1,0:T(8,128)S(1)} %get-tuple-element.77), channel_id=1, source_target_pairs={{1,2},{3,4},{5,6},{7,8},{9,10},{11,12},{13,14},{15,16},{17,18},{19... | collective-permute-start | bytes 393224 | tf_op jit(solution)/shard_map/ppermute | solution.py:380
  148.6 5.9 %collective-permute-start.18 = (f32[32,128]{1,0:T(8,128)S(1)}, f32[32,128]{1,0:T(8,128)S(1)}, u32[]{:S(2)}, u32[]{:S(2)}) collective-permute-start(f32[32,128]{1,0:T(8,128)S(1)} %get-tuple-element.80.a), channel_id=1, source_target_pairs={{0,6},{1,7},{2,4},{3,5},{4,2},{5,3},{6,0},{7,1},{8,14},{9,15},{10,... | collective-permute-start | bytes 49160 | tf_op jit(solution)/shard_map/ppermute | solution.py:366
  151.4 7.6 %collective-permute-start.17 = (f32[32,128]{1,0:T(8,128)S(1)}, f32[32,128]{1,0:T(8,128)S(1)}, u32[]{:S(2)}, u32[]{:S(2)}) collective-permute-start(f32[32,128]{1,0:T(8,128)S(1)} %get-tuple-element.80.a), channel_id=1, source_target_pairs={{0,4},{1,5},{2,6},{3,7},{4,0},{5,1},{6,2},{7,3},{8,12},{9,13},{10,... | collective-permute-start | bytes 49160 | tf_op jit(solution)/shard_map/ppermute | solution.py:366
  154.3 4.7 %collective-permute-start.16 = (f32[32,128]{1,0:T(8,128)S(1)}, f32[32,128]{1,0:T(8,128)S(1)}, u32[]{:S(2)}, u32[]{:S(2)}) collective-permute-start(f32[32,128]{1,0:T(8,128)S(1)} %get-tuple-element.80.a), channel_id=1, source_target_pairs={{0,2},{1,3},{2,0},{3,1},{4,6},{5,7},{6,4},{7,5},{8,10},{9,11},{10,... | collective-permute-start | bytes 49160 | tf_op jit(solution)/shard_map/ppermute | solution.py:366
  173.4 4.5 %collective-permute-start.21 = (f32[1024,128]{1,0:T(8,128)S(1)}, f32[1024,128]{1,0:T(8,128)S(1)}, u32[]{:S(2)}, u32[]{:S(2)}) collective-permute-start(f32[1024,128]{1,0:T(8,128)S(1)} %bitcast.10), channel_id=1, source_target_pairs={{0,1},{1,0},{2,3},{3,2},{4,5},{5,4},{6,7},{7,6},{8,9},{9,8},{10,11... | collective-permute-start | bytes 1572872 | tf_op jit(solution)/shard_map/ppermute | solution.py:366
  (19 other events, 316.1 us)

commit v6 on v4

--- a/solution.py
+++ b/solution.py
@@ -20,6 +20,9 @@
 probe_step = 4.0
 RC = ("row", "col")
 BIT_Y, BIT_ZLO, BIT_X, BIT_ZHI, BIT_CORE = 192, 32, 24, 6, 1
+
+COUNT, DEPTH = 16, 8
+CHUNK = 1024 // COUNT
 
 f32 = jnp.float32
 bf16 = jnp.bfloat16
@@ -252,19 +255,20 @@
         out[q // 2, q % 2] = probe[q // 2, q % 2] - coeff * total
 
 
-def chunk_sum(parts, out):
-    rows = out.shape[0]
+def chunk_sum(parts, count, out):
+    rows = parts.shape[0] // count
     total = parts[:rows, :]
-    for k in range(1, parts.shape[0] // rows):
+    for k in range(1, count):
         total = total + parts[k * rows:(k + 1) * rows, :]
-    out[...] = total
+    for k in range(out.shape[0] // rows):
+        out[k * rows:(k + 1) * rows, :] = total
 
 
 def bands_kernel(parts, own, ru, rd, total, ci, cm, co, ti, tm, to, outs, *inner):
     *inner, sems = inner
     wait = fetch((own, ru, rd), inner, sems)
     own, ru, rd = inner
-    chunk_sum(parts, total)
+    chunk_sum(parts, COUNT, total)
     wait(*range(3))
     for c in range(2):
         rows = jnp.concatenate(
@@ -279,7 +283,7 @@
     *inner, sems = inner
     wait = fetch((own, ru, rd), inner, sems)
     own, ru, rd = inner
-    chunk_sum(parts, total)
+    chunk_sum(parts, COUNT, total)
     low = lanes()
     wait(*range(3))
     for c in range(2):
@@ -294,11 +298,8 @@
     finish(copies)
 
 
-def spread_kernel(a, b, c, d, out):
-    total = (a[...] + b[...]) + (c[...] + d[...])
-    rows = a.shape[0]
-    for k in range(out.shape[0] // rows):
-        out[k * rows:(k + 1) * rows, :] = total
+def spread_kernel(parts, out):
+    chunk_sum(parts, DEPTH, out)
 
 
 def last_kernel(obj, grad, probe, near, far, mine, other, out, out_probe, *inner):
@@ -368,21 +369,19 @@
     return [[base | i for i in members] for base in range(256) if base & mask == 0]
 
 
-WIDE = BIT_Y | BIT_ZLO | BIT_X
-COUNT = 32
-CHUNK = 1024 // COUNT
+def all_to_all(x, mask):
+    return lax.all_to_all(x, RC, 0, 0, axis_index_groups=groups(mask), tiled=True)
 
 
 def scatter(keep, send):
-    x = keep + exchange(send, BIT_CORE)
-    return lax.all_to_all(x, RC, 0, 0, axis_index_groups=groups(WIDE), tiled=True)
+    return all_to_all(keep + exchange(send, BIT_CORE), BIT_Y | BIT_X)
 
 
 def gather(x, *early):
-    parts = (x, exchange(x, 2), exchange(x, 4), exchange(x, 6))
-    parts, early = lax.optimization_barrier((parts, early))
-    (x,) = call(spread_kernel, [(1024, LANE)], "spread")(*parts)
-    x = lax.all_to_all(x, RC, 0, 0, axis_index_groups=groups(WIDE), tiled=True)
+    x = all_to_all(x, BIT_ZLO | BIT_ZHI)
+    x, early = lax.optimization_barrier((x, early))
+    (x,) = call(spread_kernel, [(1024, LANE)], "spread")(x)
+    x = all_to_all(x, BIT_Y | BIT_X)
     return x, exchange(x, BIT_CORE), *early
 
 
@@ -411,7 +410,7 @@
     rd = shift(su, "row", -1)
     total, ci, cm, co = call(
         bands_kernel,
-        [(CHUNK, LANE)] + [(2, SPAN, B)] * 3,
+        [(DEPTH * CHUNK, LANE)] + [(2, SPAN, B)] * 3,
         "bands",
         specs=[VM] + [HBM] * 3,
         places=[VM] + [HBM] * 3,
@@ -432,7 +431,7 @@
     rd = shift(su, "row", -1)
     total, grad, near, far = call(
         last_bands_kernel,
-        [(CHUNK, LANE), (2, TILE, SPAN)] + [(TILE, LANE)] * 2,
+        [(DEPTH * CHUNK, LANE), (2, TILE, SPAN)] + [(TILE, LANE)] * 2,
         "last_bands",
         specs=[VM] + [HBM] * 3,
         places=[VM, HBM, VM, VM],

time: 179 us -> 185 us (1.034)
  waiting for transfers between devices: 49.3 us -> 57.8 us
  blocking collectives: 35.5 us -> 32 us
    ppermute x3, waiting for transfers between devices: 5.76 us -> 23.6 us  [columns(): return (exchange(near, BIT_CORE), lax.ppermute(far, 'col', pairs))]
    ppermute x13 -> x7, starting transfers between devices: 25 us -> 12.3 us  [exchange(): return lax.ppermute(x, RC, [(i, i ^ mask) for i in range(256)])]
    all_to_all x2 -> x4, starting transfers between devices: 17.7 us -> 28.1 us  [all_to_all(): lax.all_to_all(x, RC, 0, 0, axis_index_groups=groups(mask), tiled=True)]
    ppermute x13 -> x7, waiting for transfers between devices: 15.5 us -> 6.94 us  [exchange(): return lax.ppermute(x, RC, [(i, i ^ mask) for i in range(256)])]
    all_to_all x2, blocking collectives: 35.5 us -> 32 us  [all_to_all(): lax.all_to_all(x, RC, 0, 0, axis_index_groups=groups(mask), tiled=True)]
  transfers between devices with their start and end apart: 24 -> 20, of which waited for: 16 -> 13; matrix products, arithmetic and copies ran while one was open for 0% -> 0% of each run, Pallas kernels for 0% -> 0%
where the time goes in v6:
time: 185 us; the launch traced here: 184 us
  starting transfers between devices  62.9 us (34%)
  waiting for transfers between devices  57.8 us (31%)
  blocking collectives  32 us (17%)
  Pallas kernels  21.9 us (12%)
  local copies, waits for them, and re-layouts  4.22 us (2%)
  other arithmetic  4.04 us (2%)
    all_to_all x2, blocking collectives, all_to_all(): lax.all_to_all(x, RC, 0, 0, axis_index_groups=groups(mask), tiled=True)  32 us
    all_to_all x4, starting transfers between devices, all_to_all(): lax.all_to_all(x, RC, 0, 0, axis_index_groups=groups(mask), tiled=True)  28.1 us
    ppermute x6, waiting for transfers between devices, shift(): return lax.ppermute(x, axis, pairs)  27.2 us
    ppermute x3, waiting for transfers between devices, columns(): return (exchange(near, BIT_CORE), lax.ppermute(far, 'col', pairs))  23.6 us
    pallas_call x9, Pallas kernels, run(): pl.pallas_call(kernel, out_shape=[jax.ShapeDtypeStruct(s, f32) for s in o...  21.9 us
    ppermute x7, starting transfers between devices, exchange(): return lax.ppermute(x, RC, [(i, i ^ mask) for i in range(256)])  12.3 us
    ppermute x3, starting transfers between devices, columns(): return (exchange(near, BIT_CORE), lax.ppermute(far, 'col', pairs))  11.9 us
    ppermute x6, starting transfers between devices, shift(): return lax.ppermute(x, axis, pairs)  10.6 us
  transfers between devices with their start and end apart: 20, of which 13 were waited for; matrix products, arithmetic and copies ran while one was open for 0% of the time, Pallas kernels for 0%

profile of v6, /device:TPU:1, one launch (start us, length us, event | category | flops | bytes accessed | tf_op | source)
XLA Modules:
  0.0 184.0 jit_solution(3113045931008564768)
XLA Ops:
  1.8 3.3 %collective-permute-start = (f32[256,128]{1,0:T(8,128)S(1)}, f32[256,128]{1,0:T(8,128)S(1)}, u32[]{:S(2)}, u32[]{:S(2)}) collective-permute-start(f32[256,128]{1,0:T(8,128)S(1)} %get-tuple-element.33), channel_id=1, source_target_pairs={{0,1},{1,0},{2,3},{3,2},{4,5},{5,4},{6,7},{7,6},{8,9},{9,8},{10,11... | collective-permute-start | bytes 393224 | tf_op jit(solution)/shard_map/ppermute | solution.py:357
  5.1 3.1 %collective-permute-start.1 = (f32[256,128]{1,0:T(8,128)S(1)}, f32[256,128]{1,0:T(8,128)S(1)}, u32[]{:S(2)}, u32[]{:S(2)}) collective-permute-start(f32[256,128]{1,0:T(8,128)S(1)} %get-tuple-element.34), channel_id=1, source_target_pairs={{1,2},{3,4},{5,6},{7,8},{9,10},{11,12},{13,14},{15,16},{17,18},{19... | collective-permute-start | bytes 393224 | tf_op jit(solution)/shard_map/ppermute | solution.py:364
  8.2 5.5 %collective-permute-done.1.outer = f32[256,128]{1,0:T(8,128)S(1)} collective-permute-done((f32[256,128]{1,0:T(8,128)S(1)}, f32[256,128]{1,0:T(8,128)S(1)}, u32[]{:S(2)}, u32[]{:S(2)}) %collective-permute-start.1) | collective-permute-done | bytes 131104 | tf_op jit(solution)/shard_map/ppermute | solution.py:364
  18.8 3.8 %collective-permute-done.3.refs_2_ = f32[2,64,384]{2,1,0:T(8,128)S(1)} collective-permute-done((f32[2,64,384]{2,1,0:T(8,128)S(1)}, f32[2,64,384]{2,1,0:T(8,128)S(1)}, u32[]{:S(2)}, u32[]{:S(2)}) %collective-permute-start.3) | collective-permute-done | bytes 196640 | tf_op jit(solution)/shard_map/ppermute | solution.py:353
  23.3 7.5 %frame1.1 = (f32[1024,128]{1,0:T(8,128)}, f32[1024,128]{1,0:T(8,128)}, f32[264,256]{1,0:T(8,128)}, f32[264,256]{1,0:T(8,128)}, f32[2,384,384]{2,1,0:T(8,128)}) custom-call(f32[2,64,384]{2,1,0:T(8,128)} %copy-done.10, f32[2,256,384]{2,1,0:T(8,128)} %copy-done, f32[2,64,384]{2,1,0:T(8,128)} %copy-done.11, s32[1,1,1,2]{3,2,1,0:T(1,128)} %refs_3_.3, ...), custom_call_target="tpu_custom_call" | custom-call | tf_op jit(solution)/shard_map/frame1/pallas_call | solution.py:337
  30.9 2.1 %collective-permute-done.4 = f32[1024,128]{1,0:T(8,128)S(1)} collective-permute-done((f32[1024,128]{1,0:T(8,128)}, f32[1024,128]{1,0:T(8,128)S(1)}, u32[]{:S(2)}, u32[]{:S(2)}) %collective-permute-start.4) | collective-permute-done | bytes 524320 | tf_op jit(solution)/shard_map/ppermute | solution.py:357
  33.0 2.0 %add.6 = f32[1024,128]{1,0:T(8,128)} add(f32[1024,128]{1,0:T(8,128)} %get-tuple-element.38, f32[1024,128]{1,0:T(8,128)S(1)} %collective-permute-done.4) | non-fusion elementwise | flops 131072 | bytes 1572864 | tf_op jit(solution)/shard_map/add | solution.py:377
  35.0 11.2 %all-to-all-start = ((f32[16,64,128]{2,1,0:T(8,128)}), f32[16,64,128]{2,1,0:T(8,128)S(1)}, u32[]{:S(2)}, u32[]{:S(2)}) async-start(f32[16,64,128]{2,1,0:T(8,128)} %bitcast), calls=%async_computation | async-start | bytes 1048576 | tf_op jit(solution)/shard_map/all_to_all | solution.py:373
  46.3 4.1 %collective-permute-start.5 = (f32[264,256]{1,0:T(8,128)S(1)}, f32[264,256]{1,0:T(8,128)S(1)}, u32[]{:S(2)}, u32[]{:S(2)}) collective-permute-start(f32[264,256]{1,0:T(8,128)S(1)} %copy-done.16), channel_id=1, source_target_pairs={{0,32},{32,64},{64,96},{96,128},{128,160},{160,192},{192,224},{1,3... | collective-permute-start | bytes 811016 | tf_op jit(solution)/shard_map/ppermute | solution.py:353
  51.7 3.8 %collective-permute-done.5.ru = f32[264,256]{1,0:T(8,128)S(1)} collective-permute-done((f32[264,256]{1,0:T(8,128)S(1)}, f32[264,256]{1,0:T(8,128)S(1)}, u32[]{:S(2)}, u32[]{:S(2)}) %collective-permute-start.5) | collective-permute-done | bytes 270368 | tf_op jit(solution)/shard_map/ppermute | solution.py:353
  55.5 9.2 %collective-permute-done.6.rd = f32[264,256]{1,0:T(8,128)S(1)} collective-permute-done((f32[264,256]{1,0:T(8,128)S(1)}, f32[264,256]{1,0:T(8,128)S(1)}, u32[]{:S(2)}, u32[]{:S(2)}) %collective-permute-start.6) | collective-permute-done | bytes 270368 | tf_op jit(solution)/shard_map/ppermute | solution.py:353
  64.8 2.0 %bands.1 = (f32[512,128]{1,0:T(8,128)}, f32[2,384,128]{2,1,0:T(8,128)S(1)}, f32[2,384,128]{2,1,0:T(8,128)S(1)}, f32[2,384,128]{2,1,0:T(8,128)S(1)}) custom-call(f32[1024,128]{1,0:T(8,128)S(1)} %bitcast.12, f32[2,384,384]{2,1,0:T(8,128)S(1)} %copy-done.2, f32[264,256]{1,0:T(8,128)S(1)} %collective-permute-done.5.ru, f32[264,256]{1,0:T(8,128)S(1)} %collective-permute-done.6.rd), custom_call_target="tpu_custom_call" | custom-call | tf_op jit(solution)/shard_map/bands/pallas_call | solution.py:337
  67.6 8.2 %all-to-all-start.1 = ((f32[8,64,128]{2,1,0:T(8,128)}), f32[8,64,128]{2,1,0:T(8,128)S(1)}, u32[]{:S(2)}, u32[]{:S(2)}) async-start(f32[8,64,128]{2,1,0:T(8,128)} %bitcast.2), calls=%async_computation.1 | async-start | bytes 524288 | tf_op jit(solution)/shard_map/all_to_all | solution.py:373
  77.8 4.4 %collective-permute-start.8 = (f32[2,384,128]{2,1,0:T(8,128)S(1)}, f32[2,384,128]{2,1,0:T(8,128)S(1)}, u32[]{:S(2)}, u32[]{:S(2)}) collective-permute-start(f32[2,384,128]{2,1,0:T(8,128)S(1)} %get-tuple-element.45.refs_6_), channel_id=1, source_target_pairs={{1,2},{3,4},{5,6},{7,8},{9,10},{11,12},{13,14},{15,16},{17,18},{19... | collective-permute-start | bytes 1179656 | tf_op jit(solution)/shard_map/ppermute | solution.py:364
  82.2 11.9 %collective-permute-done.8.refs_8_ = f32[2,384,128]{2,1,0:T(8,128)S(1)} collective-permute-done((f32[2,384,128]{2,1,0:T(8,128)S(1)}, f32[2,384,128]{2,1,0:T(8,128)S(1)}, u32[]{:S(2)}, u32[]{:S(2)}) %collective-permute-start.8) | collective-permute-done | bytes 393248 | tf_op jit(solution)/shard_map/ppermute | solution.py:364
  94.2 15.1 %all_to_all.68 = f32[16,64,128]{2,1,0:T(8,128)S(1)} all-to-all(f32[16,64,128]{2,1,0:T(8,128)S(1)} %bitcast.16), channel_id=1, replica_groups={{0,8,16,24,64,72,80,88,128,136,144,152,192,200,208,216},{1,9,17,25,65,7..., dimensions={0} | all-to-all | bytes 1048576 | tf_op jit(solution)/shard_map/all_to_all | solution.py:373
  109.3 2.7 %collective-permute-start.9 = (f32[1024,128]{1,0:T(8,128)S(1)}, f32[1024,128]{1,0:T(8,128)S(1)}, u32[]{:S(2)}, u32[]{:S(2)}) collective-permute-start(f32[1024,128]{1,0:T(8,128)S(1)} %bitcast.20), channel_id=1, source_target_pairs={{0,1},{1,0},{2,3},{3,2},{4,5},{5,4},{6,7},{7,6},{8,9},{9,8},{10,11... | collective-permute-start | bytes 1572872 | tf_op jit(solution)/shard_map/ppermute | solution.py:357
  114.3 8.4 %frame2.1 = (f32[1024,128]{1,0:T(8,128)}, f32[1024,128]{1,0:T(8,128)}, f32[136,256]{1,0:T(8,128)}, f32[136,256]{1,0:T(8,128)}, f32[2,256,384]{2,1,0:T(8,128)}, /...) custom-call(f32[2,64,384]{2,1,0:T(8,128)} %copy-done.10, f32[2,256,384]{2,1,0:T(8,128)} %copy-done, ...), custom_call_target="tpu_custom_call" | custom-call | tf_op jit(solution)/shard_map/frame2/pallas_call | solution.py:337
  127.1 3.6 %all-to-all-start.3 = ((f32[16,64,128]{2,1,0:T(8,128)}), f32[16,64,128]{2,1,0:T(8,128)S(1)}, u32[]{:S(2)}, u32[]{:S(2)}) async-start(f32[16,64,128]{2,1,0:T(8,128)} %bitcast.6), calls=%async_computation.3 | async-start | bytes 1048576 | tf_op jit(solution)/shard_map/all_to_all | solution.py:373
  135.0 7.4 %collective-permute-done.12.rd = f32[136,256]{1,0:T(8,128)S(1)} collective-permute-done((f32[136,256]{1,0:T(8,128)S(1)}, f32[136,256]{1,0:T(8,128)S(1)}, u32[]{:S(2)}, u32[]{:S(2)}) %collective-permute-start.12) | collective-permute-done | bytes 139296 | tf_op jit(solution)/shard_map/ppermute | solution.py:353
  144.1 5.1 %all-to-all-start.4 = ((f32[8,64,128]{2,1,0:T(8,128)}), f32[8,64,128]{2,1,0:T(8,128)S(1)}, u32[]{:S(2)}, u32[]{:S(2)}) async-start(f32[8,64,128]{2,1,0:T(8,128)} %bitcast.8), calls=%async_computation.4 | async-start | bytes 524288 | tf_op jit(solution)/shard_map/all_to_all | solution.py:373
  150.9 4.4 %collective-permute-start.14 = (f32[256,128]{1,0:T(8,128)S(1)}, f32[256,128]{1,0:T(8,128)S(1)}, u32[]{:S(2)}, u32[]{:S(2)}) collective-permute-start(f32[256,128]{1,0:T(8,128)S(1)} %get-tuple-element.60), channel_id=1, source_target_pairs={{1,2},{3,4},{5,6},{7,8},{9,10},{11,12},{13,14},{15,16},{17,18},{19... | collective-permute-start | bytes 393224 | tf_op jit(solution)/shard_map/ppermute | solution.py:364
  155.4 6.2 %collective-permute-done.14.far = f32[256,128]{1,0:T(8,128)S(1)} collective-permute-done((f32[256,128]{1,0:T(8,128)S(1)}, f32[256,128]{1,0:T(8,128)S(1)}, u32[]{:S(2)}, u32[]{:S(2)}) %collective-permute-start.14) | collective-permute-done | bytes 131104 | tf_op jit(solution)/shard_map/ppermute | solution.py:364
  161.6 16.9 %all_to_all.69 = f32[16,64,128]{2,1,0:T(8,128)S(1)} all-to-all(f32[16,64,128]{2,1,0:T(8,128)S(1)} %bitcast.17), channel_id=1, replica_groups={{0,8,16,24,64,72,80,88,128,136,144,152,192,200,208,216},{1,9,17,25,65,7..., dimensions={0} | all-to-all | bytes 1048576 | tf_op jit(solution)/shard_map/all_to_all | solution.py:373
  (67 shorter events, 30.8 us)
Async XLA Ops:
  1.8 6.4 %collective-permute-start = (f32[256,128]{1,0:T(8,128)S(1)}, f32[256,128]{1,0:T(8,128)S(1)}, u32[]{:S(2)}, u32[]{:S(2)}) collective-permute-start(f32[256,128]{1,0:T(8,128)S(1)} %get-tuple-element.33), channel_id=1, source_target_pairs={{0,1},{1,0},{2,3},{3,2},{4,5},{5,4},{6,7},{7,6},{8,9},{9,8},{10,11... | collective-permute-start | bytes 393224 | tf_op jit(solution)/shard_map/ppermute | solution.py:357
  5.1 8.6 %collective-permute-start.1 = (f32[256,128]{1,0:T(8,128)S(1)}, f32[256,128]{1,0:T(8,128)S(1)}, u32[]{:S(2)}, u32[]{:S(2)}) collective-permute-start(f32[256,128]{1,0:T(8,128)S(1)} %get-tuple-element.34), channel_id=1, source_target_pairs={{1,2},{3,4},{5,6},{7,8},{9,10},{11,12},{13,14},{15,16},{17,18},{19... | collective-permute-start | bytes 393224 | tf_op jit(solution)/shard_map/ppermute | solution.py:364
  14.9 3.9 %collective-permute-start.2 = (f32[2,64,384]{2,1,0:T(8,128)S(1)}, f32[2,64,384]{2,1,0:T(8,128)S(1)}, u32[]{:S(2)}, u32[]{:S(2)}) collective-permute-start(f32[2,64,384]{2,1,0:T(8,128)S(1)} %get-tuple-element.35), channel_id=1, source_target_pairs={{0,32},{32,64},{64,96},{96,128},{128,160},{160,192},{192,224},{1,3... | collective-permute-start | bytes 589832 | tf_op jit(solution)/shard_map/ppermute | solution.py:353
  16.2 6.4 %collective-permute-start.3 = (f32[2,64,384]{2,1,0:T(8,128)S(1)}, f32[2,64,384]{2,1,0:T(8,128)S(1)}, u32[]{:S(2)}, u32[]{:S(2)}) collective-permute-start(f32[2,64,384]{2,1,0:T(8,128)S(1)} %get-tuple-element.37), channel_id=1, source_target_pairs={{32,0},{64,32},{96,64},{128,96},{160,128},{192,160},{224,192},{33,... | collective-permute-start | bytes 589832 | tf_op jit(solution)/shard_map/ppermute | solution.py:353
  30.8 2.2 %collective-permute-start.4 = (f32[1024,128]{1,0:T(8,128)}, f32[1024,128]{1,0:T(8,128)S(1)}, u32[]{:S(2)}, u32[]{:S(2)}) collective-permute-start(f32[1024,128]{1,0:T(8,128)} %get-tuple-element.39), channel_id=1, source_target_pairs={{0,1},{1,0},{2,3},{3,2},{4,5},{5,4},{6,7},{7,6},{8,9},{9,8},{10,11... | collective-permute-start | bytes 1572872 | tf_op jit(solution)/shard_map/ppermute | solution.py:357
  35.0 29.7 %all-to-all-start = ((f32[16,64,128]{2,1,0:T(8,128)}), f32[16,64,128]{2,1,0:T(8,128)S(1)}, u32[]{:S(2)}, u32[]{:S(2)}) async-start(f32[16,64,128]{2,1,0:T(8,128)} %bitcast), calls=%async_computation | async-start | bytes 1048576 | tf_op jit(solution)/shard_map/all_to_all | solution.py:373
  46.3 9.3 %collective-permute-start.5 = (f32[264,256]{1,0:T(8,128)S(1)}, f32[264,256]{1,0:T(8,128)S(1)}, u32[]{:S(2)}, u32[]{:S(2)}) collective-permute-start(f32[264,256]{1,0:T(8,128)S(1)} %copy-done.16), channel_id=1, source_target_pairs={{0,32},{32,64},{64,96},{96,128},{128,160},{160,192},{192,224},{1,3... | collective-permute-start | bytes 811016 | tf_op jit(solution)/shard_map/ppermute | solution.py:353
  50.4 14.4 %collective-permute-start.6 = (f32[264,256]{1,0:T(8,128)S(1)}, f32[264,256]{1,0:T(8,128)S(1)}, u32[]{:S(2)}, u32[]{:S(2)}) collective-permute-start(f32[264,256]{1,0:T(8,128)S(1)} %copy-done.15), channel_id=1, source_target_pairs={{32,0},{64,32},{96,64},{128,96},{160,128},{192,160},{224,192},{33,... | collective-permute-start | bytes 811016 | tf_op jit(solution)/shard_map/ppermute | solution.py:353
  67.6 41.7 %copy-start.6 = (f32[2,384,128]{2,1,0:T(8,128)}, f32[2,384,128]{2,1,0:T(8,128)S(1)}, u32[]{:S(2)}) copy-start(f32[2,384,128]{2,1,0:T(8,128)S(1)} %get-tuple-element.43.refs_4_) | copy-start | bytes 1179652
  67.6 41.7 %copy-start.8 = (f32[2,384,128]{2,1,0:T(8,128)}, f32[2,384,128]{2,1,0:T(8,128)S(1)}, u32[]{:S(2)}) copy-start(f32[2,384,128]{2,1,0:T(8,128)S(1)} %get-tuple-element.45.refs_6_) | copy-start | bytes 1179652
  67.6 26.5 %all-to-all-start.1 = ((f32[8,64,128]{2,1,0:T(8,128)}), f32[8,64,128]{2,1,0:T(8,128)S(1)}, u32[]{:S(2)}, u32[]{:S(2)}) async-start(f32[8,64,128]{2,1,0:T(8,128)} %bitcast.2), calls=%async_computation.1 | async-start | bytes 524288 | tf_op jit(solution)/shard_map/all_to_all | solution.py:373
  75.8 6.4 %collective-permute-start.7 = (f32[2,384,128]{2,1,0:T(8,128)S(1)}, f32[2,384,128]{2,1,0:T(8,128)S(1)}, u32[]{:S(2)}, u32[]{:S(2)}) collective-permute-start(f32[2,384,128]{2,1,0:T(8,128)S(1)} %get-tuple-element.43.refs_4_), channel_id=1, source_target_pairs={{0,1},{1,0},{2,3},{3,2},{4,5},{5,4},{6,7},{7,6},{8,9},{9,8},{10,11... | collective-permute-start | bytes 1179656 | tf_op jit(solution)/shard_map/ppermute | solution.py:357
  77.8 16.3 %collective-permute-start.8 = (f32[2,384,128]{2,1,0:T(8,128)S(1)}, f32[2,384,128]{2,1,0:T(8,128)S(1)}, u32[]{:S(2)}, u32[]{:S(2)}) collective-permute-start(f32[2,384,128]{2,1,0:T(8,128)S(1)} %get-tuple-element.45.refs_6_), channel_id=1, source_target_pairs={{1,2},{3,4},{5,6},{7,8},{9,10},{11,12},{13,14},{15,16},{17,18},{19... | collective-permute-start | bytes 1179656 | tf_op jit(solution)/shard_map/ppermute | solution.py:364
  109.3 4.2 %collective-permute-start.9 = (f32[1024,128]{1,0:T(8,128)S(1)}, f32[1024,128]{1,0:T(8,128)S(1)}, u32[]{:S(2)}, u32[]{:S(2)}) collective-permute-start(f32[1024,128]{1,0:T(8,128)S(1)} %bitcast.20), channel_id=1, source_target_pairs={{0,1},{1,0},{2,3},{3,2},{4,5},{5,4},{6,7},{7,6},{8,9},{9,8},{10,11... | collective-permute-start | bytes 1572872 | tf_op jit(solution)/shard_map/ppermute | solution.py:357
  122.7 2.4 %collective-permute-start.10 = (f32[1024,128]{1,0:T(8,128)}, f32[1024,128]{1,0:T(8,128)S(1)}, u32[]{:S(2)}, u32[]{:S(2)}) collective-permute-start(f32[1024,128]{1,0:T(8,128)} %get-tuple-element.52), channel_id=1, source_target_pairs={{0,1},{1,0},{2,3},{3,2},{4,5},{5,4},{6,7},{7,6},{8,9},{9,8},{10,11... | collective-permute-start | bytes 1572872 | tf_op jit(solution)/shard_map/ppermute | solution.py:357
  127.1 15.3 %all-to-all-start.3 = ((f32[16,64,128]{2,1,0:T(8,128)}), f32[16,64,128]{2,1,0:T(8,128)S(1)}, u32[]{:S(2)}, u32[]{:S(2)}) async-start(f32[16,64,128]{2,1,0:T(8,128)} %bitcast.6), calls=%async_computation.3 | async-start | bytes 1048576 | tf_op jit(solution)/shard_map/all_to_all | solution.py:373
  130.7 4.3 %collective-permute-start.11 = (f32[136,256]{1,0:T(8,128)S(1)}, f32[136,256]{1,0:T(8,128)S(1)}, u32[]{:S(2)}, u32[]{:S(2)}) collective-permute-start(f32[136,256]{1,0:T(8,128)S(1)} %copy-done.18), channel_id=1, source_target_pairs={{0,32},{32,64},{64,96},{96,128},{128,160},{160,192},{192,224},{1,3... | collective-permute-start | bytes 417800 | tf_op jit(solution)/shard_map/ppermute | solution.py:353
  132.1 10.4 %collective-permute-start.12 = (f32[136,256]{1,0:T(8,128)S(1)}, f32[136,256]{1,0:T(8,128)S(1)}, u32[]{:S(2)}, u32[]{:S(2)}) collective-permute-start(f32[136,256]{1,0:T(8,128)S(1)} %copy-done.17), channel_id=1, source_target_pairs={{32,0},{64,32},{96,64},{128,96},{160,128},{192,160},{224,192},{33,... | collective-permute-start | bytes 417800 | tf_op jit(solution)/shard_map/ppermute | solution.py:353
  144.1 37.9 %copy-start.3 = (f32[2,2,256,256]{3,2,1,0:T(8,128)S(1)}, f32[2,2,256,256]{3,2,1,0:T(8,128)}, u32[]{:S(2)}) copy-start(f32[2,2,256,256]{3,2,1,0:T(8,128)} %get-tuple-element.57.probe) | copy-start | bytes 3145732
  144.1 37.9 %copy-start.5 = (f32[2,256,384]{2,1,0:T(8,128)S(1)}, f32[2,256,384]{2,1,0:T(8,128)}, u32[]{:S(2)}) copy-start(f32[2,256,384]{2,1,0:T(8,128)} %get-tuple-element.50.obj) | copy-start | bytes 2359300
  144.1 17.4 %all-to-all-start.4 = ((f32[8,64,128]{2,1,0:T(8,128)}), f32[8,64,128]{2,1,0:T(8,128)S(1)}, u32[]{:S(2)}, u32[]{:S(2)}) async-start(f32[8,64,128]{2,1,0:T(8,128)} %bitcast.8), calls=%async_computation.4 | async-start | bytes 524288 | tf_op jit(solution)/shard_map/all_to_all | solution.py:373
  149.2 6.2 %collective-permute-start.13 = (f32[256,128]{1,0:T(8,128)S(1)}, f32[256,128]{1,0:T(8,128)S(1)}, u32[]{:S(2)}, u32[]{:S(2)}) collective-permute-start(f32[256,128]{1,0:T(8,128)S(1)} %get-tuple-element.59), channel_id=1, source_target_pairs={{0,1},{1,0},{2,3},{3,2},{4,5},{5,4},{6,7},{7,6},{8,9},{9,8},{10,11... | collective-permute-start | bytes 393224 | tf_op jit(solution)/shard_map/ppermute | solution.py:357
  150.9 10.6 %collective-permute-start.14 = (f32[256,128]{1,0:T(8,128)S(1)}, f32[256,128]{1,0:T(8,128)S(1)}, u32[]{:S(2)}, u32[]{:S(2)}) collective-permute-start(f32[256,128]{1,0:T(8,128)S(1)} %get-tuple-element.60), channel_id=1, source_target_pairs={{1,2},{3,4},{5,6},{7,8},{9,10},{11,12},{13,14},{15,16},{17,18},{19... | collective-permute-start | bytes 393224 | tf_op jit(solution)/shard_map/ppermute | solution.py:364
  178.6 3.5 %collective-permute-start.15 = (f32[1024,128]{1,0:T(8,128)S(1)}, f32[1024,128]{1,0:T(8,128)S(1)}, u32[]{:S(2)}, u32[]{:S(2)}) collective-permute-start(f32[1024,128]{1,0:T(8,128)S(1)} %bitcast.14), channel_id=1, source_target_pairs={{0,1},{1,0},{2,3},{3,2},{4,5},{5,4},{6,7},{7,6},{8,9},{9,8},{10,11... | collective-permute-start | bytes 1572872 | tf_op jit(solution)/shard_map/ppermute | solution.py:357
  (15 other events, 155.2 us)

commit v7 on v4

--- a/solution.py
+++ b/solution.py
@@ -252,19 +252,19 @@
         out[q // 2, q % 2] = probe[q // 2, q % 2] - coeff * total
 
 
-def chunk_sum(parts, out):
-    rows = out.shape[0]
-    total = parts[:rows, :]
-    for k in range(1, parts.shape[0] // rows):
-        total = total + parts[k * rows:(k + 1) * rows, :]
-    out[...] = total
-
-
-def bands_kernel(parts, own, ru, rd, total, ci, cm, co, ti, tm, to, outs, *inner):
+def spread(parts, out):
+    a, b, c, d = parts
+    total = (a[...] + b[...]) + (c[...] + d[...])
+    rows = a.shape[0]
+    for k in range(out.shape[0] // rows):
+        out[k * rows:(k + 1) * rows, :] = total
+
+
+def bands_kernel(p0, p1, p2, p3, own, ru, rd, total, ci, cm, co, ti, tm, to, outs, *inner):
     *inner, sems = inner
     wait = fetch((own, ru, rd), inner, sems)
     own, ru, rd = inner
-    chunk_sum(parts, total)
+    spread((p0, p1, p2, p3), total)
     wait(*range(3))
     for c in range(2):
         rows = jnp.concatenate(
@@ -275,11 +275,11 @@
     finish(store(zip((ti, to, tm), (ci, co, cm)), outs))
 
 
-def last_bands_kernel(parts, own, ru, rd, total, grad_out, near, far, grad, outs, *inner):
+def last_bands_kernel(p0, p1, p2, p3, own, ru, rd, total, grad_out, near, far, grad, outs, *inner):
     *inner, sems = inner
     wait = fetch((own, ru, rd), inner, sems)
     own, ru, rd = inner
-    chunk_sum(parts, total)
+    spread((p0, p1, p2, p3), total)
     low = lanes()
     wait(*range(3))
     for c in range(2):
@@ -292,13 +292,6 @@
     near[...] = choose(right, left)
     far[...] = choose(left, right)
     finish(copies)
-
-
-def spread_kernel(a, b, c, d, out):
-    total = (a[...] + b[...]) + (c[...] + d[...])
-    rows = a.shape[0]
-    for k in range(out.shape[0] // rows):
-        out[k * rows:(k + 1) * rows, :] = total
 
 
 def last_kernel(obj, grad, probe, near, far, mine, other, out, out_probe, *inner):
@@ -375,14 +368,14 @@
 
 def scatter(keep, send):
     x = keep + exchange(send, BIT_CORE)
-    return lax.all_to_all(x, RC, 0, 0, axis_index_groups=groups(WIDE), tiled=True)
+    x = lax.all_to_all(x, RC, 0, 0, axis_index_groups=groups(WIDE), tiled=True)
+    x = x.reshape(COUNT, CHUNK, LANE).sum(axis=0)
+    return x, exchange(x, 2), exchange(x, 4), exchange(x, 6)
 
 
 def gather(x, *early):
-    parts = (x, exchange(x, 2), exchange(x, 4), exchange(x, 6))
-    parts, early = lax.optimization_barrier((parts, early))
-    (x,) = call(spread_kernel, [(1024, LANE)], "spread")(*parts)
     x = lax.all_to_all(x, RC, 0, 0, axis_index_groups=groups(WIDE), tiled=True)
+    x, early = lax.optimization_barrier((x, early))
     return x, exchange(x, BIT_CORE), *early
 
 
@@ -411,12 +404,12 @@
     rd = shift(su, "row", -1)
     total, ci, cm, co = call(
         bands_kernel,
-        [(CHUNK, LANE)] + [(2, SPAN, B)] * 3,
+        [(1024, LANE)] + [(2, SPAN, B)] * 3,
         "bands",
-        specs=[VM] + [HBM] * 3,
+        specs=[VM] * 4 + [HBM] * 3,
         places=[VM] + [HBM] * 3,
         scratch=[pltpu.VMEM((2, SPAN, B), f32)] * 3 + [pltpu.SemaphoreType.DMA((3,))],
-    )(scatter(keep, send), own, ru, rd)
+    )(*scatter(keep, send), own, ru, rd)
     mine, other, di, do = gather(total, *columns(ci, co))
 
     keep, send, su, sd, own, obj, probe = call(
@@ -432,12 +425,12 @@
     rd = shift(su, "row", -1)
     total, grad, near, far = call(
         last_bands_kernel,
-        [(CHUNK, LANE), (2, TILE, SPAN)] + [(TILE, LANE)] * 2,
+        [(1024, LANE), (2, TILE, SPAN)] + [(TILE, LANE)] * 2,
         "last_bands",
-        specs=[VM] + [HBM] * 3,
+        specs=[VM] * 4 + [HBM] * 3,
         places=[VM, HBM, VM, VM],
         scratch=[pltpu.VMEM((2, TILE, SPAN), f32), pltpu.SemaphoreType.DMA((1,))],
-    )(scatter(keep, send), own, ru, rd)
+    )(*scatter(keep, send), own, ru, rd)
     mine, other, near, far = gather(total, *columns(near, far))
     return tuple(
         call(

time: 179 us -> 169 us (0.944)
  blocking collectives: 35.5 us -> 0 us
  starting transfers between devices: 64.4 us -> 84.9 us
  local copies, waits for them, and re-layouts: 3.41 us -> 6.19 us
    all_to_all x2 -> x0, blocking collectives: 35.5 us -> none  [gather(): x = lax.all_to_all(x, RC, 0, 0, axis_index_groups=groups(WIDE), tiled=True)]
    ppermute x6, waiting for transfers between devices: 28.1 us -> 6.73 us  [shift(): return lax.ppermute(x, axis, pairs)]
    all_to_all x2 -> x4, starting transfers between devices: 17.7 us -> 37.7 us  [the longest x2 23.4 us: scatter(): x = lax.all_to_all(x, RC, 0, 0, axis_index_groups=groups(WIDE), tiled=True)]
    ppermute x3, waiting for transfers between devices: 5.76 us -> 19.4 us  [columns(): return (exchange(near, BIT_CORE), lax.ppermute(far, 'col', pairs))]
    all_to_all x2 -> x4, waiting for transfers between devices: 0.01 us -> 11.4 us  [the longest x2 11.4 us: scatter(): x = lax.all_to_all(x, RC, 0, 0, axis_index_groups=groups(WIDE), tiled=True)]
    ppermute x13, waiting for transfers between devices: 15.5 us -> 12.2 us  [exchange(): return lax.ppermute(x, RC, [(i, i ^ mask) for i in range(256)])]
    unnamed x38 -> x42, local copies, waits for them, and re-layouts: 3.41 us -> 6.19 us
    pallas_call x9 -> x7, Pallas kernels: 20.6 us -> 22 us  [run(): pl.pallas_call(kernel, out_shape=[jax.ShapeDtypeStruct(s, f32) for s in o...]
  transfers between devices with their start and end apart: 24 -> 26, of which waited for: 16 -> 15; matrix products, arithmetic and copies ran while one was open for 0% -> 0% of each run, Pallas kernels for 0% -> 0%
where the time goes in v7:
time: 169 us; the launch traced here: 168 us
  starting transfers between devices  84.9 us (50%)
  waiting for transfers between devices  49.8 us (29%)
  Pallas kernels  22 us (13%)
  local copies, waits for them, and re-layouts  6.19 us (4%)
  other arithmetic  3.97 us (2%)
    ppermute x13, starting transfers between devices, exchange(): return lax.ppermute(x, RC, [(i, i ^ mask) for i in range(256)])  24.9 us
    all_to_all x2, starting transfers between devices, scatter(): x = lax.all_to_all(x, RC, 0, 0, axis_index_groups=groups(WIDE), tiled=True)  23.4 us
    pallas_call x7, Pallas kernels, run(): pl.pallas_call(kernel, out_shape=[jax.ShapeDtypeStruct(s, f32) for s in o...  22 us
    ppermute x3, waiting for transfers between devices, columns(): return (exchange(near, BIT_CORE), lax.ppermute(far, 'col', pairs))  19.4 us
    all_to_all x2, starting transfers between devices, gather(): x = lax.all_to_all(x, RC, 0, 0, axis_index_groups=groups(WIDE), tiled=True)  14.3 us
    ppermute x13, waiting for transfers between devices, exchange(): return lax.ppermute(x, RC, [(i, i ^ mask) for i in range(256)])  12.2 us
    ppermute x6, starting transfers between devices, shift(): return lax.ppermute(x, axis, pairs)  11.5 us
    all_to_all x2, waiting for transfers between devices, scatter(): x = lax.all_to_all(x, RC, 0, 0, axis_index_groups=groups(WIDE), tiled=True)  11.4 us
  transfers between devices with their start and end apart: 26, of which 15 were waited for; matrix products, arithmetic and copies ran while one was open for 0% of the time, Pallas kernels for 0%

profile of v7, /device:TPU:1, one launch (start us, length us, event | category | flops | bytes accessed | tf_op | source)
XLA Modules:
  0.0 168.0 jit_solution(1174612045347324705)
XLA Ops:
  1.8 3.3 %collective-permute-start = (f32[256,128]{1,0:T(8,128)S(1)}, f32[256,128]{1,0:T(8,128)S(1)}, u32[]{:S(2)}, u32[]{:S(2)}) collective-permute-start(f32[256,128]{1,0:T(8,128)S(1)} %get-tuple-element.33), channel_id=1, source_target_pairs={{0,1},{1,0},{2,3},{3,2},{4,5},{5,4},{6,7},{7,6},{8,9},{9,8},{10,11... | collective-permute-start | bytes 393224 | tf_op jit(solution)/shard_map/ppermute | solution.py:349
  5.1 3.1 %collective-permute-start.1 = (f32[256,128]{1,0:T(8,128)S(1)}, f32[256,128]{1,0:T(8,128)S(1)}, u32[]{:S(2)}, u32[]{:S(2)}) collective-permute-start(f32[256,128]{1,0:T(8,128)S(1)} %get-tuple-element.34), channel_id=1, source_target_pairs={{1,2},{3,4},{5,6},{7,8},{9,10},{11,12},{13,14},{15,16},{17,18},{19... | collective-permute-start | bytes 393224 | tf_op jit(solution)/shard_map/ppermute | solution.py:356
  8.2 5.5 %collective-permute-done.1.outer = f32[256,128]{1,0:T(8,128)S(1)} collective-permute-done((f32[256,128]{1,0:T(8,128)S(1)}, f32[256,128]{1,0:T(8,128)S(1)}, u32[]{:S(2)}, u32[]{:S(2)}) %collective-permute-start.1) | collective-permute-done | bytes 131104 | tf_op jit(solution)/shard_map/ppermute | solution.py:356
  18.8 3.8 %collective-permute-done.3.refs_2_ = f32[2,64,384]{2,1,0:T(8,128)S(1)} collective-permute-done((f32[2,64,384]{2,1,0:T(8,128)S(1)}, f32[2,64,384]{2,1,0:T(8,128)S(1)}, u32[]{:S(2)}, u32[]{:S(2)}) %collective-permute-start.3) | collective-permute-done | bytes 196640 | tf_op jit(solution)/shard_map/ppermute | solution.py:345
  23.3 7.5 %frame1.1 = (f32[1024,128]{1,0:T(8,128)}, f32[1024,128]{1,0:T(8,128)}, f32[264,256]{1,0:T(8,128)}, f32[264,256]{1,0:T(8,128)}, f32[2,384,384]{2,1,0:T(8,128)}) custom-call(f32[2,64,384]{2,1,0:T(8,128)} %copy-done.12, f32[2,256,384]{2,1,0:T(8,128)} %copy-done, f32[2,64,384]{2,1,0:T(8,128)} %copy-done.13, s32[1,1,1,2]{3,2,1,0:T(1,128)} %refs_3_.3, ...), custom_call_target="tpu_custom_call" | custom-call | tf_op jit(solution)/shard_map/frame1/pallas_call | solution.py:329
  34.9 13.5 %all-to-all-start = ((f32[32,32,128]{2,1,0:T(8,128)}), f32[32,32,128]{2,1,0:T(8,128)S(1)}, u32[]{:S(2)}, u32[]{:S(2)}) async-start(f32[32,32,128]{2,1,0:T(8,128)} %bitcast), calls=%async_computation | async-start | bytes 1048576 | tf_op jit(solution)/shard_map/all_to_all | solution.py:371
  48.5 3.2 %collective-permute-start.8 = (f32[264,256]{1,0:T(8,128)S(1)}, f32[264,256]{1,0:T(8,128)S(1)}, u32[]{:S(2)}, u32[]{:S(2)}) collective-permute-start(f32[264,256]{1,0:T(8,128)S(1)} %copy-done.18), channel_id=1, source_target_pairs={{0,32},{32,64},{64,96},{96,128},{128,160},{160,192},{192,224},{1,3... | collective-permute-start | bytes 811016 | tf_op jit(solution)/shard_map/ppermute | solution.py:345
  53.0 5.7 %all-to-all-done = f32[32,32,128]{2,1,0:T(8,128)S(1)} async-done(((f32[32,32,128]{2,1,0:T(8,128)}), f32[32,32,128]{2,1,0:T(8,128)S(1)}, u32[]{:S(2)}, u32[]{:S(2)}) %all-to-all-start) | async-done | bytes 524320 | tf_op jit(solution)/shard_map/all_to_all | solution.py:371
  58.7 4.9 %collective-permute-start.7 = (f32[32,128]{1,0:T(8,128)S(1)}, f32[32,128]{1,0:T(8,128)S(1)}, u32[]{:S(2)}, u32[]{:S(2)}) collective-permute-start(f32[32,128]{1,0:T(8,128)S(1)} %reduce_sum.18.p0), channel_id=1, source_target_pairs={{0,6},{1,7},{2,4},{3,5},{4,2},{5,3},{6,0},{7,1},{8,14},{9,15},{10,... | collective-permute-start | bytes 49160 | tf_op jit(solution)/shard_map/ppermute | solution.py:349
  67.4 2.7 %collective-permute-done.6.p2 = f32[32,128]{1,0:T(8,128)S(1)} collective-permute-done((f32[32,128]{1,0:T(8,128)S(1)}, f32[32,128]{1,0:T(8,128)S(1)}, u32[]{:S(2)}, u32[]{:S(2)}) %collective-permute-start.6) | collective-permute-done | bytes 16416 | tf_op jit(solution)/shard_map/ppermute | solution.py:349
  73.0 9.3 %all-to-all-start.1 = ((f32[32,32,128]{2,1,0:T(8,128)}), f32[32,32,128]{2,1,0:T(8,128)S(1)}, u32[]{:S(2)}, u32[]{:S(2)}) async-start(f32[32,32,128]{2,1,0:T(8,128)} %bitcast.1), calls=%async_computation.1 | async-start | bytes 1048576 | tf_op jit(solution)/shard_map/all_to_all | solution.py:377
  82.3 2.4 %collective-permute-start.10 = (f32[2,384,128]{2,1,0:T(8,128)S(1)}, f32[2,384,128]{2,1,0:T(8,128)S(1)}, u32[]{:S(2)}, u32[]{:S(2)}) collective-permute-start(f32[2,384,128]{2,1,0:T(8,128)S(1)} %get-tuple-element.43.refs_4_), channel_id=1, source_target_pairs={{0,1},{1,0},{2,3},{3,2},{4,5},{5,4},{6,7},{7,6},{8,9},{9,8},{10,11... | collective-permute-start | bytes 1179656 | tf_op jit(solution)/shard_map/ppermute | solution.py:349
  84.7 3.6 %collective-permute-start.11 = (f32[2,384,128]{2,1,0:T(8,128)S(1)}, f32[2,384,128]{2,1,0:T(8,128)S(1)}, u32[]{:S(2)}, u32[]{:S(2)}) collective-permute-start(f32[2,384,128]{2,1,0:T(8,128)S(1)} %get-tuple-element.45.refs_6_), channel_id=1, source_target_pairs={{1,2},{3,4},{5,6},{7,8},{9,10},{11,12},{13,14},{15,16},{17,18},{19... | collective-permute-start | bytes 1179656 | tf_op jit(solution)/shard_map/ppermute | solution.py:356
  88.3 10.6 %collective-permute-done.11.refs_8_ = f32[2,384,128]{2,1,0:T(8,128)S(1)} collective-permute-done((f32[2,384,128]{2,1,0:T(8,128)S(1)}, f32[2,384,128]{2,1,0:T(8,128)S(1)}, u32[]{:S(2)}, u32[]{:S(2)}) %collective-permute-start.11) | collective-permute-done | bytes 393248 | tf_op jit(solution)/shard_map/ppermute | solution.py:356
  101.9 8.4 %frame2.1 = (f32[1024,128]{1,0:T(8,128)}, f32[1024,128]{1,0:T(8,128)}, f32[136,256]{1,0:T(8,128)}, f32[136,256]{1,0:T(8,128)}, f32[2,256,384]{2,1,0:T(8,128)}, /...) custom-call(f32[2,64,384]{2,1,0:T(8,128)} %copy-done.12, f32[2,256,384]{2,1,0:T(8,128)} %copy-done, ...), custom_call_target="tpu_custom_call" | custom-call | tf_op jit(solution)/shard_map/frame2/pallas_call | solution.py:329
  114.4 9.9 %all-to-all-start.2 = ((f32[32,32,128]{2,1,0:T(8,128)}), f32[32,32,128]{2,1,0:T(8,128)S(1)}, u32[]{:S(2)}, u32[]{:S(2)}) async-start(f32[32,32,128]{2,1,0:T(8,128)} %bitcast.3), calls=%async_computation.2 | async-start | bytes 1048576 | tf_op jit(solution)/shard_map/all_to_all | solution.py:371
  124.3 3.1 %collective-permute-start.17 = (f32[136,256]{1,0:T(8,128)S(1)}, f32[136,256]{1,0:T(8,128)S(1)}, u32[]{:S(2)}, u32[]{:S(2)}) collective-permute-start(f32[136,256]{1,0:T(8,128)S(1)} %copy-done.20), channel_id=1, source_target_pairs={{0,32},{32,64},{64,96},{96,128},{128,160},{160,192},{192,224},{1,3... | collective-permute-start | bytes 417800 | tf_op jit(solution)/shard_map/ppermute | solution.py:345
  128.8 5.7 %all-to-all-done.2 = f32[32,32,128]{2,1,0:T(8,128)S(1)} async-done(((f32[32,32,128]{2,1,0:T(8,128)}), f32[32,32,128]{2,1,0:T(8,128)S(1)}, u32[]{:S(2)}, u32[]{:S(2)}) %all-to-all-start.2) | async-done | bytes 524320 | tf_op jit(solution)/shard_map/all_to_all | solution.py:371
  135.6 2.9 %collective-permute-start.15 = (f32[32,128]{1,0:T(8,128)S(1)}, f32[32,128]{1,0:T(8,128)S(1)}, u32[]{:S(2)}, u32[]{:S(2)}) collective-permute-start(f32[32,128]{1,0:T(8,128)S(1)} %reduce_sum.19.p0), channel_id=1, source_target_pairs={{0,4},{1,5},{2,6},{3,7},{4,0},{5,1},{6,2},{7,3},{8,12},{9,13},{10,... | collective-permute-start | bytes 49160 | tf_op jit(solution)/shard_map/ppermute | solution.py:349
  145.0 5.0 %all-to-all-start.3 = ((f32[32,32,128]{2,1,0:T(8,128)}), f32[32,32,128]{2,1,0:T(8,128)S(1)}, u32[]{:S(2)}, u32[]{:S(2)}) async-start(f32[32,32,128]{2,1,0:T(8,128)} %bitcast.4), calls=%async_computation.3 | async-start | bytes 1048576 | tf_op jit(solution)/shard_map/all_to_all | solution.py:377
  150.0 3.4 %collective-permute-start.19 = (f32[256,128]{1,0:T(8,128)S(1)}, f32[256,128]{1,0:T(8,128)S(1)}, u32[]{:S(2)}, u32[]{:S(2)}) collective-permute-start(f32[256,128]{1,0:T(8,128)S(1)} %get-tuple-element.59), channel_id=1, source_target_pairs={{0,1},{1,0},{2,3},{3,2},{4,5},{5,4},{6,7},{7,6},{8,9},{9,8},{10,11... | collective-permute-start | bytes 393224 | tf_op jit(solution)/shard_map/ppermute | solution.py:349
  153.4 4.1 %collective-permute-start.20 = (f32[256,128]{1,0:T(8,128)S(1)}, f32[256,128]{1,0:T(8,128)S(1)}, u32[]{:S(2)}, u32[]{:S(2)}) collective-permute-start(f32[256,128]{1,0:T(8,128)S(1)} %get-tuple-element.60), channel_id=1, source_target_pairs={{1,2},{3,4},{5,6},{7,8},{9,10},{11,12},{13,14},{15,16},{17,18},{19... | collective-permute-start | bytes 393224 | tf_op jit(solution)/shard_map/ppermute | solution.py:356
  157.5 3.4 %collective-permute-done.20.far = f32[256,128]{1,0:T(8,128)S(1)} collective-permute-done((f32[256,128]{1,0:T(8,128)S(1)}, f32[256,128]{1,0:T(8,128)S(1)}, u32[]{:S(2)}, u32[]{:S(2)}) %collective-permute-start.20) | collective-permute-done | bytes 131104 | tf_op jit(solution)/shard_map/ppermute | solution.py:356
  160.9 2.5 %collective-permute-start.21 = (f32[1024,128]{1,0:T(8,128)S(1)}, f32[1024,128]{1,0:T(8,128)S(1)}, u32[]{:S(2)}, u32[]{:S(2)}) collective-permute-start(f32[1024,128]{1,0:T(8,128)S(1)} %bitcast.6), channel_id=1, source_target_pairs={{0,1},{1,0},{2,3},{3,2},{4,5},{5,4},{6,7},{7,6},{8,9},{9,8},{10,11... | collective-permute-start | bytes 1572872 | tf_op jit(solution)/shard_map/ppermute | solution.py:349
  (81 shorter events, 39.5 us)
Async XLA Ops:
  1.8 6.4 %collective-permute-start = (f32[256,128]{1,0:T(8,128)S(1)}, f32[256,128]{1,0:T(8,128)S(1)}, u32[]{:S(2)}, u32[]{:S(2)}) collective-permute-start(f32[256,128]{1,0:T(8,128)S(1)} %get-tuple-element.33), channel_id=1, source_target_pairs={{0,1},{1,0},{2,3},{3,2},{4,5},{5,4},{6,7},{7,6},{8,9},{9,8},{10,11... | collective-permute-start | bytes 393224 | tf_op jit(solution)/shard_map/ppermute | solution.py:349
  5.1 8.6 %collective-permute-start.1 = (f32[256,128]{1,0:T(8,128)S(1)}, f32[256,128]{1,0:T(8,128)S(1)}, u32[]{:S(2)}, u32[]{:S(2)}) collective-permute-start(f32[256,128]{1,0:T(8,128)S(1)} %get-tuple-element.34), channel_id=1, source_target_pairs={{1,2},{3,4},{5,6},{7,8},{9,10},{11,12},{13,14},{15,16},{17,18},{19... | collective-permute-start | bytes 393224 | tf_op jit(solution)/shard_map/ppermute | solution.py:356
  14.9 3.9 %collective-permute-start.2 = (f32[2,64,384]{2,1,0:T(8,128)S(1)}, f32[2,64,384]{2,1,0:T(8,128)S(1)}, u32[]{:S(2)}, u32[]{:S(2)}) collective-permute-start(f32[2,64,384]{2,1,0:T(8,128)S(1)} %get-tuple-element.35), channel_id=1, source_target_pairs={{0,32},{32,64},{64,96},{96,128},{128,160},{160,192},{192,224},{1,3... | collective-permute-start | bytes 589832 | tf_op jit(solution)/shard_map/ppermute | solution.py:345
  16.2 6.4 %collective-permute-start.3 = (f32[2,64,384]{2,1,0:T(8,128)S(1)}, f32[2,64,384]{2,1,0:T(8,128)S(1)}, u32[]{:S(2)}, u32[]{:S(2)}) collective-permute-start(f32[2,64,384]{2,1,0:T(8,128)S(1)} %get-tuple-element.37), channel_id=1, source_target_pairs={{32,0},{64,32},{96,64},{128,96},{160,128},{192,160},{224,192},{33,... | collective-permute-start | bytes 589832 | tf_op jit(solution)/shard_map/ppermute | solution.py:345
  30.8 2.2 %collective-permute-start.4 = (f32[1024,128]{1,0:T(8,128)}, f32[1024,128]{1,0:T(8,128)S(1)}, u32[]{:S(2)}, u32[]{:S(2)}) collective-permute-start(f32[1024,128]{1,0:T(8,128)} %get-tuple-element.39), channel_id=1, source_target_pairs={{0,1},{1,0},{2,3},{3,2},{4,5},{5,4},{6,7},{7,6},{8,9},{9,8},{10,11... | collective-permute-start | bytes 1572872 | tf_op jit(solution)/shard_map/ppermute | solution.py:349
  34.9 23.7 %all-to-all-start = ((f32[32,32,128]{2,1,0:T(8,128)}), f32[32,32,128]{2,1,0:T(8,128)S(1)}, u32[]{:S(2)}, u32[]{:S(2)}) async-start(f32[32,32,128]{2,1,0:T(8,128)} %bitcast), calls=%async_computation | async-start | bytes 1048576 | tf_op jit(solution)/shard_map/all_to_all | solution.py:371
  48.5 17.3 %collective-permute-start.8 = (f32[264,256]{1,0:T(8,128)S(1)}, f32[264,256]{1,0:T(8,128)S(1)}, u32[]{:S(2)}, u32[]{:S(2)}) collective-permute-start(f32[264,256]{1,0:T(8,128)S(1)} %copy-done.18), channel_id=1, source_target_pairs={{0,32},{32,64},{64,96},{96,128},{128,160},{160,192},{192,224},{1,3... | collective-permute-start | bytes 811016 | tf_op jit(solution)/shard_map/ppermute | solution.py:345
  51.7 15.7 %collective-permute-start.9 = (f32[264,256]{1,0:T(8,128)S(1)}, f32[264,256]{1,0:T(8,128)S(1)}, u32[]{:S(2)}, u32[]{:S(2)}) collective-permute-start(f32[264,256]{1,0:T(8,128)S(1)} %copy-done.17), channel_id=1, source_target_pairs={{32,0},{64,32},{96,64},{128,96},{160,128},{192,160},{224,192},{33,... | collective-permute-start | bytes 811016 | tf_op jit(solution)/shard_map/ppermute | solution.py:345
  58.7 8.7 %collective-permute-start.7 = (f32[32,128]{1,0:T(8,128)S(1)}, f32[32,128]{1,0:T(8,128)S(1)}, u32[]{:S(2)}, u32[]{:S(2)}) collective-permute-start(f32[32,128]{1,0:T(8,128)S(1)} %reduce_sum.18.p0), channel_id=1, source_target_pairs={{0,6},{1,7},{2,4},{3,5},{4,2},{5,3},{6,0},{7,1},{8,14},{9,15},{10,... | collective-permute-start | bytes 49160 | tf_op jit(solution)/shard_map/ppermute | solution.py:349
  63.6 6.5 %collective-permute-start.6 = (f32[32,128]{1,0:T(8,128)S(1)}, f32[32,128]{1,0:T(8,128)S(1)}, u32[]{:S(2)}, u32[]{:S(2)}) collective-permute-start(f32[32,128]{1,0:T(8,128)S(1)} %reduce_sum.18.p0), channel_id=1, source_target_pairs={{0,4},{1,5},{2,6},{3,7},{4,0},{5,1},{6,2},{7,3},{8,12},{9,13},{10,... | collective-permute-start | bytes 49160 | tf_op jit(solution)/shard_map/ppermute | solution.py:349
  64.2 5.9 %collective-permute-start.5 = (f32[32,128]{1,0:T(8,128)S(1)}, f32[32,128]{1,0:T(8,128)S(1)}, u32[]{:S(2)}, u32[]{:S(2)}) collective-permute-start(f32[32,128]{1,0:T(8,128)S(1)} %reduce_sum.18.p0), channel_id=1, source_target_pairs={{0,2},{1,3},{2,0},{3,1},{4,6},{5,7},{6,4},{7,5},{8,10},{9,11},{10,... | collective-permute-start | bytes 49160 | tf_op jit(solution)/shard_map/ppermute | solution.py:349
  73.0 25.8 %all-to-all-start.1 = ((f32[32,32,128]{2,1,0:T(8,128)}), f32[32,32,128]{2,1,0:T(8,128)S(1)}, u32[]{:S(2)}, u32[]{:S(2)}) async-start(f32[32,32,128]{2,1,0:T(8,128)} %bitcast.1), calls=%async_computation.1 | async-start | bytes 1048576 | tf_op jit(solution)/shard_map/all_to_all | solution.py:377
  82.3 6.0 %collective-permute-start.10 = (f32[2,384,128]{2,1,0:T(8,128)S(1)}, f32[2,384,128]{2,1,0:T(8,128)S(1)}, u32[]{:S(2)}, u32[]{:S(2)}) collective-permute-start(f32[2,384,128]{2,1,0:T(8,128)S(1)} %get-tuple-element.43.refs_4_), channel_id=1, source_target_pairs={{0,1},{1,0},{2,3},{3,2},{4,5},{5,4},{6,7},{7,6},{8,9},{9,8},{10,11... | collective-permute-start | bytes 1179656 | tf_op jit(solution)/shard_map/ppermute | solution.py:349
  84.7 14.2 %collective-permute-start.11 = (f32[2,384,128]{2,1,0:T(8,128)S(1)}, f32[2,384,128]{2,1,0:T(8,128)S(1)}, u32[]{:S(2)}, u32[]{:S(2)}) collective-permute-start(f32[2,384,128]{2,1,0:T(8,128)S(1)} %get-tuple-element.45.refs_6_), channel_id=1, source_target_pairs={{1,2},{3,4},{5,6},{7,8},{9,10},{11,12},{13,14},{15,16},{17,18},{19... | collective-permute-start | bytes 1179656 | tf_op jit(solution)/shard_map/ppermute | solution.py:356
  114.4 20.1 %all-to-all-start.2 = ((f32[32,32,128]{2,1,0:T(8,128)}), f32[32,32,128]{2,1,0:T(8,128)S(1)}, u32[]{:S(2)}, u32[]{:S(2)}) async-start(f32[32,32,128]{2,1,0:T(8,128)} %bitcast.3), calls=%async_computation.2 | async-start | bytes 1048576 | tf_op jit(solution)/shard_map/all_to_all | solution.py:371
  124.3 16.0 %collective-permute-start.17 = (f32[136,256]{1,0:T(8,128)S(1)}, f32[136,256]{1,0:T(8,128)S(1)}, u32[]{:S(2)}, u32[]{:S(2)}) collective-permute-start(f32[136,256]{1,0:T(8,128)S(1)} %copy-done.20), channel_id=1, source_target_pairs={{0,32},{32,64},{64,96},{96,128},{128,160},{160,192},{192,224},{1,3... | collective-permute-start | bytes 417800 | tf_op jit(solution)/shard_map/ppermute | solution.py:345
  127.5 12.8 %collective-permute-start.18 = (f32[136,256]{1,0:T(8,128)S(1)}, f32[136,256]{1,0:T(8,128)S(1)}, u32[]{:S(2)}, u32[]{:S(2)}) collective-permute-start(f32[136,256]{1,0:T(8,128)S(1)} %copy-done.19), channel_id=1, source_target_pairs={{32,0},{64,32},{96,64},{128,96},{160,128},{192,160},{224,192},{33,... | collective-permute-start | bytes 417800 | tf_op jit(solution)/shard_map/ppermute | solution.py:345
  134.5 5.8 %collective-permute-start.16 = (f32[32,128]{1,0:T(8,128)S(1)}, f32[32,128]{1,0:T(8,128)S(1)}, u32[]{:S(2)}, u32[]{:S(2)}) collective-permute-start(f32[32,128]{1,0:T(8,128)S(1)} %reduce_sum.19.p0), channel_id=1, source_target_pairs={{0,6},{1,7},{2,4},{3,5},{4,2},{5,3},{6,0},{7,1},{8,14},{9,15},{10,... | collective-permute-start | bytes 49160 | tf_op jit(solution)/shard_map/ppermute | solution.py:349
  135.6 6.5 %collective-permute-start.15 = (f32[32,128]{1,0:T(8,128)S(1)}, f32[32,128]{1,0:T(8,128)S(1)}, u32[]{:S(2)}, u32[]{:S(2)}) collective-permute-start(f32[32,128]{1,0:T(8,128)S(1)} %reduce_sum.19.p0), channel_id=1, source_target_pairs={{0,4},{1,5},{2,6},{3,7},{4,0},{5,1},{6,2},{7,3},{8,12},{9,13},{10,... | collective-permute-start | bytes 49160 | tf_op jit(solution)/shard_map/ppermute | solution.py:349
  138.5 3.8 %collective-permute-start.14 = (f32[32,128]{1,0:T(8,128)S(1)}, f32[32,128]{1,0:T(8,128)S(1)}, u32[]{:S(2)}, u32[]{:S(2)}) collective-permute-start(f32[32,128]{1,0:T(8,128)S(1)} %reduce_sum.19.p0), channel_id=1, source_target_pairs={{0,2},{1,3},{2,0},{3,1},{4,6},{5,7},{6,4},{7,5},{8,10},{9,11},{10,... | collective-permute-start | bytes 49160 | tf_op jit(solution)/shard_map/ppermute | solution.py:349
  145.0 15.9 %all-to-all-start.3 = ((f32[32,32,128]{2,1,0:T(8,128)}), f32[32,32,128]{2,1,0:T(8,128)S(1)}, u32[]{:S(2)}, u32[]{:S(2)}) async-start(f32[32,32,128]{2,1,0:T(8,128)} %bitcast.4), calls=%async_computation.3 | async-start | bytes 1048576 | tf_op jit(solution)/shard_map/all_to_all | solution.py:377
  150.0 7.5 %collective-permute-start.19 = (f32[256,128]{1,0:T(8,128)S(1)}, f32[256,128]{1,0:T(8,128)S(1)}, u32[]{:S(2)}, u32[]{:S(2)}) collective-permute-start(f32[256,128]{1,0:T(8,128)S(1)} %get-tuple-element.59), channel_id=1, source_target_pairs={{0,1},{1,0},{2,3},{3,2},{4,5},{5,4},{6,7},{7,6},{8,9},{9,8},{10,11... | collective-permute-start | bytes 393224 | tf_op jit(solution)/shard_map/ppermute | solution.py:349
  153.4 7.5 %collective-permute-start.20 = (f32[256,128]{1,0:T(8,128)S(1)}, f32[256,128]{1,0:T(8,128)S(1)}, u32[]{:S(2)}, u32[]{:S(2)}) collective-permute-start(f32[256,128]{1,0:T(8,128)S(1)} %get-tuple-element.60), channel_id=1, source_target_pairs={{1,2},{3,4},{5,6},{7,8},{9,10},{11,12},{13,14},{15,16},{17,18},{19... | collective-permute-start | bytes 393224 | tf_op jit(solution)/shard_map/ppermute | solution.py:356
  160.9 4.0 %collective-permute-start.21 = (f32[1024,128]{1,0:T(8,128)S(1)}, f32[1024,128]{1,0:T(8,128)S(1)}, u32[]{:S(2)}, u32[]{:S(2)}) collective-permute-start(f32[1024,128]{1,0:T(8,128)S(1)} %bitcast.6), channel_id=1, source_target_pairs={{0,1},{1,0},{2,3},{3,2},{4,5},{5,4},{6,7},{7,6},{8,9},{9,8},{10,11... | collective-permute-start | bytes 1572872 | tf_op jit(solution)/shard_map/ppermute | solution.py:349
  (23 other events, 272.4 us)

commit v8 on v7

--- a/solution.py
+++ b/solution.py
@@ -25,6 +25,7 @@
 bf16 = jnp.bfloat16
 VMEM_LIMIT = 56 * 1024 * 1024
 SMALL_LIMIT = 24 * 1024 * 1024
+BANDS_LIMIT = 53 * 1024 * 1024
 
 
 def tables():
@@ -138,6 +139,8 @@
         ext, canvas, raw, head, keep, send, outs, probe, *inner, sems = refs[7:]
         up, mid, down, off, ci, cm, co, di, do, probe_in, mine, other, amps, table = inner
     wait = fetch(arrays, inner, sems)
+    canvas[...] = jnp.zeros(canvas.shape, f32)
+    raw[...] = jnp.zeros(raw.shape, f32)
     wait(*range(4 if first else 9))
     o0 = off[0, 0, 0, 0]
     o1 = off[0, 0, 0, 1]
@@ -216,8 +219,6 @@
     skip = (SPAN - own.shape[1]) // 2
     head[...] = jnp.full((8, F), o1.astype(f32))
     for c, value in enumerate((ore, oim)):
-        canvas[c] = jnp.zeros((SPAN + 8, SPAN), f32)
-        raw[c] = jnp.zeros((SPAN + 8, F), f32)
         value = jnp.concatenate([value, jnp.zeros((8, F), f32)], axis=0)
         value = pltpu.roll(value, rest, 0)
         raw[c, pl.ds(base, F + 8), :] = value
@@ -406,6 +407,7 @@
         bands_kernel,
         [(1024, LANE)] + [(2, SPAN, B)] * 3,
         "bands",
+        BANDS_LIMIT,
         specs=[VM] * 4 + [HBM] * 3,
         places=[VM] + [HBM] * 3,
         scratch=[pltpu.VMEM((2, SPAN, B), f32)] * 3 + [pltpu.SemaphoreType.DMA((3,))],
@@ -427,6 +429,7 @@
         last_bands_kernel,
         [(1024, LANE), (2, TILE, SPAN)] + [(TILE, LANE)] * 2,
         "last_bands",
+        BANDS_LIMIT,
         specs=[VM] * 4 + [HBM] * 3,
         places=[VM, HBM, VM, VM],
         scratch=[pltpu.VMEM((2, TILE, SPAN), f32), pltpu.SemaphoreType.DMA((1,))],

time: 169 us -> 170 us (level)
  Pallas kernels: 22 us -> 24.7 us
    pallas_call x7, Pallas kernels: 22 us -> 24.7 us  [run(): pl.pallas_call(kernel, out_shape=[jax.ShapeDtypeStruct(s, f32) for s in o...]
    unnamed x42 -> x30, local copies, waits for them, and re-layouts: 6.19 us -> 4.53 us
where the time goes in v8:
time: 170 us; the launch traced here: 169 us
  starting transfers between devices  84.6 us (50%)
  waiting for transfers between devices  50 us (29%)
  Pallas kernels  24.7 us (15%)
  local copies, waits for them, and re-layouts  4.53 us (3%)
  other arithmetic  3.97 us (2%)
    ppermute x13, starting transfers between devices, exchange(): return lax.ppermute(x, RC, [(i, i ^ mask) for i in range(256)])  24.8 us
    pallas_call x7, Pallas kernels, run(): pl.pallas_call(kernel, out_shape=[jax.ShapeDtypeStruct(s, f32) for s in o...  24.7 us
    all_to_all x2, starting transfers between devices, scatter(): x = lax.all_to_all(x, RC, 0, 0, axis_index_groups=groups(WIDE), tiled=True)  23.2 us
    ppermute x3, waiting for transfers between devices, columns(): return (exchange(near, BIT_CORE), lax.ppermute(far, 'col', pairs))  19.6 us
    all_to_all x2, starting transfers between devices, gather(): x = lax.all_to_all(x, RC, 0, 0, axis_index_groups=groups(WIDE), tiled=True)  14.4 us
    ppermute x13, waiting for transfers between devices, exchange(): return lax.ppermute(x, RC, [(i, i ^ mask) for i in range(256)])  12.2 us
    ppermute x6, starting transfers between devices, shift(): return lax.ppermute(x, axis, pairs)  11.5 us
    all_to_all x2, waiting for transfers between devices, scatter(): x = lax.all_to_all(x, RC, 0, 0, axis_index_groups=groups(WIDE), tiled=True)  11.4 us
  transfers between devices with their start and end apart: 26, of which 15 were waited for; matrix products, arithmetic and copies ran while one was open for 0% of the time, Pallas kernels for 0%

profile of v8, /device:TPU:1, one launch (start us, length us, event | category | flops | bytes accessed | tf_op | source)
XLA Modules:
  0.0 168.9 jit_solution(8915278735792106265)
XLA Ops:
  1.8 3.3 %collective-permute-start = (f32[256,128]{1,0:T(8,128)S(1)}, f32[256,128]{1,0:T(8,128)S(1)}, u32[]{:S(2)}, u32[]{:S(2)}) collective-permute-start(f32[256,128]{1,0:T(8,128)S(1)} %get-tuple-element.33), channel_id=1, source_target_pairs={{0,1},{1,0},{2,3},{3,2},{4,5},{5,4},{6,7},{7,6},{8,9},{9,8},{10,11... | collective-permute-start | bytes 393224 | tf_op jit(solution)/shard_map/ppermute | solution.py:350
  5.1 3.1 %collective-permute-start.1 = (f32[256,128]{1,0:T(8,128)S(1)}, f32[256,128]{1,0:T(8,128)S(1)}, u32[]{:S(2)}, u32[]{:S(2)}) collective-permute-start(f32[256,128]{1,0:T(8,128)S(1)} %get-tuple-element.34), channel_id=1, source_target_pairs={{1,2},{3,4},{5,6},{7,8},{9,10},{11,12},{13,14},{15,16},{17,18},{19... | collective-permute-start | bytes 393224 | tf_op jit(solution)/shard_map/ppermute | solution.py:357
  8.2 5.5 %collective-permute-done.1.outer = f32[256,128]{1,0:T(8,128)S(1)} collective-permute-done((f32[256,128]{1,0:T(8,128)S(1)}, f32[256,128]{1,0:T(8,128)S(1)}, u32[]{:S(2)}, u32[]{:S(2)}) %collective-permute-start.1) | collective-permute-done | bytes 131104 | tf_op jit(solution)/shard_map/ppermute | solution.py:357
  18.7 3.8 %collective-permute-done.3.refs_2_ = f32[2,64,384]{2,1,0:T(8,128)S(1)} collective-permute-done((f32[2,64,384]{2,1,0:T(8,128)S(1)}, f32[2,64,384]{2,1,0:T(8,128)S(1)}, u32[]{:S(2)}, u32[]{:S(2)}) %collective-permute-start.3) | collective-permute-done | bytes 196640 | tf_op jit(solution)/shard_map/ppermute | solution.py:346
  23.3 7.5 %frame1.1 = (f32[1024,128]{1,0:T(8,128)}, f32[1024,128]{1,0:T(8,128)}, f32[264,256]{1,0:T(8,128)}, f32[264,256]{1,0:T(8,128)}, f32[2,384,384]{2,1,0:T(8,128)}) custom-call(f32[2,64,384]{2,1,0:T(8,128)} %copy-done.6, f32[2,256,384]{2,1,0:T(8,128)} %copy-done, f32[2,64,384]{2,1,0:T(8,128)} %copy-done.7, s32[1,1,1,2]{3,2,1,0:T(1,128)} %refs_3_.3, ...), custom_call_target="tpu_custom_call" | custom-call | tf_op jit(solution)/shard_map/frame1/pallas_call | solution.py:330
  34.9 13.4 %all-to-all-start = ((f32[32,32,128]{2,1,0:T(8,128)}), f32[32,32,128]{2,1,0:T(8,128)S(1)}, u32[]{:S(2)}, u32[]{:S(2)}) async-start(f32[32,32,128]{2,1,0:T(8,128)} %bitcast), calls=%async_computation | async-start | bytes 1048576 | tf_op jit(solution)/shard_map/all_to_all | solution.py:372
  48.3 3.2 %collective-permute-start.8 = (f32[264,256]{1,0:T(8,128)S(1)}, f32[264,256]{1,0:T(8,128)S(1)}, u32[]{:S(2)}, u32[]{:S(2)}) collective-permute-start(f32[264,256]{1,0:T(8,128)S(1)} %copy-done.12), channel_id=1, source_target_pairs={{0,32},{32,64},{64,96},{96,128},{128,160},{160,192},{192,224},{1,3... | collective-permute-start | bytes 811016 | tf_op jit(solution)/shard_map/ppermute | solution.py:346
  52.8 5.7 %all-to-all-done = f32[32,32,128]{2,1,0:T(8,128)S(1)} async-done(((f32[32,32,128]{2,1,0:T(8,128)}), f32[32,32,128]{2,1,0:T(8,128)S(1)}, u32[]{:S(2)}, u32[]{:S(2)}) %all-to-all-start) | async-done | bytes 524320 | tf_op jit(solution)/shard_map/all_to_all | solution.py:372
  58.5 4.9 %collective-permute-start.7 = (f32[32,128]{1,0:T(8,128)S(1)}, f32[32,128]{1,0:T(8,128)S(1)}, u32[]{:S(2)}, u32[]{:S(2)}) collective-permute-start(f32[32,128]{1,0:T(8,128)S(1)} %reduce_sum.18.p0), channel_id=1, source_target_pairs={{0,6},{1,7},{2,4},{3,5},{4,2},{5,3},{6,0},{7,1},{8,14},{9,15},{10,... | collective-permute-start | bytes 49160 | tf_op jit(solution)/shard_map/ppermute | solution.py:350
  67.2 2.7 %collective-permute-done.6.p2 = f32[32,128]{1,0:T(8,128)S(1)} collective-permute-done((f32[32,128]{1,0:T(8,128)S(1)}, f32[32,128]{1,0:T(8,128)S(1)}, u32[]{:S(2)}, u32[]{:S(2)}) %collective-permute-start.6) | collective-permute-done | bytes 16416 | tf_op jit(solution)/shard_map/ppermute | solution.py:350
  69.9 3.5 %bands.1 = (f32[1024,128]{1,0:T(8,128)}, f32[2,384,128]{2,1,0:T(8,128)}, f32[2,384,128]{2,1,0:T(8,128)}, f32[2,384,128]{2,1,0:T(8,128)}) custom-call(f32[32,128]{1,0:T(8,128)S(1)} %reduce_sum.18.p0, f32[32,128]{1,0:T(8,128)S(1)} %collective-permute-done.5.p1, f32[32,128]{1,0:T(8,128)S(1)} %collective-permute-done.6.p2, ...), custom_call_target="tpu_custom_call" | custom-call | tf_op jit(solution)/shard_map/bands/pallas_call | solution.py:330
  73.5 9.3 %all-to-all-start.1 = ((f32[32,32,128]{2,1,0:T(8,128)}), f32[32,32,128]{2,1,0:T(8,128)S(1)}, u32[]{:S(2)}, u32[]{:S(2)}) async-start(f32[32,32,128]{2,1,0:T(8,128)} %bitcast.10), calls=%async_computation.1 | async-start | bytes 1048576 | tf_op jit(solution)/shard_map/all_to_all | solution.py:378
  85.1 3.6 %collective-permute-start.11 = (f32[2,384,128]{2,1,0:T(8,128)}, f32[2,384,128]{2,1,0:T(8,128)S(1)}, u32[]{:S(2)}, u32[]{:S(2)}) collective-permute-start(f32[2,384,128]{2,1,0:T(8,128)} %get-tuple-element.45.refs_6_), channel_id=1, source_target_pairs={{1,2},{3,4},{5,6},{7,8},{9,10},{11,12},{13,14},{15,16},{17,18},{19... | collective-permute-start | bytes 1179656 | tf_op jit(solution)/shard_map/ppermute | solution.py:357
  88.8 10.8 %collective-permute-done.11.refs_8_ = f32[2,384,128]{2,1,0:T(8,128)S(1)} collective-permute-done((f32[2,384,128]{2,1,0:T(8,128)}, f32[2,384,128]{2,1,0:T(8,128)S(1)}, u32[]{:S(2)}, u32[]{:S(2)}) %collective-permute-start.11) | collective-permute-done | bytes 393248 | tf_op jit(solution)/shard_map/ppermute | solution.py:357
  102.5 8.4 %frame2.1 = (f32[1024,128]{1,0:T(8,128)}, f32[1024,128]{1,0:T(8,128)}, f32[136,256]{1,0:T(8,128)}, f32[136,256]{1,0:T(8,128)}, f32[2,256,384]{2,1,0:T(8,128)}, /...) custom-call(f32[2,64,384]{2,1,0:T(8,128)} %copy-done.6, f32[2,256,384]{2,1,0:T(8,128)} %copy-done, ...), custom_call_target="tpu_custom_call" | custom-call | tf_op jit(solution)/shard_map/frame2/pallas_call | solution.py:330
  115.0 9.8 %all-to-all-start.2 = ((f32[32,32,128]{2,1,0:T(8,128)}), f32[32,32,128]{2,1,0:T(8,128)S(1)}, u32[]{:S(2)}, u32[]{:S(2)}) async-start(f32[32,32,128]{2,1,0:T(8,128)} %bitcast.3), calls=%async_computation.2 | async-start | bytes 1048576 | tf_op jit(solution)/shard_map/all_to_all | solution.py:372
  124.8 3.1 %collective-permute-start.17 = (f32[136,256]{1,0:T(8,128)S(1)}, f32[136,256]{1,0:T(8,128)S(1)}, u32[]{:S(2)}, u32[]{:S(2)}) collective-permute-start(f32[136,256]{1,0:T(8,128)S(1)} %copy-done.14), channel_id=1, source_target_pairs={{0,32},{32,64},{64,96},{96,128},{128,160},{160,192},{192,224},{1,3... | collective-permute-start | bytes 417800 | tf_op jit(solution)/shard_map/ppermute | solution.py:346
  129.3 5.7 %all-to-all-done.2 = f32[32,32,128]{2,1,0:T(8,128)S(1)} async-done(((f32[32,32,128]{2,1,0:T(8,128)}), f32[32,32,128]{2,1,0:T(8,128)S(1)}, u32[]{:S(2)}, u32[]{:S(2)}) %all-to-all-start.2) | async-done | bytes 524320 | tf_op jit(solution)/shard_map/all_to_all | solution.py:372
  135.5 3.5 %collective-permute-start.15 = (f32[32,128]{1,0:T(8,128)S(1)}, f32[32,128]{1,0:T(8,128)S(1)}, u32[]{:S(2)}, u32[]{:S(2)}) collective-permute-start(f32[32,128]{1,0:T(8,128)S(1)} %reduce_sum.19.p0), channel_id=1, source_target_pairs={{0,4},{1,5},{2,6},{3,7},{4,0},{5,1},{6,2},{7,3},{8,12},{9,13},{10,... | collective-permute-start | bytes 49160 | tf_op jit(solution)/shard_map/ppermute | solution.py:350
  142.8 3.1 %last_bands.1 = (f32[1024,128]{1,0:T(8,128)}, f32[2,256,384]{2,1,0:T(8,128)}, f32[256,128]{1,0:T(8,128)S(1)}, f32[256,128]{1,0:T(8,128)S(1)}) custom-call(f32[32,128]{1,0:T(8,128)S(1)} %reduce_sum.19.p0, f32[32,128]{1,0:T(8,128)S(1)} %collective-permute-done.14.p1, f32[32,128]{1,0:T(8,128)S(1)} %collective-permute-done.15.p2, ...), custom_call_target="tpu_custom_call" | custom-call | tf_op jit(solution)/shard_map/last_bands/pallas_call | solution.py:330
  145.9 5.1 %all-to-all-start.3 = ((f32[32,32,128]{2,1,0:T(8,128)}), f32[32,32,128]{2,1,0:T(8,128)S(1)}, u32[]{:S(2)}, u32[]{:S(2)}) async-start(f32[32,32,128]{2,1,0:T(8,128)} %bitcast.11), calls=%async_computation.3 | async-start | bytes 1048576 | tf_op jit(solution)/shard_map/all_to_all | solution.py:378
  151.1 3.3 %collective-permute-start.19 = (f32[256,128]{1,0:T(8,128)S(1)}, f32[256,128]{1,0:T(8,128)S(1)}, u32[]{:S(2)}, u32[]{:S(2)}) collective-permute-start(f32[256,128]{1,0:T(8,128)S(1)} %get-tuple-element.59), channel_id=1, source_target_pairs={{0,1},{1,0},{2,3},{3,2},{4,5},{5,4},{6,7},{7,6},{8,9},{9,8},{10,11... | collective-permute-start | bytes 393224 | tf_op jit(solution)/shard_map/ppermute | solution.py:350
  154.4 4.1 %collective-permute-start.20 = (f32[256,128]{1,0:T(8,128)S(1)}, f32[256,128]{1,0:T(8,128)S(1)}, u32[]{:S(2)}, u32[]{:S(2)}) collective-permute-start(f32[256,128]{1,0:T(8,128)S(1)} %get-tuple-element.60), channel_id=1, source_target_pairs={{1,2},{3,4},{5,6},{7,8},{9,10},{11,12},{13,14},{15,16},{17,18},{19... | collective-permute-start | bytes 393224 | tf_op jit(solution)/shard_map/ppermute | solution.py:357
  158.4 3.4 %collective-permute-done.20.far = f32[256,128]{1,0:T(8,128)S(1)} collective-permute-done((f32[256,128]{1,0:T(8,128)S(1)}, f32[256,128]{1,0:T(8,128)S(1)}, u32[]{:S(2)}, u32[]{:S(2)}) %collective-permute-start.20) | collective-permute-done | bytes 131104 | tf_op jit(solution)/shard_map/ppermute | solution.py:357
  (69 shorter events, 38.1 us)
Async XLA Ops:
  1.8 6.4 %collective-permute-start = (f32[256,128]{1,0:T(8,128)S(1)}, f32[256,128]{1,0:T(8,128)S(1)}, u32[]{:S(2)}, u32[]{:S(2)}) collective-permute-start(f32[256,128]{1,0:T(8,128)S(1)} %get-tuple-element.33), channel_id=1, source_target_pairs={{0,1},{1,0},{2,3},{3,2},{4,5},{5,4},{6,7},{7,6},{8,9},{9,8},{10,11... | collective-permute-start | bytes 393224 | tf_op jit(solution)/shard_map/ppermute | solution.py:350
  5.1 8.6 %collective-permute-start.1 = (f32[256,128]{1,0:T(8,128)S(1)}, f32[256,128]{1,0:T(8,128)S(1)}, u32[]{:S(2)}, u32[]{:S(2)}) collective-permute-start(f32[256,128]{1,0:T(8,128)S(1)} %get-tuple-element.34), channel_id=1, source_target_pairs={{1,2},{3,4},{5,6},{7,8},{9,10},{11,12},{13,14},{15,16},{17,18},{19... | collective-permute-start | bytes 393224 | tf_op jit(solution)/shard_map/ppermute | solution.py:357
  14.9 3.9 %collective-permute-start.2 = (f32[2,64,384]{2,1,0:T(8,128)S(1)}, f32[2,64,384]{2,1,0:T(8,128)S(1)}, u32[]{:S(2)}, u32[]{:S(2)}) collective-permute-start(f32[2,64,384]{2,1,0:T(8,128)S(1)} %get-tuple-element.35), channel_id=1, source_target_pairs={{0,32},{32,64},{64,96},{96,128},{128,160},{160,192},{192,224},{1,3... | collective-permute-start | bytes 589832 | tf_op jit(solution)/shard_map/ppermute | solution.py:346
  16.2 6.4 %collective-permute-start.3 = (f32[2,64,384]{2,1,0:T(8,128)S(1)}, f32[2,64,384]{2,1,0:T(8,128)S(1)}, u32[]{:S(2)}, u32[]{:S(2)}) collective-permute-start(f32[2,64,384]{2,1,0:T(8,128)S(1)} %get-tuple-element.37), channel_id=1, source_target_pairs={{32,0},{64,32},{96,64},{128,96},{160,128},{192,160},{224,192},{33,... | collective-permute-start | bytes 589832 | tf_op jit(solution)/shard_map/ppermute | solution.py:346
  30.7 2.2 %collective-permute-start.4 = (f32[1024,128]{1,0:T(8,128)}, f32[1024,128]{1,0:T(8,128)S(1)}, u32[]{:S(2)}, u32[]{:S(2)}) collective-permute-start(f32[1024,128]{1,0:T(8,128)} %get-tuple-element.39), channel_id=1, source_target_pairs={{0,1},{1,0},{2,3},{3,2},{4,5},{5,4},{6,7},{7,6},{8,9},{9,8},{10,11... | collective-permute-start | bytes 1572872 | tf_op jit(solution)/shard_map/ppermute | solution.py:350
  34.9 23.6 %all-to-all-start = ((f32[32,32,128]{2,1,0:T(8,128)}), f32[32,32,128]{2,1,0:T(8,128)S(1)}, u32[]{:S(2)}, u32[]{:S(2)}) async-start(f32[32,32,128]{2,1,0:T(8,128)} %bitcast), calls=%async_computation | async-start | bytes 1048576 | tf_op jit(solution)/shard_map/all_to_all | solution.py:372
  48.3 17.3 %collective-permute-start.8 = (f32[264,256]{1,0:T(8,128)S(1)}, f32[264,256]{1,0:T(8,128)S(1)}, u32[]{:S(2)}, u32[]{:S(2)}) collective-permute-start(f32[264,256]{1,0:T(8,128)S(1)} %copy-done.12), channel_id=1, source_target_pairs={{0,32},{32,64},{64,96},{96,128},{128,160},{160,192},{192,224},{1,3... | collective-permute-start | bytes 811016 | tf_op jit(solution)/shard_map/ppermute | solution.py:346
  51.5 15.7 %collective-permute-start.9 = (f32[264,256]{1,0:T(8,128)S(1)}, f32[264,256]{1,0:T(8,128)S(1)}, u32[]{:S(2)}, u32[]{:S(2)}) collective-permute-start(f32[264,256]{1,0:T(8,128)S(1)} %copy-done.11), channel_id=1, source_target_pairs={{32,0},{64,32},{96,64},{128,96},{160,128},{192,160},{224,192},{33,... | collective-permute-start | bytes 811016 | tf_op jit(solution)/shard_map/ppermute | solution.py:346
  58.5 8.7 %collective-permute-start.7 = (f32[32,128]{1,0:T(8,128)S(1)}, f32[32,128]{1,0:T(8,128)S(1)}, u32[]{:S(2)}, u32[]{:S(2)}) collective-permute-start(f32[32,128]{1,0:T(8,128)S(1)} %reduce_sum.18.p0), channel_id=1, source_target_pairs={{0,6},{1,7},{2,4},{3,5},{4,2},{5,3},{6,0},{7,1},{8,14},{9,15},{10,... | collective-permute-start | bytes 49160 | tf_op jit(solution)/shard_map/ppermute | solution.py:350
  63.4 6.5 %collective-permute-start.6 = (f32[32,128]{1,0:T(8,128)S(1)}, f32[32,128]{1,0:T(8,128)S(1)}, u32[]{:S(2)}, u32[]{:S(2)}) collective-permute-start(f32[32,128]{1,0:T(8,128)S(1)} %reduce_sum.18.p0), channel_id=1, source_target_pairs={{0,4},{1,5},{2,6},{3,7},{4,0},{5,1},{6,2},{7,3},{8,12},{9,13},{10,... | collective-permute-start | bytes 49160 | tf_op jit(solution)/shard_map/ppermute | solution.py:350
  64.0 5.9 %collective-permute-start.5 = (f32[32,128]{1,0:T(8,128)S(1)}, f32[32,128]{1,0:T(8,128)S(1)}, u32[]{:S(2)}, u32[]{:S(2)}) collective-permute-start(f32[32,128]{1,0:T(8,128)S(1)} %reduce_sum.18.p0), channel_id=1, source_target_pairs={{0,2},{1,3},{2,0},{3,1},{4,6},{5,7},{6,4},{7,5},{8,10},{9,11},{10,... | collective-permute-start | bytes 49160 | tf_op jit(solution)/shard_map/ppermute | solution.py:350
  73.5 26.1 %all-to-all-start.1 = ((f32[32,32,128]{2,1,0:T(8,128)}), f32[32,32,128]{2,1,0:T(8,128)S(1)}, u32[]{:S(2)}, u32[]{:S(2)}) async-start(f32[32,32,128]{2,1,0:T(8,128)} %bitcast.10), calls=%async_computation.1 | async-start | bytes 1048576 | tf_op jit(solution)/shard_map/all_to_all | solution.py:378
  82.8 6.0 %collective-permute-start.10 = (f32[2,384,128]{2,1,0:T(8,128)}, f32[2,384,128]{2,1,0:T(8,128)S(1)}, u32[]{:S(2)}, u32[]{:S(2)}) collective-permute-start(f32[2,384,128]{2,1,0:T(8,128)} %get-tuple-element.43.refs_4_), channel_id=1, source_target_pairs={{0,1},{1,0},{2,3},{3,2},{4,5},{5,4},{6,7},{7,6},{8,9},{9,8},{10,11... | collective-permute-start | bytes 1179656 | tf_op jit(solution)/shard_map/ppermute | solution.py:350
  85.1 14.4 %collective-permute-start.11 = (f32[2,384,128]{2,1,0:T(8,128)}, f32[2,384,128]{2,1,0:T(8,128)S(1)}, u32[]{:S(2)}, u32[]{:S(2)}) collective-permute-start(f32[2,384,128]{2,1,0:T(8,128)} %get-tuple-element.45.refs_6_), channel_id=1, source_target_pairs={{1,2},{3,4},{5,6},{7,8},{9,10},{11,12},{13,14},{15,16},{17,18},{19... | collective-permute-start | bytes 1179656 | tf_op jit(solution)/shard_map/ppermute | solution.py:357
  115.0 19.9 %all-to-all-start.2 = ((f32[32,32,128]{2,1,0:T(8,128)}), f32[32,32,128]{2,1,0:T(8,128)S(1)}, u32[]{:S(2)}, u32[]{:S(2)}) async-start(f32[32,32,128]{2,1,0:T(8,128)} %bitcast.3), calls=%async_computation.2 | async-start | bytes 1048576 | tf_op jit(solution)/shard_map/all_to_all | solution.py:372
  124.8 16.0 %collective-permute-start.17 = (f32[136,256]{1,0:T(8,128)S(1)}, f32[136,256]{1,0:T(8,128)S(1)}, u32[]{:S(2)}, u32[]{:S(2)}) collective-permute-start(f32[136,256]{1,0:T(8,128)S(1)} %copy-done.14), channel_id=1, source_target_pairs={{0,32},{32,64},{64,96},{96,128},{128,160},{160,192},{192,224},{1,3... | collective-permute-start | bytes 417800 | tf_op jit(solution)/shard_map/ppermute | solution.py:346
  128.0 12.8 %collective-permute-start.18 = (f32[136,256]{1,0:T(8,128)S(1)}, f32[136,256]{1,0:T(8,128)S(1)}, u32[]{:S(2)}, u32[]{:S(2)}) collective-permute-start(f32[136,256]{1,0:T(8,128)S(1)} %copy-done.13), channel_id=1, source_target_pairs={{32,0},{64,32},{96,64},{128,96},{160,128},{192,160},{224,192},{33,... | collective-permute-start | bytes 417800 | tf_op jit(solution)/shard_map/ppermute | solution.py:346
  135.0 5.8 %collective-permute-start.16 = (f32[32,128]{1,0:T(8,128)S(1)}, f32[32,128]{1,0:T(8,128)S(1)}, u32[]{:S(2)}, u32[]{:S(2)}) collective-permute-start(f32[32,128]{1,0:T(8,128)S(1)} %reduce_sum.19.p0), channel_id=1, source_target_pairs={{0,6},{1,7},{2,4},{3,5},{4,2},{5,3},{6,0},{7,1},{8,14},{9,15},{10,... | collective-permute-start | bytes 49160 | tf_op jit(solution)/shard_map/ppermute | solution.py:350
  135.5 6.5 %collective-permute-start.15 = (f32[32,128]{1,0:T(8,128)S(1)}, f32[32,128]{1,0:T(8,128)S(1)}, u32[]{:S(2)}, u32[]{:S(2)}) collective-permute-start(f32[32,128]{1,0:T(8,128)S(1)} %reduce_sum.19.p0), channel_id=1, source_target_pairs={{0,4},{1,5},{2,6},{3,7},{4,0},{5,1},{6,2},{7,3},{8,12},{9,13},{10,... | collective-permute-start | bytes 49160 | tf_op jit(solution)/shard_map/ppermute | solution.py:350
  139.0 3.8 %collective-permute-start.14 = (f32[32,128]{1,0:T(8,128)S(1)}, f32[32,128]{1,0:T(8,128)S(1)}, u32[]{:S(2)}, u32[]{:S(2)}) collective-permute-start(f32[32,128]{1,0:T(8,128)S(1)} %reduce_sum.19.p0), channel_id=1, source_target_pairs={{0,2},{1,3},{2,0},{3,1},{4,6},{5,7},{6,4},{7,5},{8,10},{9,11},{10,... | collective-permute-start | bytes 49160 | tf_op jit(solution)/shard_map/ppermute | solution.py:350
  145.9 15.9 %all-to-all-start.3 = ((f32[32,32,128]{2,1,0:T(8,128)}), f32[32,32,128]{2,1,0:T(8,128)S(1)}, u32[]{:S(2)}, u32[]{:S(2)}) async-start(f32[32,32,128]{2,1,0:T(8,128)} %bitcast.11), calls=%async_computation.3 | async-start | bytes 1048576 | tf_op jit(solution)/shard_map/all_to_all | solution.py:378
  151.1 7.3 %collective-permute-start.19 = (f32[256,128]{1,0:T(8,128)S(1)}, f32[256,128]{1,0:T(8,128)S(1)}, u32[]{:S(2)}, u32[]{:S(2)}) collective-permute-start(f32[256,128]{1,0:T(8,128)S(1)} %get-tuple-element.59), channel_id=1, source_target_pairs={{0,1},{1,0},{2,3},{3,2},{4,5},{5,4},{6,7},{7,6},{8,9},{9,8},{10,11... | collective-permute-start | bytes 393224 | tf_op jit(solution)/shard_map/ppermute | solution.py:350
  154.4 7.5 %collective-permute-start.20 = (f32[256,128]{1,0:T(8,128)S(1)}, f32[256,128]{1,0:T(8,128)S(1)}, u32[]{:S(2)}, u32[]{:S(2)}) collective-permute-start(f32[256,128]{1,0:T(8,128)S(1)} %get-tuple-element.60), channel_id=1, source_target_pairs={{1,2},{3,4},{5,6},{7,8},{9,10},{11,12},{13,14},{15,16},{17,18},{19... | collective-permute-start | bytes 393224 | tf_op jit(solution)/shard_map/ppermute | solution.py:357
  161.8 4.0 %collective-permute-start.21 = (f32[1024,128]{1,0:T(8,128)S(1)}, f32[1024,128]{1,0:T(8,128)S(1)}, u32[]{:S(2)}, u32[]{:S(2)}) collective-permute-start(f32[1024,128]{1,0:T(8,128)S(1)} %bitcast.6), channel_id=1, source_target_pairs={{0,1},{1,0},{2,3},{3,2},{4,5},{5,4},{6,7},{7,6},{8,9},{9,8},{10,11... | collective-permute-start | bytes 1572872 | tf_op jit(solution)/shard_map/ppermute | solution.py:350
  (17 other events, 152.2 us)

commit v9 on v8

--- a/solution.py
+++ b/solution.py
@@ -25,7 +25,7 @@
 bf16 = jnp.bfloat16
 VMEM_LIMIT = 56 * 1024 * 1024
 SMALL_LIMIT = 24 * 1024 * 1024
-BANDS_LIMIT = 53 * 1024 * 1024
+LAST_LIMIT = 53 * 1024 * 1024
 
 
 def tables():
@@ -407,7 +407,6 @@
         bands_kernel,
         [(1024, LANE)] + [(2, SPAN, B)] * 3,
         "bands",
-        BANDS_LIMIT,
         specs=[VM] * 4 + [HBM] * 3,
         places=[VM] + [HBM] * 3,
         scratch=[pltpu.VMEM((2, SPAN, B), f32)] * 3 + [pltpu.SemaphoreType.DMA((3,))],
@@ -429,7 +428,6 @@
         last_bands_kernel,
         [(1024, LANE), (2, TILE, SPAN)] + [(TILE, LANE)] * 2,
         "last_bands",
-        BANDS_LIMIT,
         specs=[VM] * 4 + [HBM] * 3,
         places=[VM, HBM, VM, VM],
         scratch=[pltpu.VMEM((2, TILE, SPAN), f32), pltpu.SemaphoreType.DMA((1,))],
@@ -440,6 +438,7 @@
             last_kernel,
             [(2, TILE, TILE), (2, M, F, F)],
             "last",
+            LAST_LIMIT,
             specs=[HBM] * 3 + [VM] * 4,
         )(obj, grad, probe, near, far, mine, other)
     )

time: 170 us -> 171 us (level)
    unnamed x30 -> x38, local copies, waits for them, and re-layouts: 4.53 us -> 5.83 us
where the time goes in v9:
time: 171 us; the launch traced here: 170 us
  starting transfers between devices  84.9 us (50%)
  waiting for transfers between devices  49.8 us (29%)
  Pallas kernels  24.5 us (14%)
  local copies, waits for them, and re-layouts  5.83 us (3%)
  other arithmetic  4.02 us (2%)
    ppermute x13, starting transfers between devices, exchange(): return lax.ppermute(x, RC, [(i, i ^ mask) for i in range(256)])  24.9 us
    pallas_call x7, Pallas kernels, run(): pl.pallas_call(kernel, out_shape=[jax.ShapeDtypeStruct(s, f32) for s in o...  24.5 us
    all_to_all x2, starting transfers between devices, scatter(): x = lax.all_to_all(x, RC, 0, 0, axis_index_groups=groups(WIDE), tiled=True)  23.4 us
    ppermute x3, waiting for transfers between devices, columns(): return (exchange(near, BIT_CORE), lax.ppermute(far, 'col', pairs))  19.4 us
    all_to_all x2, starting transfers between devices, gather(): x = lax.all_to_all(x, RC, 0, 0, axis_index_groups=groups(WIDE), tiled=True)  14.3 us
    ppermute x13, waiting for transfers between devices, exchange(): return lax.ppermute(x, RC, [(i, i ^ mask) for i in range(256)])  12.2 us
    ppermute x6, starting transfers between devices, shift(): return lax.ppermute(x, axis, pairs)  11.5 us
    all_to_all x2, waiting for transfers between devices, scatter(): x = lax.all_to_all(x, RC, 0, 0, axis_index_groups=groups(WIDE), tiled=True)  11.4 us
  transfers between devices with their start and end apart: 26, of which 15 were waited for; matrix products, arithmetic and copies ran while one was open for 0% of the time, Pallas kernels for 0%

profile of v9, /device:TPU:1, one launch (start us, length us, event | category | flops | bytes accessed | tf_op | source)
XLA Modules:
  0.0 170.1 jit_solution(5969619468609341836)
XLA Ops:
  1.8 3.3 %collective-permute-start = (f32[256,128]{1,0:T(8,128)S(1)}, f32[256,128]{1,0:T(8,128)S(1)}, u32[]{:S(2)}, u32[]{:S(2)}) collective-permute-start(f32[256,128]{1,0:T(8,128)S(1)} %get-tuple-element.33), channel_id=1, source_target_pairs={{0,1},{1,0},{2,3},{3,2},{4,5},{5,4},{6,7},{7,6},{8,9},{9,8},{10,11... | collective-permute-start | bytes 393224 | tf_op jit(solution)/shard_map/ppermute | solution.py:350
  5.1 3.1 %collective-permute-start.1 = (f32[256,128]{1,0:T(8,128)S(1)}, f32[256,128]{1,0:T(8,128)S(1)}, u32[]{:S(2)}, u32[]{:S(2)}) collective-permute-start(f32[256,128]{1,0:T(8,128)S(1)} %get-tuple-element.34), channel_id=1, source_target_pairs={{1,2},{3,4},{5,6},{7,8},{9,10},{11,12},{13,14},{15,16},{17,18},{19... | collective-permute-start | bytes 393224 | tf_op jit(solution)/shard_map/ppermute | solution.py:357
  8.2 5.5 %collective-permute-done.1.outer = f32[256,128]{1,0:T(8,128)S(1)} collective-permute-done((f32[256,128]{1,0:T(8,128)S(1)}, f32[256,128]{1,0:T(8,128)S(1)}, u32[]{:S(2)}, u32[]{:S(2)}) %collective-permute-start.1) | collective-permute-done | bytes 131104 | tf_op jit(solution)/shard_map/ppermute | solution.py:357
  18.7 3.8 %collective-permute-done.3.refs_2_ = f32[2,64,384]{2,1,0:T(8,128)S(1)} collective-permute-done((f32[2,64,384]{2,1,0:T(8,128)S(1)}, f32[2,64,384]{2,1,0:T(8,128)S(1)}, u32[]{:S(2)}, u32[]{:S(2)}) %collective-permute-start.3) | collective-permute-done | bytes 196640 | tf_op jit(solution)/shard_map/ppermute | solution.py:346
  23.3 7.5 %frame1.1 = (f32[1024,128]{1,0:T(8,128)}, f32[1024,128]{1,0:T(8,128)}, f32[264,256]{1,0:T(8,128)}, f32[264,256]{1,0:T(8,128)}, f32[2,384,384]{2,1,0:T(8,128)}) custom-call(f32[2,64,384]{2,1,0:T(8,128)} %copy-done.9, f32[2,256,384]{2,1,0:T(8,128)} %copy-done, f32[2,64,384]{2,1,0:T(8,128)} %copy-done.10, s32[1,1,1,2]{3,2,1,0:T(1,128)} %refs_3_.3, ...), custom_call_target="tpu_custom_call" | custom-call | tf_op jit(solution)/shard_map/frame1/pallas_call | solution.py:330
  34.9 13.6 %all-to-all-start = ((f32[32,32,128]{2,1,0:T(8,128)}), f32[32,32,128]{2,1,0:T(8,128)S(1)}, u32[]{:S(2)}, u32[]{:S(2)}) async-start(f32[32,32,128]{2,1,0:T(8,128)} %bitcast), calls=%async_computation | async-start | bytes 1048576 | tf_op jit(solution)/shard_map/all_to_all | solution.py:372
  48.5 3.2 %collective-permute-start.8 = (f32[264,256]{1,0:T(8,128)S(1)}, f32[264,256]{1,0:T(8,128)S(1)}, u32[]{:S(2)}, u32[]{:S(2)}) collective-permute-start(f32[264,256]{1,0:T(8,128)S(1)} %copy-done.16), channel_id=1, source_target_pairs={{0,32},{32,64},{64,96},{96,128},{128,160},{160,192},{192,224},{1,3... | collective-permute-start | bytes 811016 | tf_op jit(solution)/shard_map/ppermute | solution.py:346
  52.9 5.7 %all-to-all-done = f32[32,32,128]{2,1,0:T(8,128)S(1)} async-done(((f32[32,32,128]{2,1,0:T(8,128)}), f32[32,32,128]{2,1,0:T(8,128)S(1)}, u32[]{:S(2)}, u32[]{:S(2)}) %all-to-all-start) | async-done | bytes 524320 | tf_op jit(solution)/shard_map/all_to_all | solution.py:372
  58.7 4.9 %collective-permute-start.7 = (f32[32,128]{1,0:T(8,128)S(1)}, f32[32,128]{1,0:T(8,128)S(1)}, u32[]{:S(2)}, u32[]{:S(2)}) collective-permute-start(f32[32,128]{1,0:T(8,128)S(1)} %reduce_sum.18.p0), channel_id=1, source_target_pairs={{0,6},{1,7},{2,4},{3,5},{4,2},{5,3},{6,0},{7,1},{8,14},{9,15},{10,... | collective-permute-start | bytes 49160 | tf_op jit(solution)/shard_map/ppermute | solution.py:350
  67.4 2.7 %collective-permute-done.6.p2 = f32[32,128]{1,0:T(8,128)S(1)} collective-permute-done((f32[32,128]{1,0:T(8,128)S(1)}, f32[32,128]{1,0:T(8,128)S(1)}, u32[]{:S(2)}, u32[]{:S(2)}) %collective-permute-start.6) | collective-permute-done | bytes 16416 | tf_op jit(solution)/shard_map/ppermute | solution.py:350
  73.0 9.3 %all-to-all-start.1 = ((f32[32,32,128]{2,1,0:T(8,128)}), f32[32,32,128]{2,1,0:T(8,128)S(1)}, u32[]{:S(2)}, u32[]{:S(2)}) async-start(f32[32,32,128]{2,1,0:T(8,128)} %bitcast.1), calls=%async_computation.1 | async-start | bytes 1048576 | tf_op jit(solution)/shard_map/all_to_all | solution.py:378
  84.7 3.6 %collective-permute-start.11 = (f32[2,384,128]{2,1,0:T(8,128)S(1)}, f32[2,384,128]{2,1,0:T(8,128)S(1)}, u32[]{:S(2)}, u32[]{:S(2)}) collective-permute-start(f32[2,384,128]{2,1,0:T(8,128)S(1)} %get-tuple-element.45.refs_6_), channel_id=1, source_target_pairs={{1,2},{3,4},{5,6},{7,8},{9,10},{11,12},{13,14},{15,16},{17,18},{19... | collective-permute-start | bytes 1179656 | tf_op jit(solution)/shard_map/ppermute | solution.py:357
  88.3 10.5 %collective-permute-done.11.refs_8_ = f32[2,384,128]{2,1,0:T(8,128)S(1)} collective-permute-done((f32[2,384,128]{2,1,0:T(8,128)S(1)}, f32[2,384,128]{2,1,0:T(8,128)S(1)}, u32[]{:S(2)}, u32[]{:S(2)}) %collective-permute-start.11) | collective-permute-done | bytes 393248 | tf_op jit(solution)/shard_map/ppermute | solution.py:357
  101.8 8.3 %frame2.1 = (f32[1024,128]{1,0:T(8,128)}, f32[1024,128]{1,0:T(8,128)}, f32[136,256]{1,0:T(8,128)}, f32[136,256]{1,0:T(8,128)}, f32[2,256,384]{2,1,0:T(8,128)}, /...) custom-call(f32[2,64,384]{2,1,0:T(8,128)} %copy-done.9, f32[2,256,384]{2,1,0:T(8,128)} %copy-done, ...), custom_call_target="tpu_custom_call" | custom-call | tf_op jit(solution)/shard_map/frame2/pallas_call | solution.py:330
  114.3 9.9 %all-to-all-start.2 = ((f32[32,32,128]{2,1,0:T(8,128)}), f32[32,32,128]{2,1,0:T(8,128)S(1)}, u32[]{:S(2)}, u32[]{:S(2)}) async-start(f32[32,32,128]{2,1,0:T(8,128)} %bitcast.3), calls=%async_computation.2 | async-start | bytes 1048576 | tf_op jit(solution)/shard_map/all_to_all | solution.py:372
  124.3 3.1 %collective-permute-start.17 = (f32[136,256]{1,0:T(8,128)S(1)}, f32[136,256]{1,0:T(8,128)S(1)}, u32[]{:S(2)}, u32[]{:S(2)}) collective-permute-start(f32[136,256]{1,0:T(8,128)S(1)} %copy-done.18), channel_id=1, source_target_pairs={{0,32},{32,64},{64,96},{96,128},{128,160},{160,192},{192,224},{1,3... | collective-permute-start | bytes 417800 | tf_op jit(solution)/shard_map/ppermute | solution.py:346
  128.7 5.7 %all-to-all-done.2 = f32[32,32,128]{2,1,0:T(8,128)S(1)} async-done(((f32[32,32,128]{2,1,0:T(8,128)}), f32[32,32,128]{2,1,0:T(8,128)S(1)}, u32[]{:S(2)}, u32[]{:S(2)}) %all-to-all-start.2) | async-done | bytes 524320 | tf_op jit(solution)/shard_map/all_to_all | solution.py:372
  135.5 2.9 %collective-permute-start.15 = (f32[32,128]{1,0:T(8,128)S(1)}, f32[32,128]{1,0:T(8,128)S(1)}, u32[]{:S(2)}, u32[]{:S(2)}) collective-permute-start(f32[32,128]{1,0:T(8,128)S(1)} %reduce_sum.19.p0), channel_id=1, source_target_pairs={{0,4},{1,5},{2,6},{3,7},{4,0},{5,1},{6,2},{7,3},{8,12},{9,13},{10,... | collective-permute-start | bytes 49160 | tf_op jit(solution)/shard_map/ppermute | solution.py:350
  144.9 5.0 %all-to-all-start.3 = ((f32[32,32,128]{2,1,0:T(8,128)}), f32[32,32,128]{2,1,0:T(8,128)S(1)}, u32[]{:S(2)}, u32[]{:S(2)}) async-start(f32[32,32,128]{2,1,0:T(8,128)} %bitcast.4), calls=%async_computation.3 | async-start | bytes 1048576 | tf_op jit(solution)/shard_map/all_to_all | solution.py:378
  149.9 3.4 %collective-permute-start.19 = (f32[256,128]{1,0:T(8,128)S(1)}, f32[256,128]{1,0:T(8,128)S(1)}, u32[]{:S(2)}, u32[]{:S(2)}) collective-permute-start(f32[256,128]{1,0:T(8,128)S(1)} %get-tuple-element.59), channel_id=1, source_target_pairs={{0,1},{1,0},{2,3},{3,2},{4,5},{5,4},{6,7},{7,6},{8,9},{9,8},{10,11... | collective-permute-start | bytes 393224 | tf_op jit(solution)/shard_map/ppermute | solution.py:350
  153.3 4.1 %collective-permute-start.20 = (f32[256,128]{1,0:T(8,128)S(1)}, f32[256,128]{1,0:T(8,128)S(1)}, u32[]{:S(2)}, u32[]{:S(2)}) collective-permute-start(f32[256,128]{1,0:T(8,128)S(1)} %get-tuple-element.60), channel_id=1, source_target_pairs={{1,2},{3,4},{5,6},{7,8},{9,10},{11,12},{13,14},{15,16},{17,18},{19... | collective-permute-start | bytes 393224 | tf_op jit(solution)/shard_map/ppermute | solution.py:357
  157.4 3.4 %collective-permute-done.20.far = f32[256,128]{1,0:T(8,128)S(1)} collective-permute-done((f32[256,128]{1,0:T(8,128)S(1)}, f32[256,128]{1,0:T(8,128)S(1)}, u32[]{:S(2)}, u32[]{:S(2)}) %collective-permute-start.20) | collective-permute-done | bytes 131104 | tf_op jit(solution)/shard_map/ppermute | solution.py:357
  160.8 2.5 %collective-permute-start.21 = (f32[1024,128]{1,0:T(8,128)S(1)}, f32[1024,128]{1,0:T(8,128)S(1)}, u32[]{:S(2)}, u32[]{:S(2)}) collective-permute-start(f32[1024,128]{1,0:T(8,128)S(1)} %bitcast.6), channel_id=1, source_target_pairs={{0,1},{1,0},{2,3},{3,2},{4,5},{5,4},{6,7},{7,6},{8,9},{9,8},{10,11... | collective-permute-start | bytes 1572872 | tf_op jit(solution)/shard_map/ppermute | solution.py:350
  165.6 4.3 %last.1 = (f32[2,256,256]{2,1,0:T(8,128)}, f32[2,2,256,256]{3,2,1,0:T(8,128)}) custom-call(f32[2,256,384]{2,1,0:T(8,128)} %get-tuple-element.50.obj, f32[2,256,384]{2,1,0:T(8,128)} %copy-done.4, f32[2,2,256,256]{3,2,1,0:T(8,128)} %get-tuple-element.57.probe, f32[256,128]{1,0:T(8,128)S(1)} %collective-permute-done.19.near, ...), custom_call_target="tpu_custom_call" | custom-call | tf_op jit(solution)/shard_map/last/pallas_call | solution.py:330
  (77 shorter events, 39.8 us)
Async XLA Ops:
  1.8 6.4 %collective-permute-start = (f32[256,128]{1,0:T(8,128)S(1)}, f32[256,128]{1,0:T(8,128)S(1)}, u32[]{:S(2)}, u32[]{:S(2)}) collective-permute-start(f32[256,128]{1,0:T(8,128)S(1)} %get-tuple-element.33), channel_id=1, source_target_pairs={{0,1},{1,0},{2,3},{3,2},{4,5},{5,4},{6,7},{7,6},{8,9},{9,8},{10,11... | collective-permute-start | bytes 393224 | tf_op jit(solution)/shard_map/ppermute | solution.py:350
  5.1 8.6 %collective-permute-start.1 = (f32[256,128]{1,0:T(8,128)S(1)}, f32[256,128]{1,0:T(8,128)S(1)}, u32[]{:S(2)}, u32[]{:S(2)}) collective-permute-start(f32[256,128]{1,0:T(8,128)S(1)} %get-tuple-element.34), channel_id=1, source_target_pairs={{1,2},{3,4},{5,6},{7,8},{9,10},{11,12},{13,14},{15,16},{17,18},{19... | collective-permute-start | bytes 393224 | tf_op jit(solution)/shard_map/ppermute | solution.py:357
  14.9 3.9 %collective-permute-start.2 = (f32[2,64,384]{2,1,0:T(8,128)S(1)}, f32[2,64,384]{2,1,0:T(8,128)S(1)}, u32[]{:S(2)}, u32[]{:S(2)}) collective-permute-start(f32[2,64,384]{2,1,0:T(8,128)S(1)} %get-tuple-element.35), channel_id=1, source_target_pairs={{0,32},{32,64},{64,96},{96,128},{128,160},{160,192},{192,224},{1,3... | collective-permute-start | bytes 589832 | tf_op jit(solution)/shard_map/ppermute | solution.py:346
  16.2 6.4 %collective-permute-start.3 = (f32[2,64,384]{2,1,0:T(8,128)S(1)}, f32[2,64,384]{2,1,0:T(8,128)S(1)}, u32[]{:S(2)}, u32[]{:S(2)}) collective-permute-start(f32[2,64,384]{2,1,0:T(8,128)S(1)} %get-tuple-element.37), channel_id=1, source_target_pairs={{32,0},{64,32},{96,64},{128,96},{160,128},{192,160},{224,192},{33,... | collective-permute-start | bytes 589832 | tf_op jit(solution)/shard_map/ppermute | solution.py:346
  30.7 2.2 %collective-permute-start.4 = (f32[1024,128]{1,0:T(8,128)}, f32[1024,128]{1,0:T(8,128)S(1)}, u32[]{:S(2)}, u32[]{:S(2)}) collective-permute-start(f32[1024,128]{1,0:T(8,128)} %get-tuple-element.39), channel_id=1, source_target_pairs={{0,1},{1,0},{2,3},{3,2},{4,5},{5,4},{6,7},{7,6},{8,9},{9,8},{10,11... | collective-permute-start | bytes 1572872 | tf_op jit(solution)/shard_map/ppermute | solution.py:350
  34.9 23.7 %all-to-all-start = ((f32[32,32,128]{2,1,0:T(8,128)}), f32[32,32,128]{2,1,0:T(8,128)S(1)}, u32[]{:S(2)}, u32[]{:S(2)}) async-start(f32[32,32,128]{2,1,0:T(8,128)} %bitcast), calls=%async_computation | async-start | bytes 1048576 | tf_op jit(solution)/shard_map/all_to_all | solution.py:372
  48.5 17.3 %collective-permute-start.8 = (f32[264,256]{1,0:T(8,128)S(1)}, f32[264,256]{1,0:T(8,128)S(1)}, u32[]{:S(2)}, u32[]{:S(2)}) collective-permute-start(f32[264,256]{1,0:T(8,128)S(1)} %copy-done.16), channel_id=1, source_target_pairs={{0,32},{32,64},{64,96},{96,128},{128,160},{160,192},{192,224},{1,3... | collective-permute-start | bytes 811016 | tf_op jit(solution)/shard_map/ppermute | solution.py:346
  51.6 15.7 %collective-permute-start.9 = (f32[264,256]{1,0:T(8,128)S(1)}, f32[264,256]{1,0:T(8,128)S(1)}, u32[]{:S(2)}, u32[]{:S(2)}) collective-permute-start(f32[264,256]{1,0:T(8,128)S(1)} %copy-done.15), channel_id=1, source_target_pairs={{32,0},{64,32},{96,64},{128,96},{160,128},{192,160},{224,192},{33,... | collective-permute-start | bytes 811016 | tf_op jit(solution)/shard_map/ppermute | solution.py:346
  58.7 8.7 %collective-permute-start.7 = (f32[32,128]{1,0:T(8,128)S(1)}, f32[32,128]{1,0:T(8,128)S(1)}, u32[]{:S(2)}, u32[]{:S(2)}) collective-permute-start(f32[32,128]{1,0:T(8,128)S(1)} %reduce_sum.18.p0), channel_id=1, source_target_pairs={{0,6},{1,7},{2,4},{3,5},{4,2},{5,3},{6,0},{7,1},{8,14},{9,15},{10,... | collective-permute-start | bytes 49160 | tf_op jit(solution)/shard_map/ppermute | solution.py:350
  63.6 6.5 %collective-permute-start.6 = (f32[32,128]{1,0:T(8,128)S(1)}, f32[32,128]{1,0:T(8,128)S(1)}, u32[]{:S(2)}, u32[]{:S(2)}) collective-permute-start(f32[32,128]{1,0:T(8,128)S(1)} %reduce_sum.18.p0), channel_id=1, source_target_pairs={{0,4},{1,5},{2,6},{3,7},{4,0},{5,1},{6,2},{7,3},{8,12},{9,13},{10,... | collective-permute-start | bytes 49160 | tf_op jit(solution)/shard_map/ppermute | solution.py:350
  64.2 5.9 %collective-permute-start.5 = (f32[32,128]{1,0:T(8,128)S(1)}, f32[32,128]{1,0:T(8,128)S(1)}, u32[]{:S(2)}, u32[]{:S(2)}) collective-permute-start(f32[32,128]{1,0:T(8,128)S(1)} %reduce_sum.18.p0), channel_id=1, source_target_pairs={{0,2},{1,3},{2,0},{3,1},{4,6},{5,7},{6,4},{7,5},{8,10},{9,11},{10,... | collective-permute-start | bytes 49160 | tf_op jit(solution)/shard_map/ppermute | solution.py:350
  73.0 25.8 %all-to-all-start.1 = ((f32[32,32,128]{2,1,0:T(8,128)}), f32[32,32,128]{2,1,0:T(8,128)S(1)}, u32[]{:S(2)}, u32[]{:S(2)}) async-start(f32[32,32,128]{2,1,0:T(8,128)} %bitcast.1), calls=%async_computation.1 | async-start | bytes 1048576 | tf_op jit(solution)/shard_map/all_to_all | solution.py:378
  82.3 6.0 %collective-permute-start.10 = (f32[2,384,128]{2,1,0:T(8,128)S(1)}, f32[2,384,128]{2,1,0:T(8,128)S(1)}, u32[]{:S(2)}, u32[]{:S(2)}) collective-permute-start(f32[2,384,128]{2,1,0:T(8,128)S(1)} %get-tuple-element.43.refs_4_), channel_id=1, source_target_pairs={{0,1},{1,0},{2,3},{3,2},{4,5},{5,4},{6,7},{7,6},{8,9},{9,8},{10,11... | collective-permute-start | bytes 1179656 | tf_op jit(solution)/shard_map/ppermute | solution.py:350
  84.7 14.2 %collective-permute-start.11 = (f32[2,384,128]{2,1,0:T(8,128)S(1)}, f32[2,384,128]{2,1,0:T(8,128)S(1)}, u32[]{:S(2)}, u32[]{:S(2)}) collective-permute-start(f32[2,384,128]{2,1,0:T(8,128)S(1)} %get-tuple-element.45.refs_6_), channel_id=1, source_target_pairs={{1,2},{3,4},{5,6},{7,8},{9,10},{11,12},{13,14},{15,16},{17,18},{19... | collective-permute-start | bytes 1179656 | tf_op jit(solution)/shard_map/ppermute | solution.py:357
  114.3 20.1 %all-to-all-start.2 = ((f32[32,32,128]{2,1,0:T(8,128)}), f32[32,32,128]{2,1,0:T(8,128)S(1)}, u32[]{:S(2)}, u32[]{:S(2)}) async-start(f32[32,32,128]{2,1,0:T(8,128)} %bitcast.3), calls=%async_computation.2 | async-start | bytes 1048576 | tf_op jit(solution)/shard_map/all_to_all | solution.py:372
  124.3 16.0 %collective-permute-start.17 = (f32[136,256]{1,0:T(8,128)S(1)}, f32[136,256]{1,0:T(8,128)S(1)}, u32[]{:S(2)}, u32[]{:S(2)}) collective-permute-start(f32[136,256]{1,0:T(8,128)S(1)} %copy-done.18), channel_id=1, source_target_pairs={{0,32},{32,64},{64,96},{96,128},{128,160},{160,192},{192,224},{1,3... | collective-permute-start | bytes 417800 | tf_op jit(solution)/shard_map/ppermute | solution.py:346
  127.4 12.8 %collective-permute-start.18 = (f32[136,256]{1,0:T(8,128)S(1)}, f32[136,256]{1,0:T(8,128)S(1)}, u32[]{:S(2)}, u32[]{:S(2)}) collective-permute-start(f32[136,256]{1,0:T(8,128)S(1)} %copy-done.17), channel_id=1, source_target_pairs={{32,0},{64,32},{96,64},{128,96},{160,128},{192,160},{224,192},{33,... | collective-permute-start | bytes 417800 | tf_op jit(solution)/shard_map/ppermute | solution.py:346
  134.5 5.8 %collective-permute-start.16 = (f32[32,128]{1,0:T(8,128)S(1)}, f32[32,128]{1,0:T(8,128)S(1)}, u32[]{:S(2)}, u32[]{:S(2)}) collective-permute-start(f32[32,128]{1,0:T(8,128)S(1)} %reduce_sum.19.p0), channel_id=1, source_target_pairs={{0,6},{1,7},{2,4},{3,5},{4,2},{5,3},{6,0},{7,1},{8,14},{9,15},{10,... | collective-permute-start | bytes 49160 | tf_op jit(solution)/shard_map/ppermute | solution.py:350
  135.5 6.5 %collective-permute-start.15 = (f32[32,128]{1,0:T(8,128)S(1)}, f32[32,128]{1,0:T(8,128)S(1)}, u32[]{:S(2)}, u32[]{:S(2)}) collective-permute-start(f32[32,128]{1,0:T(8,128)S(1)} %reduce_sum.19.p0), channel_id=1, source_target_pairs={{0,4},{1,5},{2,6},{3,7},{4,0},{5,1},{6,2},{7,3},{8,12},{9,13},{10,... | collective-permute-start | bytes 49160 | tf_op jit(solution)/shard_map/ppermute | solution.py:350
  138.4 3.8 %collective-permute-start.14 = (f32[32,128]{1,0:T(8,128)S(1)}, f32[32,128]{1,0:T(8,128)S(1)}, u32[]{:S(2)}, u32[]{:S(2)}) collective-permute-start(f32[32,128]{1,0:T(8,128)S(1)} %reduce_sum.19.p0), channel_id=1, source_target_pairs={{0,2},{1,3},{2,0},{3,1},{4,6},{5,7},{6,4},{7,5},{8,10},{9,11},{10,... | collective-permute-start | bytes 49160 | tf_op jit(solution)/shard_map/ppermute | solution.py:350
  144.9 15.9 %all-to-all-start.3 = ((f32[32,32,128]{2,1,0:T(8,128)}), f32[32,32,128]{2,1,0:T(8,128)S(1)}, u32[]{:S(2)}, u32[]{:S(2)}) async-start(f32[32,32,128]{2,1,0:T(8,128)} %bitcast.4), calls=%async_computation.3 | async-start | bytes 1048576 | tf_op jit(solution)/shard_map/all_to_all | solution.py:378
  149.9 7.5 %collective-permute-start.19 = (f32[256,128]{1,0:T(8,128)S(1)}, f32[256,128]{1,0:T(8,128)S(1)}, u32[]{:S(2)}, u32[]{:S(2)}) collective-permute-start(f32[256,128]{1,0:T(8,128)S(1)} %get-tuple-element.59), channel_id=1, source_target_pairs={{0,1},{1,0},{2,3},{3,2},{4,5},{5,4},{6,7},{7,6},{8,9},{9,8},{10,11... | collective-permute-start | bytes 393224 | tf_op jit(solution)/shard_map/ppermute | solution.py:350
  153.3 7.5 %collective-permute-start.20 = (f32[256,128]{1,0:T(8,128)S(1)}, f32[256,128]{1,0:T(8,128)S(1)}, u32[]{:S(2)}, u32[]{:S(2)}) collective-permute-start(f32[256,128]{1,0:T(8,128)S(1)} %get-tuple-element.60), channel_id=1, source_target_pairs={{1,2},{3,4},{5,6},{7,8},{9,10},{11,12},{13,14},{15,16},{17,18},{19... | collective-permute-start | bytes 393224 | tf_op jit(solution)/shard_map/ppermute | solution.py:357
  160.8 4.0 %collective-permute-start.21 = (f32[1024,128]{1,0:T(8,128)S(1)}, f32[1024,128]{1,0:T(8,128)S(1)}, u32[]{:S(2)}, u32[]{:S(2)}) collective-permute-start(f32[1024,128]{1,0:T(8,128)S(1)} %bitcast.6), channel_id=1, source_target_pairs={{0,1},{1,0},{2,3},{3,2},{4,5},{5,4},{6,7},{7,6},{8,9},{9,8},{10,11... | collective-permute-start | bytes 1572872 | tf_op jit(solution)/shard_map/ppermute | solution.py:350
  (21 other events, 211.4 us)
